TPU v7x, 32 devices: a whole 2x2x4 slice. The times are simulated.
32 devices in a mesh: tm: 8 (over z, y), row: 4 (over x, core).
Axes of the slice: x: 2, y: 2, z: 4, core: 2. Of those that a mesh axis runs over, the one named last changes fastest.
Arguments:
- output_first_half: bfloat16 [16, 4, 64, 320], P('tm', 'row'), may hold values from -6 to 6
- y_second: bfloat16 [16, 4, 64, 320], P('tm', 'row'), may hold values from -6 to 6
- cot_first: bfloat16 [16, 4, 64, 320], P('tm', 'row'), may hold values from -6 to 6
- cot_second: bfloat16 [16, 4, 64, 320], P('tm', 'row'), may hold values from -6 to 6
- weight_space: bfloat16 [3, 3, 2, 160, 160], replicated, may hold values from -0.15625 to 0.15625
- temporal_weight: bfloat16 [3, 5, 128, 128], replicated, may hold values from -0.3125 to 0.3125
Outputs:
- x_first: bfloat16 [16, 4, 64, 320], P('tm', 'row')
- x_second: bfloat16 [16, 4, 64, 320], P('tm', 'row')
- grad_first: bfloat16 [16, 4, 64, 320], P('tm', 'row')
- grad_second: bfloat16 [16, 4, 64, 320], P('tm', 'row')
- spatial_weight_gradient: float32 [460800], P(('tm', 'row'))
- grad_time: float32 [245760], P(('tm', 'row'))
All inputs are finite; a program needn't handle non-finite values.
Results may differ from a plain program's by a relative error of at most 0.007.
Values may be sent and summed in bfloat16 or wider, within the bound.
No kernel may reach another device: no remote copies, remote signals or barrier semaphores. Data moves between devices by JAX's collectives and lax.ppermute only.
A program may use at most 64 MiB of HBM per device.

v0:
```python
import math

import jax
import jax.numpy as jnp
from jax import lax
from jax.sharding import PartitionSpec as P

HAAR = 0.7071067811865476


def extended(x, sides, width):
    for axis, dim in sides:
        peers, length = (lax.axis_size(axis), x.shape[dim])
        up = [(i, (i + 1) % peers) for i in range(peers - 1)]
        down = [(j, i) for i, j in up]
        last = lax.slice_in_dim(x, length - width, length, axis=dim)
        initial = lax.slice_in_dim(x, 0, width, axis=dim)
        before = lax.ppermute(last, axis, up)
        after = lax.ppermute(initial, axis, down)
        x = jnp.concatenate([before, x, after], axis=dim)
    return x


def haar_pair_squeeze(input_frames):
    even_frames = input_frames[0::2].astype(jnp.float32)
    odd_frames = input_frames[1::2].astype(jnp.float32)
    return jnp.concatenate(
        [(even_frames + odd_frames) * HAAR, (even_frames - odd_frames) * HAAR], axis=-1
    )


def unsqueeze_pairs(packed):
    half_ch = packed.shape[-1] // 2
    low_band = packed[..., :half_ch]
    high_band = packed[..., half_ch:]
    stacked = jnp.stack([(low_band + high_band) * HAAR, (low_band - high_band) * HAAR], axis=1)
    return stacked.reshape((2 * low_band.shape[0],) + low_band.shape[1:])


def silu_slope(values):
    sigmoid_v = jax.nn.sigmoid(values)
    return sigmoid_v * (1.0 + values * (1.0 - sigmoid_v))


def split_groups(tensor, groups):
    return tensor.reshape(tensor.shape[:-1] + (groups, tensor.shape[-1] // groups))


def merge_groups(tensor):
    return tensor.reshape(tensor.shape[:-2] + (tensor.shape[-2] * tensor.shape[-1],))


def time_apply(act_ext, temporal_weight):
    length = act_ext.shape[0] - 2
    groups = temporal_weight.shape[1]
    summed = None
    for offset in range(3):
        window = split_groups(act_ext[offset : offset + length], groups)
        partial_sum = jnp.einsum(
            "t...gi,gio->t...go",
            window,
            temporal_weight[offset],
            preferred_element_type=jnp.float32,
        )
        summed = partial_sum if summed is None else summed + partial_sum
    return merge_groups(summed)


def time_back(cot_ext, temporal_weight):
    length = cot_ext.shape[0] - 2
    groups = temporal_weight.shape[1]
    summed = None
    for offset in range(3):
        window = split_groups(cot_ext[2 - offset : 2 - offset + length], groups)
        partial_sum = jnp.einsum(
            "t...go,gio->t...gi",
            window,
            temporal_weight[offset],
            preferred_element_type=jnp.float32,
        )
        summed = partial_sum if summed is None else summed + partial_sum
    return merge_groups(summed)


def time_wgrad(act_ext, cot_inner, groups):
    length = cot_inner.shape[0]
    cot_split = split_groups(cot_inner, groups)
    result = []
    for offset in range(3):
        window = split_groups(act_ext[offset : offset + length], groups)
        result.append(
            jnp.einsum("t...gi,t...go->gio", window, cot_split, preferred_element_type=jnp.float32)
        )
    return jnp.stack(result)


def time_core(y_ext, cot_ext, temporal_weight):
    squeezed = haar_pair_squeeze(y_ext)
    act_time = jax.nn.silu(squeezed).astype(jnp.bfloat16)
    temporal_cotangent = haar_pair_squeeze(cot_ext).astype(jnp.bfloat16)
    branch_time = unsqueeze_pairs(time_apply(act_time, temporal_weight)).astype(jnp.bfloat16)
    back_sum = time_back(temporal_cotangent, temporal_weight) * silu_slope(squeezed[1:-1])
    back_time = unsqueeze_pairs(back_sum).astype(jnp.bfloat16)
    sum_time = time_wgrad(act_time, temporal_cotangent[1:-1], temporal_weight.shape[1])
    return (branch_time, back_time, sum_time)


def space_apply(act_pad, weight_space):
    rows_in = act_pad.shape[-3] - 2
    cols_in = act_pad.shape[-2] - 2
    groups = weight_space.shape[2]
    summed = None
    for row_tap in range(3):
        for col_tap in range(3):
            window = split_groups(
                act_pad[..., row_tap : row_tap + rows_in, col_tap : col_tap + cols_in, :], groups
            )
            partial_sum = jnp.einsum(
                "...gi,gio->...go",
                window,
                weight_space[row_tap, col_tap],
                preferred_element_type=jnp.float32,
            )
            summed = partial_sum if summed is None else summed + partial_sum
    return merge_groups(summed)


def space_back(cot_pad, weight_space):
    rows_in = cot_pad.shape[-3] - 2
    cols_in = cot_pad.shape[-2] - 2
    groups = weight_space.shape[2]
    summed = None
    for row_tap in range(3):
        for col_tap in range(3):
            window = cot_pad[
                ..., 2 - row_tap : 2 - row_tap + rows_in, 2 - col_tap : 2 - col_tap + cols_in, :
            ]
            window = split_groups(window, groups)
            partial_sum = jnp.einsum(
                "...go,gio->...gi",
                window,
                weight_space[row_tap, col_tap],
                preferred_element_type=jnp.float32,
            )
            summed = partial_sum if summed is None else summed + partial_sum
    return merge_groups(summed)


def space_wgrad(act_pad, cot_inner, groups):
    rows_in = cot_inner.shape[-3]
    cols_in = cot_inner.shape[-2]
    cot_split = split_groups(cot_inner, groups)
    result = []
    for row_tap in range(3):
        row_list = []
        for col_tap in range(3):
            window = split_groups(
                act_pad[..., row_tap : row_tap + rows_in, col_tap : col_tap + cols_in, :], groups
            )
            row_list.append(
                jnp.einsum(
                    "...gi,...go->gio", window, cot_split, preferred_element_type=jnp.float32
                )
            )
        result.append(jnp.stack(row_list))
    return jnp.stack(result)


def per_device(output_first_half, y_second, cot_first, cot_second, weight_space, temporal_weight):
    joined = jnp.stack([output_first_half, cot_second])
    rimmed = extended(joined, (("tm", 1),), 2)
    branch_time, back_time, sum_time = time_core(rimmed[0], rimmed[1], temporal_weight)
    cells_all = (
        output_first_half.shape[0]
        * output_first_half.shape[1]
        * output_first_half.shape[2]
        * lax.axis_size("tm")
        * lax.axis_size("row")
    )
    factor = 1.0 / math.sqrt(cells_all)
    recovered = (y_second.astype(jnp.float32) - branch_time.astype(jnp.float32)).astype(
        jnp.bfloat16
    )
    first_grad = (cot_first.astype(jnp.float32) + back_time.astype(jnp.float32)).astype(
        jnp.bfloat16
    )
    stacked = jnp.stack([recovered, first_grad])
    row_ext = extended(stacked, (("row", 2),), 1)
    col_pad = ((0, 0), (0, 0), (1, 1), (0, 0))
    act_pad = jax.nn.silu(jnp.pad(row_ext[0], col_pad).astype(jnp.float32)).astype(jnp.bfloat16)
    cot_pad = jnp.pad(row_ext[1], col_pad)
    first_rec = (output_first_half.astype(jnp.float32) - space_apply(act_pad, weight_space)).astype(
        jnp.bfloat16
    )
    back_sum = space_back(cot_pad, weight_space) * silu_slope(recovered.astype(jnp.float32))
    second_grad = (cot_second.astype(jnp.float32) + back_sum).astype(jnp.bfloat16)
    sum_space = space_wgrad(act_pad, first_grad, weight_space.shape[2])
    space_share, time_share = (
        lax.psum_scatter(sum_space.reshape(-1), ("tm", "row"), scatter_dimension=0, tiled=True),
        lax.psum_scatter(sum_time.reshape(-1), ("tm", "row"), scatter_dimension=0, tiled=True),
    )
    return (
        first_rec,
        recovered,
        first_grad,
        second_grad,
        space_share * factor,
        time_share * factor,
    )


def solution(mesh):
    in_specs = (
        P("tm", "row", None, None),
        P("tm", "row", None, None),
        P("tm", "row", None, None),
        P("tm", "row", None, None),
        P(),
        P(),
    )
    out_specs = (
        P("tm", "row", None, None),
        P("tm", "row", None, None),
        P("tm", "row", None, None),
        P("tm", "row", None, None),
        P(("tm", "row")),
        P(("tm", "row")),
    )
    return jax.shard_map(
        per_device, mesh=mesh, in_specs=in_specs, out_specs=out_specs, check_vma=False
    )
```

profile of v0, /device:TPU:0, one launch (start us, length us, event | category | flops | bytes accessed | tf_op | source)
XLA Modules:
  0.0 216.1 jit_solution(16467395215027182419)
XLA Ops:
  8.2 1.3 collective-permute-start.1
  9.5 5.5 %collective-permute-start = (bf16[2,2,1,64,320]{4,3,1,2,0:T(8,128)(2,1)S(1)}, bf16[2,2,1,64,320]{4,3,1,2,0:T(8,128)(2,1)S(1)}, u32[]{:S(2)}, u32[]{:S(2)}) collective-permute-start(bf16[2,2,1,64,320]{4,3,1,2,0:T(8,128)(2,1)S(1)} %pad_maximum_fusion.5), channel_id=1, source_target_pairs={{0,4},{4,8},{8,12},{12,16},{16,20},{20,24},{24,28},{1,5},{5,9},{9,... | collective-permute-start | bytes 491528 | tf_op jit(solution)/shard_map/ppermute | solution.py:18
  15.0 2.9 %collective-permute-done.1 = bf16[2,2,1,64,320]{4,3,1,2,0:T(8,128)(2,1)S(1)} collective-permute-done((bf16[2,2,1,64,320]{4,3,1,2,0:T(8,128)(2,1)S(1)}, bf16[2,2,1,64,320]{4,3,1,2,0:T(8,128)(2,1)S(1)}, u32[]{:S(2)}, u32[]{:S(2)}) %collective-permute-start.1) | collective-permute-done | bytes 163872 | tf_op jit(solution)/shard_map/ppermute | solution.py:19
  18.0 4.4 %collective-permute-done = bf16[2,2,1,64,320]{4,3,1,2,0:T(8,128)(2,1)S(1)} collective-permute-done((bf16[2,2,1,64,320]{4,3,1,2,0:T(8,128)(2,1)S(1)}, bf16[2,2,1,64,320]{4,3,1,2,0:T(8,128)(2,1)S(1)}, u32[]{:S(2)}, u32[]{:S(2)}) %collective-permute-start) | collective-permute-done | bytes 163872 | tf_op jit(solution)/shard_map/ppermute | solution.py:18
  26.9 1.3 collective-permute-start.3
  28.2 3.0 %collective-permute-start.2 = (bf16[2,2,1,64,320]{4,3,1,2,0:T(8,128)(2,1)S(1)}, bf16[2,2,1,64,320]{4,3,1,2,0:T(8,128)(2,1)S(1)}, u32[]{:S(2)}, u32[]{:S(2)}) collective-permute-start(bf16[2,2,1,64,320]{4,3,1,2,0:T(8,128)(2,1)S(1)} %pad_maximum_fusion.6), channel_id=1, source_target_pairs={{0,1},{1,2},{2,3},{4,5},{5,6},{6,7},{8,9},{9,10},{10,11},{12,13},{... | collective-permute-start | bytes 491528 | tf_op jit(solution)/shard_map/ppermute | solution.py:18
  36.9 1.1 convolution_add_fusion.15
  38.3 1.1 convolution_add_fusion.14
  39.8 1.1 convolution_add_fusion.13
  41.2 1.1 convolution_add_fusion.12
  42.7 1.1 convolution_add_fusion.11
  44.1 1.8 convolution_add_fusion.10
  46.3 1.2 convolution_add_fusion.9
  50.4 1.8 fusion.43
  52.3 1.6 reshape.407
  53.9 1.7 reshape.408
  55.6 1.6 reshape.409
  58.8 3.4 %reshape.417 = f32[460800]{0:T(1024)} reshape(f32[3,3,2,160,160]{4,3,2,1,0:T(8,128)S(1)} %pad_maximum_fusion) | data formatting | bytes 3686400 | tf_op jit(solution)/shard_map/reshape | solution.py:199
  62.2 1.4 convolution_add_fusion.7
  63.6 1.2 convolution_add_fusion.6
  64.8 1.1 convolution_add_fusion.5
  70.3 136.0 %all-reduce.7.cloned.1.call-done = (f32[460800]{0:T(1024)}, f32[245760]{0:T(1024)}) async-done(((f32[460800]{0:T(1024)}, f32[245760]{0:T(1024)}), (f32[460800]{0:T(1024)}, f32[245760]{0:T(1024)})) %all-reduce.7.cloned.1.call-update) | async-done | bytes 2826256
  206.3 1.6 dynamic-slice_multiply_fusion
  207.8 1.5 dynamic-slice_multiply_fusion.1
  (110 shorter events, 21.6 us)
Async XLA Ops:
  7.2 199.1 %all-reduce.7.cloned.1.call-start = ((), (), s32[]{:S(2)}) async-start(), calls=%async_computation | async-start | bytes 5652480
  8.2 9.8 %collective-permute-start.1 = (bf16[2,2,1,64,320]{4,3,1,2,0:T(8,128)(2,1)S(1)}, bf16[2,2,1,64,320]{4,3,1,2,0:T(8,128)(2,1)S(1)}, u32[]{:S(2)}, u32[]{:S(2)}) collective-permute-start(bf16[2,2,1,64,320]{4,3,1,2,0:T(8,128)(2,1)S(1)} %pad_maximum_fusion.5), channel_id=1, source_target_pairs={{4,0},{8,4},{12,8},{16,12},{20,16},{24,20},{28,24},{5,1},{9,5},{13... | collective-permute-start | bytes 491528 | tf_op jit(solution)/shard_map/ppermute | solution.py:19
  9.5 12.8 %collective-permute-start = (bf16[2,2,1,64,320]{4,3,1,2,0:T(8,128)(2,1)S(1)}, bf16[2,2,1,64,320]{4,3,1,2,0:T(8,128)(2,1)S(1)}, u32[]{:S(2)}, u32[]{:S(2)}) collective-permute-start(bf16[2,2,1,64,320]{4,3,1,2,0:T(8,128)(2,1)S(1)} %pad_maximum_fusion.5), channel_id=1, source_target_pairs={{0,4},{4,8},{8,12},{12,16},{16,20},{20,24},{24,28},{1,5},{5,9},{9,... | collective-permute-start | bytes 491528 | tf_op jit(solution)/shard_map/ppermute | solution.py:18
  23.5 1.0 copy-start.1
  25.7 1.0 copy-start.3
  25.8 1.0 copy-start.11
  26.9 6.9 %collective-permute-start.3 = (bf16[2,2,1,64,320]{4,3,1,2,0:T(8,128)(2,1)S(1)}, bf16[2,2,1,64,320]{4,3,1,2,0:T(8,128)(2,1)S(1)}, u32[]{:S(2)}, u32[]{:S(2)}) collective-permute-start(bf16[2,2,1,64,320]{4,3,1,2,0:T(8,128)(2,1)S(1)} %pad_maximum_fusion.6), channel_id=1, source_target_pairs={{1,0},{2,1},{3,2},{5,4},{6,5},{7,6},{9,8},{10,9},{11,10},{13,12},{... | collective-permute-start | bytes 491528 | tf_op jit(solution)/shard_map/ppermute | solution.py:19
  28.2 5.6 %collective-permute-start.2 = (bf16[2,2,1,64,320]{4,3,1,2,0:T(8,128)(2,1)S(1)}, bf16[2,2,1,64,320]{4,3,1,2,0:T(8,128)(2,1)S(1)}, u32[]{:S(2)}, u32[]{:S(2)}) collective-permute-start(bf16[2,2,1,64,320]{4,3,1,2,0:T(8,128)(2,1)S(1)} %pad_maximum_fusion.6), channel_id=1, source_target_pairs={{0,1},{1,2},{2,3},{4,5},{5,6},{6,7},{8,9},{9,10},{10,11},{12,13},{... | collective-permute-start | bytes 491528 | tf_op jit(solution)/shard_map/ppermute | solution.py:18
  49.4 7.8 %copy-start.10 = (bf16[2,1,64,320]{3,2,0,1:T(8,128)(2,1)S(1)}, bf16[2,1,64,320]{3,2,0,1:T(8,128)(2,1)}, u32[]{:S(2)}) copy-start(bf16[2,1,64,320]{3,2,0,1:T(8,128)(2,1)} %get-tuple-element.45) | copy-start | bytes 245764
  62.2 2.6 %copy-start = (bf16[3,3,2,160,160]{4,3,2,1,0:T(8,128)(2,1)S(1)}, bf16[3,3,2,160,160]{4,3,2,1,0:T(8,128)(2,1)}, u32[]{:S(2)}) copy-start(bf16[3,3,2,160,160]{4,3,2,1,0:T(8,128)(2,1)} %param.10) | copy-start | bytes 2764804
  62.2 3.7 %copy-start.5 = (bf16[2,64,2,160]{3,2,1,0:T(2,128)(2,1)S(1)}, bf16[2,64,2,160]{3,2,1,0:T(2,128)(2,1)}, u32[]{:S(2)}) copy-start(bf16[2,64,2,160]{3,2,1,0:T(2,128)(2,1)} %reshape.410) | copy-start | bytes 245764
  66.2 0.9 copy-start.9
  66.2 1.0 copy-start.8
  66.2 1.1 copy-start.7
  66.2 1.2 copy-start.6
  67.9 0.9 copy-start.2
  68.0 1.5 copy-start.4
  68.0 1.5 copy-start.12
Sparse Core Ops, SparseCore 0:
  66.3 139.9 all-reduce.6
where the time goes:
time: 217 us; the launch traced here: 216 us
  waiting for transfers between devices  143 us (66%)
  matrix products  20.4 us (9%)
  local copies, waits for them, and re-layouts  16.5 us (8%)
  between operations  14.7 us (7%)
  starting transfers between devices  11.2 us (5%)
  other arithmetic  10 us (5%)
    unnamed x2, waiting for transfers between devices  136 us
    dot_general x9, matrix products, space_apply(): jnp.einsum('...gi,gio->...go', window, weight_space[row_tap, col_tap], pr...  9.77 us
    another operation x24, local copies, waits for them, and re-layouts  9.59 us
    ppermute x2, starting transfers between devices, extended(): before = lax.ppermute(last, axis, up)  8.55 us
    dot_general x9, matrix products, space_back(): jnp.einsum('...go,gio->...gi', window, weight_space[row_tap, col_tap], pr...  6.51 us
    ppermute x2, waiting for transfers between devices, extended(): before = lax.ppermute(last, axis, up)  4.37 us
  transfers between devices with their start and end apart: 5, of which 3 were waited for; matrix products, arithmetic and copies ran while one was open for 3% of the time, Pallas kernels for 0%

commit v1 on v0

v1 whole, which is shorter than its diff:
```python
import functools
import math

import jax
import jax.numpy as jnp
from jax import lax
from jax.experimental import pallas as pl
from jax.experimental.pallas import tpu as pltpu
from jax.sharding import PartitionSpec as P

HAAR = 0.7071067811865476
LANES = 128
F32 = jnp.float32
BF16 = jnp.bfloat16


def round_up(value, unit):
    return (value + unit - 1) // unit * unit


def on_device(body, args, outs, scratch=(), flops=0):
    whole = pl.BlockSpec(memory_space=pltpu.VMEM)
    moved = sum(math.prod(a.shape) * a.dtype.itemsize for a in (*args, *outs))
    return pl.pallas_call(
        body,
        out_shape=outs,
        in_specs=[whole] * len(args),
        out_specs=[whole] * len(outs),
        scratch_shapes=list(scratch),
        compiler_params=pltpu.CompilerParams(vmem_limit_bytes=40 * 1024 * 1024),
        cost_estimate=pl.CostEstimate(flops=flops, bytes_accessed=moved, transcendentals=0),
    )(*args)


def shape(dims, dtype):
    return jax.ShapeDtypeStruct(tuple(dims), dtype)


def sigmoid(v):
    return 1.0 / (1.0 + jnp.exp(-v))


def silu_slope(v):
    s = sigmoid(v)
    return s * (1.0 + v * (1.0 - s))


def dot(left, right, left_dim, right_dim):
    return lax.dot_general(
        left, right, (((left_dim,), (right_dim,)), ((), ())), preferred_element_type=F32
    )


def squeezed(ref):
    even, odd = ref[0, 0].astype(F32), ref[1, 0].astype(F32)
    return jnp.concatenate([(even + odd) * HAAR, (even - odd) * HAAR], axis=-1)


def unsqueezed(packed):
    half = packed.shape[-1] // 2
    low, high = packed[:, :half], packed[:, half:]
    return (low + high) * HAAR, (low - high) * HAAR


def open_body(y_ref, cot_ref, out_ref):
    sq = squeezed(y_ref)
    cols = sq.shape[0]
    out_ref[:cols] = (sq * sigmoid(sq)).astype(BF16)
    out_ref[cols:] = squeezed(cot_ref).astype(BF16)


def time_body(own, before, after, y1, y2, c1, weight, x2_out, g1_out, packed_out):
    cols, ch = y2.shape[2:]
    groups, width = weight.shape[1:3]
    forth, back = [], []
    for q in range(groups):
        lanes = slice(q * width, (q + 1) * width)
        forth.append(
            dot(before[:cols, lanes], weight[0, q], 1, 0)
            + dot(own[:cols, lanes], weight[1, q], 1, 0)
            + dot(after[:cols, lanes], weight[2, q], 1, 0)
        )
        back.append(
            dot(after[cols:, lanes], weight[0, q], 1, 1)
            + dot(own[cols:, lanes], weight[1, q], 1, 1)
            + dot(before[cols:, lanes], weight[2, q], 1, 1)
        )
    branch = unsqueezed(jnp.concatenate(forth, axis=-1))
    back = unsqueezed(jnp.concatenate(back, axis=-1) * silu_slope(squeezed(y1)))
    frames = []
    for f in range(2):
        x2 = (y2[f, 0].astype(F32) - branch[f].astype(BF16).astype(F32)).astype(BF16)
        g1 = (c1[f, 0].astype(F32) + back[f].astype(BF16).astype(F32)).astype(BF16)
        x2_out[f, 0] = x2
        g1_out[f, 0] = g1
        v = x2.astype(F32)
        frames.append(jnp.concatenate([v * sigmoid(v), g1.astype(F32)], axis=-1))
    packed_out[...] = jnp.concatenate(frames, axis=0).T.astype(BF16)


def time_terms(own, before, after, total):
    cols = own.shape[0] // 2
    width = total.shape[1]
    groups = own.shape[1] // width
    for k, ref in enumerate((before, own, after)):
        for q in range(groups):
            lanes = slice(q * width, (q + 1) * width)
            term = dot(ref[:cols, lanes].astype(F32).T.astype(BF16), own[cols:, lanes], 1, 0)
            total[pl.ds((k * groups + q) * width, width), :] = term


def time_sum_body(offsets, rows, own, before, after, keep, send, total):
    time_terms(own, before, after, total)
    me, peers, steps = lax.axis_index("row"), lax.axis_size("row"), lax.axis_size("tm")
    held = keep.shape[2]
    for u, offset in enumerate(offsets):
        for t in range(steps):
            mine = (t * peers + (me ^ offset)) * rows
            other = (t * peers + (me ^ offset ^ 1)) * rows
            keep[u, t] = total[pl.ds(mine, held), :]
            send[u, t] = total[pl.ds(other, held), :].astype(BF16)


def time_sum_whole_body(own, before, after, total):
    time_terms(own, before, after, total)


def fold_body(kept, came, keep, send):
    half = keep.shape[0]
    keep[...] = kept[:half] + came[:half].astype(F32)
    send[...] = (kept[half:] + came[half:].astype(F32)).astype(BF16)


def space_terms(slots, rows_ref, cols, store):
    peers = len(slots)
    me = lax.axis_index("row")
    for k, ref in enumerate(slots):
        rows_ref[me ^ k] = ref[...]
    ch = rows_ref.shape[1] // 2
    column = lax.broadcasted_iota(jnp.int32, (ch, LANES), 1) % cols
    act, shifts = [], ([], [], [])
    for r in range(peers):
        act.append(rows_ref[r, :ch])
        cot = rows_ref[r, ch:]
        wide = cot.astype(F32)
        later = jnp.where(column == cols - 1, 0.0, pltpu.roll(wide, LANES - 1, 1))
        sooner = jnp.where(column == 0, 0.0, pltpu.roll(wide, 1, 1))
        for held, value in zip(shifts, (later.astype(BF16), cot, sooner.astype(BF16))):
            held.append(value)
    for a in range(3):
        pairs = [(r, r - a + 1) for r in range(peers) if 0 <= r - a + 1 < peers]
        left = jnp.concatenate([act[r] for r, _ in pairs], axis=1)
        for b in range(3):
            right = jnp.concatenate([shifts[b][r] for _, r in pairs], axis=1)
            store(a * 3 + b, left, right)


def segments(width):
    period = LANES // math.gcd(width, LANES)
    found = []
    for j in range(period * width // LANES):
        row, lane = [], 0
        while lane < LANES:
            at = j * LANES + lane
            source, column = divmod(at, width)
            tile, first = divmod(column, LANES)
            row.append((lane, source, tile, (lane - first) % LANES))
            lane += min(LANES - first, width - column, LANES - lane)
        found.append(row)
    return period, found


def space_sum_body(groups, rows, *refs):
    peers, steps = lax.axis_size("row"), lax.axis_size("tm")
    slots, (kept, came), refs = refs[:peers], refs[peers : peers + 2], refs[peers + 2 :]
    mine, sends, (rows_ref, main, rest) = refs[0], refs[1:steps], refs[steps:]
    ch = rows_ref.shape[1] // 2
    width = ch // groups

    def store(tap, left, right):
        for q in range(groups):
            part = slice(q * width, (q + 1) * width)
            term = dot(left[part], right[part], 1, 1)
            at = pl.ds((tap * groups + q) * width, width)
            main[at, :] = term[:, :LANES]
            rest[at, : width - LANES] = term[:, LANES:]

    space_terms(slots, rows_ref, LANES // 2, store)
    period, layout = segments(width)
    held = round_up(-(-rows // period), 8)
    lane = lax.broadcasted_iota(jnp.int32, (held, LANES), 1)
    here, me = lax.axis_index("tm"), lax.axis_index("row")
    early = kept.shape[2]
    for k in range(steps):
        t = here ^ k
        start = (t * peers + me) * rows
        rolled = {}

        def source(j, tile, amount):
            if (j, tile, amount) not in rolled:
                ref = (main, rest)[tile]
                value = ref[pl.ds(start + j, held, stride=period), :]
                rolled[j, tile, amount] = pltpu.roll(value, amount, 1) if amount else value
            return rolled[j, tile, amount]

        parts = [kept[0, t] + came[0, t].astype(F32)]
        for row in layout:
            value = None
            for first, j, tile, amount in row:
                piece = source(j, tile, amount)
                value = piece if value is None else jnp.where(lane < first, value, piece)
            parts.append(value)
        blank = mine.shape[0] - early - held * len(layout)
        if blank:
            parts.append(jnp.zeros((blank, LANES), F32))
        piece = jnp.concatenate(parts, axis=0)
        if k == 0:
            mine[...] = piece
        else:
            sends[k - 1][...] = piece.astype(BF16)


def space_sum_whole_body(groups, *refs):
    peers = lax.axis_size("row")
    slots, (total, rows_ref) = refs[:peers], refs[peers:]
    ch = rows_ref.shape[1] // 2
    width = ch // groups

    def store(tap, left, right):
        for q in range(groups):
            part = slice(q * width, (q + 1) * width)
            at = pl.ds((tap * groups + q) * width, width)
            total[at, :] = dot(left[part], right[part], 1, 1)

    space_terms(slots, rows_ref, LANES // 2, store)


def final_body(factor, early, period, stride, *refs):
    (mine, *came), (space_out, time_out) = refs[:-2], refs[-2:]
    total = mine[...]
    for ref in came:
        total = total + ref[...].astype(F32)
    total = total * factor
    time_out[...] = total[: time_out.shape[0]]
    held = space_out.shape[0] // stride
    tall = (total.shape[0] - early) // stride // 8 * 8
    for j in range(stride):
        first = early + j * tall
        space_out[pl.ds(j, held, stride=stride), :] = total[first : first + held]


def space_body(*refs):
    peers = lax.axis_size("row")
    slots, (y1, c2, x2, weight, x1_out, g2_out, rows_ref) = refs[:peers], refs[peers:]
    me = lax.axis_index("row")
    cols, ch = y1.shape[2:]
    groups, width = weight.shape[2:4]
    rows_ref[0] = jnp.zeros(rows_ref.shape[1:], BF16)
    rows_ref[peers + 1] = jnp.zeros(rows_ref.shape[1:], BF16)
    for k, ref in enumerate(slots):
        rows_ref[(me ^ k) + 1] = ref[...]
    column = lax.broadcasted_iota(jnp.int32, (LANES, width), 0) % cols
    forth, back = [None] * groups, [None] * groups
    for a in range(3):
        row = rows_ref[me + a].astype(F32).T
        for q in range(groups):
            for first, sums in ((0, forth), (ch, back)):
                value = row[:, first + q * width : first + (q + 1) * width]
                sooner = jnp.where(column == 0, 0.0, pltpu.roll(value, 1, 0))
                later = jnp.where(column == cols - 1, 0.0, pltpu.roll(value, LANES - 1, 0))
                for b, moved in enumerate((sooner, value, later)):
                    if first:
                        term = dot(moved.astype(BF16), weight[2 - a, 2 - b, q], 1, 1)
                    else:
                        term = dot(moved.astype(BF16), weight[a, b, q], 1, 0)
                    sums[q] = term if sums[q] is None else sums[q] + term
    forth = jnp.concatenate(forth, axis=-1)
    back = jnp.concatenate(back, axis=-1)
    for f in range(2):
        part = slice(f * cols, (f + 1) * cols)
        x1_out[f, 0] = (y1[f, 0].astype(F32) - forth[part]).astype(BF16)
        slope = silu_slope(x2[f, 0].astype(F32))
        g2_out[f, 0] = (c2[f, 0].astype(F32) + slope * back[part]).astype(BF16)


def swap(x, axis, bit):
    return lax.ppermute(x, axis, [(i, i ^ bit) for i in range(lax.axis_size(axis))])


def row_offsets(bits):
    if not bits:
        return [0]
    rest = row_offsets(bits[1:])
    return rest + [o ^ bits[0] for o in rest]


def per_device(y1, y2, c1, c2, weight_space, temporal_weight):
    steps, peers = lax.axis_size("tm"), lax.axis_size("row")
    devices = steps * peers
    frames, rows_here, cols, ch = y1.shape
    groups = weight_space.shape[2]
    width = ch // groups
    taps = weight_space.shape[0] * weight_space.shape[1]
    factor = 1.0 / math.sqrt(frames * rows_here * cols * devices)
    time_groups, time_width = temporal_weight.shape[1:3]
    time_rows = 3 * time_groups * time_width
    space_rows = taps * ch

    packed = on_device(open_body, (y1, c2), [shape((2 * cols, 2 * ch), BF16)])[0]
    up = [(i, i + 1) for i in range(steps - 1)]
    before = lax.ppermute(packed, "tm", up)
    after = lax.ppermute(packed, "tm", [(j, i) for i, j in up])
    x2, g1, held = on_device(
        time_body,
        (packed, before, after, y1, y2, c1, temporal_weight),
        [shape(y1.shape, BF16), shape(y1.shape, BF16), shape((2 * ch, 2 * cols), BF16)],
    )

    slots = {0: held}
    bits = [1 << i for i in range(peers.bit_length() - 1)]
    for bit in reversed(bits):
        for k in list(slots):
            slots[k ^ bit] = swap(slots[k], "row", bit)
    gathered = [slots[k] for k in range(peers)]

    even = time_rows % devices == 0 and space_rows % devices == 0
    if even:
        rows = time_rows // devices
        tall = round_up(rows, 16)
        offsets = row_offsets(bits[1:])
        block = (len(offsets), steps, tall, time_width)
        kept, sent = on_device(
            functools.partial(time_sum_body, offsets, rows),
            (packed, before, after),
            [shape(block, F32), shape(block, BF16)],
            [pltpu.VMEM((round_up(time_rows + tall, 8), time_width), F32)],
        )
        came = swap(sent, "row", 1)
        for bit in bits[1:]:
            block = (block[0] // 2, *block[1:])
            kept, sent = on_device(fold_body, (kept, came), [shape(block, F32), shape(block, BF16)])
            came = swap(sent, "row", bit)

        rows = space_rows // devices
        period, layout = segments(width)
        deep = round_up(tall + round_up(-(-rows // period), 8) * len(layout), 16)
        piece = (deep, LANES)
        scratch = (round_up(space_rows + 8 * period + rows, 8), LANES)
        mine, *sends = on_device(
            functools.partial(space_sum_body, groups, rows),
            (*gathered, kept, came),
            [shape(piece, F32)] + [shape(piece, BF16)] * (steps - 1),
            [pltpu.VMEM((peers, 2 * ch, 2 * cols), BF16)] + [pltpu.VMEM(scratch, F32)] * 2,
        )
        arrived = [swap(sends[k - 1], "tm", k) for k in range(1, steps)]
        full = -(-rows // period) * len(layout)
        space_share, time_share = on_device(
            functools.partial(final_body, factor, tall, period, len(layout)),
            (mine, *arrived),
            [shape((full, LANES), F32), shape((time_rows // devices, time_width), F32)],
        )
        space_share = space_share.reshape(-1)[: rows * width]
        time_share = time_share.reshape(-1)
    else:
        total = on_device(
            time_sum_whole_body, (packed, before, after), [shape((time_rows, time_width), F32)]
        )[0]
        time_share = factor * lax.psum_scatter(
            total.reshape(-1), ("tm", "row"), scatter_dimension=0, tiled=True
        )
        total = on_device(
            functools.partial(space_sum_whole_body, groups),
            gathered,
            [shape((space_rows, width), F32)],
            [pltpu.VMEM((peers, 2 * ch, 2 * cols), BF16)],
        )[0]
        total = total.reshape(steps, peers, -1)
        total = lax.dynamic_index_in_dim(total, lax.axis_index("row"), 1, keepdims=False)
        space_share = factor * lax.psum_scatter(
            total.reshape(-1), "tm", scatter_dimension=0, tiled=True
        )

    x1, g2 = on_device(
        space_body,
        (*gathered, y1, c2, x2, weight_space),
        [shape(y1.shape, BF16), shape(y1.shape, BF16)],
        [pltpu.VMEM((peers + 2, 2 * ch, 2 * cols), BF16)],
    )
    return x1, x2, g1, g2, space_share, time_share


def solution(mesh):
    video = P("tm", "row", None, None)
    share = P(("tm", "row"))
    return jax.shard_map(
        per_device,
        mesh=mesh,
        in_specs=(video,) * 4 + (P(), P()),
        out_specs=(video,) * 4 + (share, share),
        check_vma=False,
    )
```

time: 217 us -> 52 us (0.24)
  waiting for transfers between devices: 143 us -> 20.9 us
  matrix products: 20.4 us -> 0 us
  between operations: 14.7 us -> 0.76 us
  local copies, waits for them, and re-layouts: 16.5 us -> 4.71 us
  other arithmetic: 10 us -> 0 us
  starting transfers between devices: 11.2 us -> 19.5 us
  Pallas kernels: 0 us -> 5.88 us
    unnamed x2 -> x0, waiting for transfers between devices: 136 us -> none
    dot_general x36 -> x0, matrix products: 20.4 us -> none  [the longest x9 9.77 us: space_apply(): jnp.einsum('...gi,gio->...go', window, weight_space[row_tap, col_tap], pr...]
    ppermute x4 -> x14, waiting for transfers between devices: 7.31 us -> 20.9 us  [the longest x12 14.6 us: swap(): lax.ppermute(x, axis, [(i, i ^ bit) for i in range(lax.axis_size(axis))])]
    another operation x24 -> x0, local copies, waits for them, and re-layouts: 9.59 us -> none
    ppermute x4 -> x14, starting transfers between devices: 11.1 us -> 19.5 us  [the longest x12 13.4 us: swap(): lax.ppermute(x, axis, [(i, i ^ bit) for i in range(lax.axis_size(axis))])]
    pallas_call x0 -> x7, Pallas kernels: none -> 5.88 us  [on_device(): pl.pallas_call(body, out_shape=outs, in_specs=[whole] * len(args), out_sp...]
    unnamed x26 -> x18, local copies, waits for them, and re-layouts: 0.69 us -> 4.71 us
    reshape x5 -> x0, local copies, waits for them, and re-layouts: 3.94 us -> none  [the longest x1 3.37 us: per_device(): sum_space.reshape(-1)]
  transfers between devices with their start and end apart: 5 -> 14, of which waited for: 3 -> 6; matrix products, arithmetic and copies ran while one was open for 3% -> 0% of each run, Pallas kernels for 0% -> 7%
where the time goes in v1:
time: 52 us; the launch traced here: 51.7 us
  waiting for transfers between devices  20.9 us (40%)
  starting transfers between devices  19.5 us (38%)
  Pallas kernels  5.88 us (11%)
  local copies, waits for them, and re-layouts  4.71 us (9%)
  between operations  0.76 us (1%)
    ppermute x12, waiting for transfers between devices, swap(): lax.ppermute(x, axis, [(i, i ^ bit) for i in range(lax.axis_size(axis))])  14.6 us
    ppermute x12, starting transfers between devices, swap(): lax.ppermute(x, axis, [(i, i ^ bit) for i in range(lax.axis_size(axis))])  13.4 us
    pallas_call x7, Pallas kernels, on_device(): pl.pallas_call(body, out_shape=outs, in_specs=[whole] * len(args), out_sp...  5.88 us
    ppermute x1, starting transfers between devices, per_device(): before = lax.ppermute(packed, 'tm', up)  4.88 us
    unnamed x18, local copies, waits for them, and re-layouts  4.71 us
    ppermute x1, waiting for transfers between devices, per_device(): after = lax.ppermute(packed, 'tm', [(j, i) for i, j in up])  4.12 us
    ppermute x1, waiting for transfers between devices, per_device(): before = lax.ppermute(packed, 'tm', up)  2.13 us
    ppermute x1, starting transfers between devices, per_device(): after = lax.ppermute(packed, 'tm', [(j, i) for i, j in up])  1.29 us
  transfers between devices with their start and end apart: 14, of which 6 were waited for; matrix products, arithmetic and copies ran while one was open for 0% of the time, Pallas kernels for 7%

profile of v1, /device:TPU:0, one launch (start us, length us, event | category | flops | bytes accessed | tf_op | source)
XLA Modules:
  0.0 51.7 jit_solution(10500292174294001917)
XLA Ops:
  0.6 0.9 %copy-done.1 = bf16[2,1,64,320]{3,2,1,0:T(8,128)(2,1)S(1)} copy-done((bf16[2,1,64,320]{3,2,1,0:T(8,128)(2,1)S(1)}, bf16[2,1,64,320]{3,2,1,0:T(8,128)(2,1)}, u32[]{:S(2)}) %copy-start.1) | copy-done | bytes 81944
  1.5 0.9 %copy-done.4 = bf16[2,1,64,320]{3,2,1,0:T(8,128)(2,1)S(1)} copy-done((bf16[2,1,64,320]{3,2,1,0:T(8,128)(2,1)S(1)}, bf16[2,1,64,320]{3,2,1,0:T(8,128)(2,1)}, u32[]{:S(2)}) %copy-start.4) | copy-done | bytes 81944
  2.5 4.9 %collective-permute-start = (bf16[128,640]{1,0:T(8,128)(2,1)S(1)}, bf16[128,640]{1,0:T(8,128)(2,1)S(1)}, u32[]{:S(2)}, u32[]{:S(2)}) collective-permute-start(bf16[128,640]{1,0:T(8,128)(2,1)S(1)} %shard_map.109.own), channel_id=1, source_target_pairs={{0,4},{4,8},{8,12},{12,16},{16,20},{20,24},{24,28},{1,5},{5,9},{9,... | collective-permute-start | bytes 491528 | tf_op jit(solution)/shard_map/ppermute | solution.py:311
  7.4 1.3 %collective-permute-start.1 = (bf16[128,640]{1,0:T(8,128)(2,1)S(1)}, bf16[128,640]{1,0:T(8,128)(2,1)S(1)}, u32[]{:S(2)}, u32[]{:S(2)}) collective-permute-start(bf16[128,640]{1,0:T(8,128)(2,1)S(1)} %shard_map.109.own), channel_id=1, source_target_pairs={{4,0},{8,4},{12,8},{16,12},{20,16},{24,20},{28,24},{5,1},{9,5},{13... | collective-permute-start | bytes 491528 | tf_op jit(solution)/shard_map/ppermute | solution.py:312
  8.7 2.1 %collective-permute-done.before = bf16[128,640]{1,0:T(8,128)(2,1)S(1)} collective-permute-done((bf16[128,640]{1,0:T(8,128)(2,1)S(1)}, bf16[128,640]{1,0:T(8,128)(2,1)S(1)}, u32[]{:S(2)}, u32[]{:S(2)}) %collective-permute-start) | collective-permute-done | bytes 163872 | tf_op jit(solution)/shard_map/ppermute | solution.py:311
  10.9 4.1 %collective-permute-done.1.after = bf16[128,640]{1,0:T(8,128)(2,1)S(1)} collective-permute-done((bf16[128,640]{1,0:T(8,128)(2,1)S(1)}, bf16[128,640]{1,0:T(8,128)(2,1)S(1)}, u32[]{:S(2)}, u32[]{:S(2)}) %collective-permute-start.1) | collective-permute-done | bytes 163872 | tf_op jit(solution)/shard_map/ppermute | solution.py:312
  15.5 1.1 %copy-done.3 = bf16[3,5,128,128]{3,2,1,0:T(8,128)(2,1)S(1)} copy-done((bf16[3,5,128,128]{3,2,1,0:T(8,128)(2,1)S(1)}, bf16[3,5,128,128]{3,2,1,0:T(8,128)(2,1)}, u32[]{:S(2)}) %copy-start.3) | copy-done | bytes 491544
  16.7 0.9 %copy-done.7 = bf16[2,1,64,320]{3,2,1,0:T(8,128)(2,1)S(1)} copy-done((bf16[2,1,64,320]{3,2,1,0:T(8,128)(2,1)S(1)}, bf16[2,1,64,320]{3,2,1,0:T(8,128)(2,1)}, u32[]{:S(2)}) %copy-start.7) | copy-done | bytes 81944
  17.5 0.9 %copy-done.8 = bf16[2,1,64,320]{3,2,1,0:T(8,128)(2,1)S(1)} copy-done((bf16[2,1,64,320]{3,2,1,0:T(8,128)(2,1)S(1)}, bf16[2,1,64,320]{3,2,1,0:T(8,128)(2,1)}, u32[]{:S(2)}) %copy-start.8) | copy-done | bytes 81944
  18.4 1.3 %shard_map.110 = (bf16[2,1,64,320]{3,2,1,0:T(8,128)(2,1)}, bf16[2,1,64,320]{3,2,1,0:T(8,128)(2,1)}, bf16[640,128]{1,0:T(8,128)(2,1)S(1)}) custom-call(bf16[128,640]{1,0:T(8,128)(2,1)S(1)} %shard_map.109.own, bf16[128,640]{1,0:T(8,128)(2,1)S(1)} %collective-permute-done.before, bf16[128,640]{1,0:T(8,128)(2,1)S(1)} %collective-permute-done.1.after, ...), custom_call_target="tpu_custom_call" | custom-call | bytes 1556480 | tf_op jit(solution)/shard_map/pallas_call | solution.py:24
  19.7 1.5 %collective-permute-start.3 = (bf16[640,128]{1,0:T(8,128)(2,1)S(1)}, bf16[640,128]{1,0:T(8,128)(2,1)S(1)}, u32[]{:S(2)}, u32[]{:S(2)}) collective-permute-start(bf16[640,128]{1,0:T(8,128)(2,1)S(1)} %get-tuple-element.25.refs_0_), channel_id=1, source_target_pairs={{0,2},{1,3},{2,0},{3,1},{4,6},{5,7},{6,4},{7,5},{8,10},{9,11},{10,... | collective-permute-start | bytes 491528 | tf_op jit(solution)/shard_map/ppermute | solution.py:287
  21.3 4.9 %collective-permute-done.3.refs_2_ = bf16[640,128]{1,0:T(8,128)(2,1)S(1)} collective-permute-done((bf16[640,128]{1,0:T(8,128)(2,1)S(1)}, bf16[640,128]{1,0:T(8,128)(2,1)S(1)}, u32[]{:S(2)}, u32[]{:S(2)}) %collective-permute-start.3) | collective-permute-done | bytes 163872 | tf_op jit(solution)/shard_map/ppermute | solution.py:287
  26.3 1.6 %collective-permute-start.6 = (bf16[1,8,64,128]{3,2,1,0:T(8,128)(2,1)S(1)}, bf16[1,8,64,128]{3,2,1,0:T(8,128)(2,1)S(1)}, u32[]{:S(2)}, u32[]{:S(2)}) collective-permute-start(bf16[1,8,64,128]{3,2,1,0:T(8,128)(2,1)S(1)} %get-tuple-element.33), channel_id=1, source_target_pairs={{0,2},{1,3},{2,0},{3,1},{4,6},{5,7},{6,4},{7,5},{8,10},{9,11},{10,... | collective-permute-start | bytes 393224 | tf_op jit(solution)/shard_map/ppermute | solution.py:287
  27.8 4.4 %collective-permute-done.6.refs_5_ = bf16[1,8,64,128]{3,2,1,0:T(8,128)(2,1)S(1)} collective-permute-done((bf16[1,8,64,128]{3,2,1,0:T(8,128)(2,1)S(1)}, bf16[1,8,64,128]{3,2,1,0:T(8,128)(2,1)S(1)}, u32[]{:S(2)}, u32[]{:S(2)}) %collective-permute-start.6) | collective-permute-done | bytes 131104 | tf_op jit(solution)/shard_map/ppermute | solution.py:287
  32.2 1.2 %shard_map.114 = (f32[192,128]{1,0:T(8,128)S(1)}, bf16[192,128]{1,0:T(8,128)(2,1)S(1)}, bf16[192,128]{1,0:T(8,128)(2,1)S(1)}, bf16[192,128]{1,0:T(8,128)(2,1)S(1...) custom-call(bf16[640,128]{1,0:T(8,128)(2,1)S(1)} %get-tuple-element., ...), custom_call_target="tpu_custom_call" | custom-call | bytes 1490944 | tf_op jit(solution)/shard_map/pallas_call | solution.py:24
  33.5 3.9 %collective-permute-start.10 = (bf16[192,128]{1,0:T(8,128)(2,1)S(1)}, bf16[192,128]{1,0:T(8,128)(2,1)S(1)}, u32[]{:S(2)}, u32[]{:S(2)}) collective-permute-start(bf16[192,128]{1,0:T(8,128)(2,1)S(1)} %get-tuple-element.38), channel_id=1, source_target_pairs={{0,16},{4,20},{8,24},{12,28},{16,0},{20,4},{24,8},{28,12},{1,17},{... | collective-permute-start | bytes 147464 | tf_op jit(solution)/shard_map/ppermute | solution.py:287
  37.4 0.9 %collective-permute-start.11 = (bf16[192,128]{1,0:T(8,128)(2,1)S(1)}, bf16[192,128]{1,0:T(8,128)(2,1)S(1)}, u32[]{:S(2)}, u32[]{:S(2)}) collective-permute-start(bf16[192,128]{1,0:T(8,128)(2,1)S(1)} %get-tuple-element.39), channel_id=1, source_target_pairs={{0,20},{4,16},{8,28},{12,24},{16,4},{20,0},{24,12},{28,8},{1,21},{... | collective-permute-start | bytes 147464 | tf_op jit(solution)/shard_map/ppermute | solution.py:287
  38.3 2.0 %collective-permute-start.12 = (bf16[192,128]{1,0:T(8,128)(2,1)S(1)}, bf16[192,128]{1,0:T(8,128)(2,1)S(1)}, u32[]{:S(2)}, u32[]{:S(2)}) collective-permute-start(bf16[192,128]{1,0:T(8,128)(2,1)S(1)} %get-tuple-element.40), channel_id=1, source_target_pairs={{0,24},{4,28},{8,16},{12,20},{16,8},{20,12},{24,0},{28,4},{1,25},{... | collective-permute-start | bytes 147464 | tf_op jit(solution)/shard_map/ppermute | solution.py:287
  40.3 1.9 %collective-permute-start.13 = (bf16[192,128]{1,0:T(8,128)(2,1)S(1)}, bf16[192,128]{1,0:T(8,128)(2,1)S(1)}, u32[]{:S(2)}, u32[]{:S(2)}) collective-permute-start(bf16[192,128]{1,0:T(8,128)(2,1)S(1)} %get-tuple-element.41), channel_id=1, source_target_pairs={{0,28},{4,24},{8,20},{12,16},{16,12},{20,8},{24,4},{28,0},{1,29},{... | collective-permute-start | bytes 147464 | tf_op jit(solution)/shard_map/ppermute | solution.py:287
  42.2 1.4 %collective-permute-start.7 = (bf16[192,128]{1,0:T(8,128)(2,1)S(1)}, bf16[192,128]{1,0:T(8,128)(2,1)S(1)}, u32[]{:S(2)}, u32[]{:S(2)}) collective-permute-start(bf16[192,128]{1,0:T(8,128)(2,1)S(1)} %get-tuple-element.35), channel_id=1, source_target_pairs={{0,4},{4,0},{8,12},{12,8},{16,20},{20,16},{24,28},{28,24},{1,5},{5... | collective-permute-start | bytes 147464 | tf_op jit(solution)/shard_map/ppermute | solution.py:287
  43.6 2.5 %collective-permute-done.11.refs_5_ = bf16[192,128]{1,0:T(8,128)(2,1)S(1)} collective-permute-done((bf16[192,128]{1,0:T(8,128)(2,1)S(1)}, bf16[192,128]{1,0:T(8,128)(2,1)S(1)}, u32[]{:S(2)}, u32[]{:S(2)}) %collective-permute-start.11) | collective-permute-done | bytes 49184 | tf_op jit(solution)/shard_map/ppermute | solution.py:287
  46.1 2.1 %shard_map.111 = (bf16[2,1,64,320]{3,2,1,0:T(8,128)(2,1)}, bf16[2,1,64,320]{3,2,1,0:T(8,128)(2,1)}) custom-call(bf16[640,128]{1,0:T(8,128)(2,1)S(1)} %get-tuple-element.25.refs_0_, bf16[640,128]{1,0:T(8,128)(2,1)S(1)} %collective-permute-done.2.refs_1_, bf16[640,128]{1,0:T(8,128)(2,1)S(1)} %collective-permute-done.3.refs_2_, ...), custom_call_target="tpu_custom_call" | custom-call | bytes 1986560 | tf_op jit(solution)/shard_map/pallas_call | solution.py:24
  48.3 2.8 %collective-permute-done.9.refs_3_ = bf16[192,128]{1,0:T(8,128)(2,1)S(1)} collective-permute-done((bf16[192,128]{1,0:T(8,128)(2,1)S(1)}, bf16[192,128]{1,0:T(8,128)(2,1)S(1)}, u32[]{:S(2)}, u32[]{:S(2)}) %collective-permute-start.9) | collective-permute-done | bytes 49184 | tf_op jit(solution)/shard_map/ppermute | solution.py:287
  51.1 0.7 %shard_map.115 = (f32[115,128]{1,0:T(8,128)}, f32[60,128]{1,0:T(8,128)}) custom-call(f32[192,128]{1,0:T(8,128)S(1)} %get-tuple-element.34.refs_0_, bf16[192,128]{1,0:T(8,128)(2,1)S(1)} %collective-permute-done.7.refs_1_, bf16[192,128]{1,0:T(8,128)(2,1)S(1)} %collective-permute-done.8.refs_2_, bf16[192,128]{1,0:T(8,128)(2,1)S(1)} %collective-permute-done.9.refs_3_, ...), custom_call_target="tpu_custom_call" | custom-call | bytes 531968 | tf_op jit(solution)/shard_map/pallas_call | solution.py:24
  (29 shorter events, 0.8 us)
Async XLA Ops:
  0.6 0.9 %copy-start.1 = (bf16[2,1,64,320]{3,2,1,0:T(8,128)(2,1)S(1)}, bf16[2,1,64,320]{3,2,1,0:T(8,128)(2,1)}, u32[]{:S(2)}) copy-start(bf16[2,1,64,320]{3,2,1,0:T(8,128)(2,1)} %refs_4_.1) | copy-start | bytes 245764
  1.5 0.9 %copy-start.4 = (bf16[2,1,64,320]{3,2,1,0:T(8,128)(2,1)S(1)}, bf16[2,1,64,320]{3,2,1,0:T(8,128)(2,1)}, u32[]{:S(2)}) copy-start(bf16[2,1,64,320]{3,2,1,0:T(8,128)(2,1)} %refs_5_.1) | copy-start | bytes 245764
  2.5 8.3 %collective-permute-start = (bf16[128,640]{1,0:T(8,128)(2,1)S(1)}, bf16[128,640]{1,0:T(8,128)(2,1)S(1)}, u32[]{:S(2)}, u32[]{:S(2)}) collective-permute-start(bf16[128,640]{1,0:T(8,128)(2,1)S(1)} %shard_map.109.own), channel_id=1, source_target_pairs={{0,4},{4,8},{8,12},{12,16},{16,20},{20,24},{24,28},{1,5},{5,9},{9,... | collective-permute-start | bytes 491528 | tf_op jit(solution)/shard_map/ppermute | solution.py:311
  7.4 7.6 %collective-permute-start.1 = (bf16[128,640]{1,0:T(8,128)(2,1)S(1)}, bf16[128,640]{1,0:T(8,128)(2,1)S(1)}, u32[]{:S(2)}, u32[]{:S(2)}) collective-permute-start(bf16[128,640]{1,0:T(8,128)(2,1)S(1)} %shard_map.109.own), channel_id=1, source_target_pairs={{4,0},{8,4},{12,8},{16,12},{20,16},{24,20},{28,24},{5,1},{9,5},{13... | collective-permute-start | bytes 491528 | tf_op jit(solution)/shard_map/ppermute | solution.py:312
  15.4 30.7 %copy-start = (bf16[3,3,2,160,160]{4,3,2,1,0:T(8,128)(2,1)S(1)}, bf16[3,3,2,160,160]{4,3,2,1,0:T(8,128)(2,1)}, u32[]{:S(2)}) copy-start(bf16[3,3,2,160,160]{4,3,2,1,0:T(8,128)(2,1)} %refs_7_.1) | copy-start | bytes 2764804
  15.4 30.7 %copy-start.2 = (bf16[2,1,64,320]{3,2,1,0:T(8,128)(2,1)S(1)}, bf16[2,1,64,320]{3,2,1,0:T(8,128)(2,1)}, u32[]{:S(2)}) copy-start(bf16[2,1,64,320]{3,2,1,0:T(8,128)(2,1)} %refs_4_.1) | copy-start | bytes 245764
  15.4 10.8 %collective-permute-start.5 = (bf16[2,8,64,128]{3,2,1,0:T(8,128)(2,1)S(1)}, bf16[2,8,64,128]{3,2,1,0:T(8,128)(2,1)S(1)}, u32[]{:S(2)}, u32[]{:S(2)}) collective-permute-start(bf16[2,8,64,128]{3,2,1,0:T(8,128)(2,1)S(1)} %get-tuple-element.31), channel_id=1, source_target_pairs={{0,1},{1,0},{2,3},{3,2},{4,5},{5,4},{6,7},{7,6},{8,9},{9,8},{10,11... | collective-permute-start | bytes 786440 | tf_op jit(solution)/shard_map/ppermute | solution.py:287
  15.5 1.1 %copy-start.3 = (bf16[3,5,128,128]{3,2,1,0:T(8,128)(2,1)S(1)}, bf16[3,5,128,128]{3,2,1,0:T(8,128)(2,1)}, u32[]{:S(2)}) copy-start(bf16[3,5,128,128]{3,2,1,0:T(8,128)(2,1)} %weight.1) | copy-start | bytes 1474564
  16.7 0.9 %copy-start.7 = (bf16[2,1,64,320]{3,2,1,0:T(8,128)(2,1)S(1)}, bf16[2,1,64,320]{3,2,1,0:T(8,128)(2,1)}, u32[]{:S(2)}) copy-start(bf16[2,1,64,320]{3,2,1,0:T(8,128)(2,1)} %y2.1) | copy-start | bytes 245764
  17.5 0.9 %copy-start.8 = (bf16[2,1,64,320]{3,2,1,0:T(8,128)(2,1)S(1)}, bf16[2,1,64,320]{3,2,1,0:T(8,128)(2,1)}, u32[]{:S(2)}) copy-start(bf16[2,1,64,320]{3,2,1,0:T(8,128)(2,1)} %c1.1) | copy-start | bytes 245764
  18.4 27.6 %copy-start.5 = (bf16[2,1,64,320]{3,2,1,0:T(8,128)(2,1)S(1)}, bf16[2,1,64,320]{3,2,1,0:T(8,128)(2,1)}, u32[]{:S(2)}) copy-start(bf16[2,1,64,320]{3,2,1,0:T(8,128)(2,1)} %refs_5_.1) | copy-start | bytes 245764
  19.7 26.4 %copy-start.6 = (bf16[2,1,64,320]{3,2,1,0:T(8,128)(2,1)S(1)}, bf16[2,1,64,320]{3,2,1,0:T(8,128)(2,1)}, u32[]{:S(2)}) copy-start(bf16[2,1,64,320]{3,2,1,0:T(8,128)(2,1)} %get-tuple-element.20.refs_6_) | copy-start | bytes 245764
  19.7 6.5 %collective-permute-start.3 = (bf16[640,128]{1,0:T(8,128)(2,1)S(1)}, bf16[640,128]{1,0:T(8,128)(2,1)S(1)}, u32[]{:S(2)}, u32[]{:S(2)}) collective-permute-start(bf16[640,128]{1,0:T(8,128)(2,1)S(1)} %get-tuple-element.25.refs_0_), channel_id=1, source_target_pairs={{0,2},{1,3},{2,0},{3,1},{4,6},{5,7},{6,4},{7,5},{8,10},{9,11},{10,... | collective-permute-start | bytes 491528 | tf_op jit(solution)/shard_map/ppermute | solution.py:287
  21.2 6.6 %collective-permute-start.2 = (bf16[640,128]{1,0:T(8,128)(2,1)S(1)}, bf16[640,128]{1,0:T(8,128)(2,1)S(1)}, u32[]{:S(2)}, u32[]{:S(2)}) collective-permute-start(bf16[640,128]{1,0:T(8,128)(2,1)S(1)} %get-tuple-element.25.refs_0_), channel_id=1, source_target_pairs={{0,1},{1,0},{2,3},{3,2},{4,5},{5,4},{6,7},{7,6},{8,9},{9,8},{10,11... | collective-permute-start | bytes 491528 | tf_op jit(solution)/shard_map/ppermute | solution.py:287
  26.2 1.6 %collective-permute-start.4 = (bf16[640,128]{1,0:T(8,128)(2,1)S(1)}, bf16[640,128]{1,0:T(8,128)(2,1)S(1)}, u32[]{:S(2)}, u32[]{:S(2)}) collective-permute-start(bf16[640,128]{1,0:T(8,128)(2,1)S(1)} %collective-permute-done.3.refs_2_), channel_id=1, source_target_pairs={{0,1},{1,0},{2,3},{3,2},{4,5},{5,4},{6,7},{7,6},{8,9},{9,8},{10,11... | collective-permute-start | bytes 491528 | tf_op jit(solution)/shard_map/ppermute | solution.py:287
  26.3 6.0 %collective-permute-start.6 = (bf16[1,8,64,128]{3,2,1,0:T(8,128)(2,1)S(1)}, bf16[1,8,64,128]{3,2,1,0:T(8,128)(2,1)S(1)}, u32[]{:S(2)}, u32[]{:S(2)}) collective-permute-start(bf16[1,8,64,128]{3,2,1,0:T(8,128)(2,1)S(1)} %get-tuple-element.33), channel_id=1, source_target_pairs={{0,2},{1,3},{2,0},{3,1},{4,6},{5,7},{6,4},{7,5},{8,10},{9,11},{10,... | collective-permute-start | bytes 393224 | tf_op jit(solution)/shard_map/ppermute | solution.py:287
  33.5 10.1 %collective-permute-start.10 = (bf16[192,128]{1,0:T(8,128)(2,1)S(1)}, bf16[192,128]{1,0:T(8,128)(2,1)S(1)}, u32[]{:S(2)}, u32[]{:S(2)}) collective-permute-start(bf16[192,128]{1,0:T(8,128)(2,1)S(1)} %get-tuple-element.38), channel_id=1, source_target_pairs={{0,16},{4,20},{8,24},{12,28},{16,0},{20,4},{24,8},{28,12},{1,17},{... | collective-permute-start | bytes 147464 | tf_op jit(solution)/shard_map/ppermute | solution.py:287
  37.4 8.7 %collective-permute-start.11 = (bf16[192,128]{1,0:T(8,128)(2,1)S(1)}, bf16[192,128]{1,0:T(8,128)(2,1)S(1)}, u32[]{:S(2)}, u32[]{:S(2)}) collective-permute-start(bf16[192,128]{1,0:T(8,128)(2,1)S(1)} %get-tuple-element.39), channel_id=1, source_target_pairs={{0,20},{4,16},{8,28},{12,24},{16,4},{20,0},{24,12},{28,8},{1,21},{... | collective-permute-start | bytes 147464 | tf_op jit(solution)/shard_map/ppermute | solution.py:287
  38.3 9.9 %collective-permute-start.12 = (bf16[192,128]{1,0:T(8,128)(2,1)S(1)}, bf16[192,128]{1,0:T(8,128)(2,1)S(1)}, u32[]{:S(2)}, u32[]{:S(2)}) collective-permute-start(bf16[192,128]{1,0:T(8,128)(2,1)S(1)} %get-tuple-element.40), channel_id=1, source_target_pairs={{0,24},{4,28},{8,16},{12,20},{16,8},{20,12},{24,0},{28,4},{1,25},{... | collective-permute-start | bytes 147464 | tf_op jit(solution)/shard_map/ppermute | solution.py:287
  40.3 8.0 %collective-permute-start.13 = (bf16[192,128]{1,0:T(8,128)(2,1)S(1)}, bf16[192,128]{1,0:T(8,128)(2,1)S(1)}, u32[]{:S(2)}, u32[]{:S(2)}) collective-permute-start(bf16[192,128]{1,0:T(8,128)(2,1)S(1)} %get-tuple-element.41), channel_id=1, source_target_pairs={{0,28},{4,24},{8,20},{12,16},{16,12},{20,8},{24,4},{28,0},{1,29},{... | collective-permute-start | bytes 147464 | tf_op jit(solution)/shard_map/ppermute | solution.py:287
  42.2 6.0 %collective-permute-start.7 = (bf16[192,128]{1,0:T(8,128)(2,1)S(1)}, bf16[192,128]{1,0:T(8,128)(2,1)S(1)}, u32[]{:S(2)}, u32[]{:S(2)}) collective-permute-start(bf16[192,128]{1,0:T(8,128)(2,1)S(1)} %get-tuple-element.35), channel_id=1, source_target_pairs={{0,4},{4,0},{8,12},{12,8},{16,20},{20,16},{24,28},{28,24},{1,5},{5... | collective-permute-start | bytes 147464 | tf_op jit(solution)/shard_map/ppermute | solution.py:287
  43.6 4.7 %collective-permute-start.8 = (bf16[192,128]{1,0:T(8,128)(2,1)S(1)}, bf16[192,128]{1,0:T(8,128)(2,1)S(1)}, u32[]{:S(2)}, u32[]{:S(2)}) collective-permute-start(bf16[192,128]{1,0:T(8,128)(2,1)S(1)} %get-tuple-element.36), channel_id=1, source_target_pairs={{0,8},{4,12},{8,0},{12,4},{16,24},{20,28},{24,16},{28,20},{1,9},{5... | collective-permute-start | bytes 147464 | tf_op jit(solution)/shard_map/ppermute | solution.py:287
  46.1 5.0 %collective-permute-start.9 = (bf16[192,128]{1,0:T(8,128)(2,1)S(1)}, bf16[192,128]{1,0:T(8,128)(2,1)S(1)}, u32[]{:S(2)}, u32[]{:S(2)}) collective-permute-start(bf16[192,128]{1,0:T(8,128)(2,1)S(1)} %get-tuple-element.37), channel_id=1, source_target_pairs={{0,12},{4,8},{8,4},{12,0},{16,28},{20,24},{24,20},{28,16},{1,13},{... | collective-permute-start | bytes 147464 | tf_op jit(solution)/shard_map/ppermute | solution.py:287

commit v2 on v1

--- a/solution.py
+++ b/solution.py
@@ -18,18 +18,21 @@
     return (value + unit - 1) // unit * unit
 
 
-def on_device(body, args, outs, scratch=(), flops=0):
+def on_device(body, args, outs, scratch=(), far=0):
     whole = pl.BlockSpec(memory_space=pltpu.VMEM)
     moved = sum(math.prod(a.shape) * a.dtype.itemsize for a in (*args, *outs))
+    scratch = [*scratch, *(pltpu.VMEM(a.shape, a.dtype) for a in args[:far])]
+    if far:
+        scratch.append(pltpu.SemaphoreType.DMA((far,)))
     return pl.pallas_call(
         body,
         out_shape=outs,
-        in_specs=[whole] * len(args),
+        in_specs=[pl.BlockSpec(memory_space=pltpu.HBM)] * far + [whole] * (len(args) - far),
         out_specs=[whole] * len(outs),
-        scratch_shapes=list(scratch),
+        scratch_shapes=scratch,
         compiler_params=pltpu.CompilerParams(vmem_limit_bytes=40 * 1024 * 1024),
-        cost_estimate=pl.CostEstimate(flops=flops, bytes_accessed=moved, transcendentals=0),
-    )(*args)
+        cost_estimate=pl.CostEstimate(flops=0, bytes_accessed=moved, transcendentals=0),
+    )(*[pltpu.with_memory_space_constraint(a, pltpu.HBM) for a in args[:far]], *args[far:])
 
 
 def shape(dims, dtype):
@@ -62,81 +65,106 @@
     return (low + high) * HAAR, (low - high) * HAAR
 
 
-def open_body(y_ref, cot_ref, out_ref):
+def fetch(far, near, sems):
+    copies = [pltpu.make_async_copy(f, n, sems.at[i]) for i, (f, n) in enumerate(zip(far, near))]
+    for copy in copies:
+        copy.start()
+    for copy in copies:
+        copy.wait()
+
+
+def open_body(y_far, cot_far, out_ref, y_ref, cot_ref, sems):
+    fetch((y_far, cot_far), (y_ref, cot_ref), sems)
     sq = squeezed(y_ref)
     cols = sq.shape[0]
     out_ref[:cols] = (sq * sigmoid(sq)).astype(BF16)
     out_ref[cols:] = squeezed(cot_ref).astype(BF16)
 
 
-def time_body(own, before, after, y1, y2, c1, weight, x2_out, g1_out, packed_out):
-    cols, ch = y2.shape[2:]
+def centre_body(y1_far, y2_far, c1_far, weight_far, own, *refs):
+    (forth, back, slope, base, weight_out), (y1, y2, c1, weight, sems) = refs[:5], refs[5:]
+    fetch((y1_far, y2_far, c1_far, weight_far), (y1, y2, c1, weight), sems)
+    cols = own.shape[0] // 2
+    groups, width = weight.shape[1:3]
+    for q in range(groups):
+        lanes = slice(q * width, (q + 1) * width)
+        forth[:, lanes] = dot(own[:cols, lanes], weight[1, q], 1, 0)
+        back[:, lanes] = dot(own[cols:, lanes], weight[1, q], 1, 1)
+    slope[...] = silu_slope(squeezed(y1))
+    for f in range(2):
+        base[0, f] = y2[f, 0]
+        base[1, f] = c1[f, 0]
+    weight_out[...] = weight[...]
+
+
+def time_body(before, after, forth0, back0, slope, base, weight, x2_out, g1_out, act_out, cot_out):
+    cols = forth0.shape[0]
     groups, width = weight.shape[1:3]
     forth, back = [], []
     for q in range(groups):
         lanes = slice(q * width, (q + 1) * width)
         forth.append(
             dot(before[:cols, lanes], weight[0, q], 1, 0)
-            + dot(own[:cols, lanes], weight[1, q], 1, 0)
+            + forth0[:, lanes]
             + dot(after[:cols, lanes], weight[2, q], 1, 0)
         )
         back.append(
             dot(after[cols:, lanes], weight[0, q], 1, 1)
-            + dot(own[cols:, lanes], weight[1, q], 1, 1)
+            + back0[:, lanes]
             + dot(before[cols:, lanes], weight[2, q], 1, 1)
         )
     branch = unsqueezed(jnp.concatenate(forth, axis=-1))
-    back = unsqueezed(jnp.concatenate(back, axis=-1) * silu_slope(squeezed(y1)))
-    frames = []
+    back = unsqueezed(jnp.concatenate(back, axis=-1) * slope[...])
+    acts, cots = [], []
     for f in range(2):
-        x2 = (y2[f, 0].astype(F32) - branch[f].astype(BF16).astype(F32)).astype(BF16)
-        g1 = (c1[f, 0].astype(F32) + back[f].astype(BF16).astype(F32)).astype(BF16)
+        x2 = (base[0, f].astype(F32) - branch[f].astype(BF16).astype(F32)).astype(BF16)
+        g1 = (base[1, f].astype(F32) + back[f].astype(BF16).astype(F32)).astype(BF16)
         x2_out[f, 0] = x2
         g1_out[f, 0] = g1
         v = x2.astype(F32)
-        frames.append(jnp.concatenate([v * sigmoid(v), g1.astype(F32)], axis=-1))
-    packed_out[...] = jnp.concatenate(frames, axis=0).T.astype(BF16)
-
-
-def time_terms(own, before, after, total):
-    cols = own.shape[0] // 2
+        acts.append(v * sigmoid(v))
+        cots.append(g1.astype(F32))
+    act_out[...] = jnp.concatenate(acts, axis=0).T.astype(BF16)
+    cot_out[...] = jnp.concatenate(cots, axis=0).T.astype(BF16)
+
+
+def time_terms(owns, afters, total):
+    cols = owns[0].shape[0] // 2
     width = total.shape[1]
-    groups = own.shape[1] // width
-    for k, ref in enumerate((before, own, after)):
+    groups = owns[0].shape[1] // width
+    acts, cots = [], []
+    for refs in (owns, afters):
+        act = jnp.concatenate([ref[:cols] for ref in refs], axis=0)
+        acts.append(act.astype(F32).T.astype(BF16))
+        cots.append(jnp.concatenate([ref[cols:] for ref in refs], axis=0))
+    for k, (act, cot) in enumerate(((acts[0], cots[1]), (acts[0], cots[0]), (acts[1], cots[0]))):
         for q in range(groups):
-            lanes = slice(q * width, (q + 1) * width)
-            term = dot(ref[:cols, lanes].astype(F32).T.astype(BF16), own[cols:, lanes], 1, 0)
+            part = slice(q * width, (q + 1) * width)
+            term = dot(act[part], cot[:, part], 1, 0)
             total[pl.ds((k * groups + q) * width, width), :] = term
 
 
-def time_sum_body(offsets, rows, own, before, after, keep, send, total):
-    time_terms(own, before, after, total)
+def time_sum_body(rows, *refs):
+    (keep, send, total), refs = refs[-3:], refs[:-3]
+    time_terms(refs[0::2], refs[1::2], total)
     me, peers, steps = lax.axis_index("row"), lax.axis_size("row"), lax.axis_size("tm")
-    held = keep.shape[2]
-    for u, offset in enumerate(offsets):
-        for t in range(steps):
-            mine = (t * peers + (me ^ offset)) * rows
-            other = (t * peers + (me ^ offset ^ 1)) * rows
-            keep[u, t] = total[pl.ds(mine, held), :]
-            send[u, t] = total[pl.ds(other, held), :].astype(BF16)
-
-
-def time_sum_whole_body(own, before, after, total):
-    time_terms(own, before, after, total)
-
-
-def fold_body(kept, came, keep, send):
-    half = keep.shape[0]
-    keep[...] = kept[:half] + came[:half].astype(F32)
-    send[...] = (kept[half:] + came[half:].astype(F32)).astype(BF16)
+    held = keep.shape[1]
+    for t in range(steps):
+        keep[t] = total[pl.ds((t * peers + me) * rows, held), :]
+        send[t] = total[pl.ds((t * peers + (me ^ 1)) * rows, held), :].astype(BF16)
+
+
+def time_sum_whole_body(own, after, total):
+    time_terms((own,), (after,), total)
 
 
 def space_terms(slots, rows_ref, cols, store):
-    peers = len(slots)
+    peers = len(slots) // 2
     me = lax.axis_index("row")
-    for k, ref in enumerate(slots):
-        rows_ref[me ^ k] = ref[...]
     ch = rows_ref.shape[1] // 2
+    for k in range(peers):
+        rows_ref[me ^ k, :ch] = slots[2 * k][...]
+        rows_ref[me ^ k, ch:] = slots[2 * k + 1][...]
     column = lax.broadcasted_iota(jnp.int32, (ch, LANES), 1) % cols
     act, shifts = [], ([], [], [])
     for r in range(peers):
@@ -172,7 +200,7 @@
 
 def space_sum_body(groups, rows, *refs):
     peers, steps = lax.axis_size("row"), lax.axis_size("tm")
-    slots, (kept, came), refs = refs[:peers], refs[peers : peers + 2], refs[peers + 2 :]
+    slots, (kept, came), refs = refs[: 2 * peers], refs[2 * peers : 2 * peers + 2], refs[2 * peers + 2 :]
     mine, sends, (rows_ref, main, rest) = refs[0], refs[1:steps], refs[steps:]
     ch = rows_ref.shape[1] // 2
     width = ch // groups
@@ -190,7 +218,7 @@
     held = round_up(-(-rows // period), 8)
     lane = lax.broadcasted_iota(jnp.int32, (held, LANES), 1)
     here, me = lax.axis_index("tm"), lax.axis_index("row")
-    early = kept.shape[2]
+    early = kept.shape[1]
     for k in range(steps):
         t = here ^ k
         start = (t * peers + me) * rows
@@ -203,7 +231,7 @@
                 rolled[j, tile, amount] = pltpu.roll(value, amount, 1) if amount else value
             return rolled[j, tile, amount]
 
-        parts = [kept[0, t] + came[0, t].astype(F32)]
+        parts = [kept[t] + came[t].astype(F32)]
         for row in layout:
             value = None
             for first, j, tile, amount in row:
@@ -222,7 +250,7 @@
 
 def space_sum_whole_body(groups, *refs):
     peers = lax.axis_size("row")
-    slots, (total, rows_ref) = refs[:peers], refs[peers:]
+    slots, (total, rows_ref) = refs[: 2 * peers], refs[2 * peers :]
     ch = rows_ref.shape[1] // 2
     width = ch // groups
 
@@ -251,14 +279,18 @@
 
 def space_body(*refs):
     peers = lax.axis_size("row")
-    slots, (y1, c2, x2, weight, x1_out, g2_out, rows_ref) = refs[:peers], refs[peers:]
+    slots, refs = refs[: 2 * peers], refs[2 * peers :]
+    y1, c2, x2, g1, weight, x1_out, x2_out, g1_out, g2_out, rows_ref = refs
+    x2_out[...] = x2[...]
+    g1_out[...] = g1[...]
     me = lax.axis_index("row")
     cols, ch = y1.shape[2:]
     groups, width = weight.shape[2:4]
     rows_ref[0] = jnp.zeros(rows_ref.shape[1:], BF16)
     rows_ref[peers + 1] = jnp.zeros(rows_ref.shape[1:], BF16)
-    for k, ref in enumerate(slots):
-        rows_ref[(me ^ k) + 1] = ref[...]
+    for k in range(peers):
+        rows_ref[(me ^ k) + 1, :ch] = slots[2 * k][...]
+        rows_ref[(me ^ k) + 1, ch:] = slots[2 * k + 1][...]
     column = lax.broadcasted_iota(jnp.int32, (LANES, width), 0) % cols
     forth, back = [None] * groups, [None] * groups
     for a in range(3):
@@ -287,11 +319,12 @@
     return lax.ppermute(x, axis, [(i, i ^ bit) for i in range(lax.axis_size(axis))])
 
 
-def row_offsets(bits):
-    if not bits:
-        return [0]
-    rest = row_offsets(bits[1:])
-    return rest + [o ^ bits[0] for o in rest]
+def gather(x, axis, bits):
+    slots = {0: x}
+    for bit in reversed(bits):
+        for k in list(slots):
+            slots[k ^ bit] = swap(slots[k], axis, bit)
+    return [slots[k] for k in sorted(slots)]
 
 
 def per_device(y1, y2, c1, c2, weight_space, temporal_weight):
@@ -306,41 +339,43 @@
     time_rows = 3 * time_groups * time_width
     space_rows = taps * ch
 
-    packed = on_device(open_body, (y1, c2), [shape((2 * cols, 2 * ch), BF16)])[0]
+    packed = on_device(open_body, (y1, c2), [shape((2 * cols, 2 * ch), BF16)], far=2)[0]
     up = [(i, i + 1) for i in range(steps - 1)]
-    before = lax.ppermute(packed, "tm", up)
-    after = lax.ppermute(packed, "tm", [(j, i) for i, j in up])
-    x2, g1, held = on_device(
-        time_body,
-        (packed, before, after, y1, y2, c1, temporal_weight),
-        [shape(y1.shape, BF16), shape(y1.shape, BF16), shape((2 * ch, 2 * cols), BF16)],
+    after = lax.ppermute(packed, "tm", [(i + 1, i) for i in range(steps - 1)])
+    before = lax.ppermute(packed, "tm", [(i, i + 1) for i in range(steps - 1)])
+    wide = shape((cols, 2 * ch), F32)
+    centre = on_device(
+        centre_body,
+        (y1, y2, c1, temporal_weight, packed),
+        [wide] * 3 + [shape((2, 2, cols, ch), BF16), shape(temporal_weight.shape, BF16)],
+        far=4,
     )
 
-    slots = {0: held}
+    even = time_rows % devices == 0 and space_rows % devices == 0
     bits = [1 << i for i in range(peers.bit_length() - 1)]
-    for bit in reversed(bits):
-        for k in list(slots):
-            slots[k ^ bit] = swap(slots[k], "row", bit)
-    gathered = [slots[k] for k in range(peers)]
-
-    even = time_rows % devices == 0 and space_rows % devices == 0
     if even:
         rows = time_rows // devices
         tall = round_up(rows, 16)
-        offsets = row_offsets(bits[1:])
-        block = (len(offsets), steps, tall, time_width)
+        part = (steps, tall, time_width)
+        held, centre = lax.optimization_barrier((after, centre))
+        owns, afters = gather(packed, "row", bits[1:]), gather(held, "row", bits[1:])
         kept, sent = on_device(
-            functools.partial(time_sum_body, offsets, rows),
-            (packed, before, after),
-            [shape(block, F32), shape(block, BF16)],
+            functools.partial(time_sum_body, rows),
+            [v for pair in zip(owns, afters) for v in pair],
+            [shape(part, F32), shape(part, BF16)],
             [pltpu.VMEM((round_up(time_rows + tall, 8), time_width), F32)],
         )
         came = swap(sent, "row", 1)
-        for bit in bits[1:]:
-            block = (block[0] // 2, *block[1:])
-            kept, sent = on_device(fold_body, (kept, came), [shape(block, F32), shape(block, BF16)])
-            came = swap(sent, "row", bit)
-
+
+    x2, g1, act, cot = on_device(
+        time_body,
+        (before, after, *centre),
+        [shape(y1.shape, BF16)] * 2 + [shape((ch, 2 * cols), BF16)] * 2,
+    )
+    pairs = zip(gather(act, "row", bits), gather(cot, "row", bits))
+    gathered = [v for pair in pairs for v in pair]
+
+    if even:
         rows = space_rows // devices
         period, layout = segments(width)
         deep = round_up(tall + round_up(-(-rows // period), 8) * len(layout), 16)
@@ -363,7 +398,7 @@
         time_share = time_share.reshape(-1)
     else:
         total = on_device(
-            time_sum_whole_body, (packed, before, after), [shape((time_rows, time_width), F32)]
+            time_sum_whole_body, (packed, after), [shape((time_rows, time_width), F32)]
         )[0]
         time_share = factor * lax.psum_scatter(
             total.reshape(-1), ("tm", "row"), scatter_dimension=0, tiled=True
@@ -380,10 +415,10 @@
             total.reshape(-1), "tm", scatter_dimension=0, tiled=True
         )
 
-    x1, g2 = on_device(
+    x1, x2, g1, g2 = on_device(
         space_body,
-        (*gathered, y1, c2, x2, weight_space),
-        [shape(y1.shape, BF16), shape(y1.shape, BF16)],
+        (*gathered, y1, c2, x2, g1, weight_space),
+        [shape(y1.shape, BF16)] * 4,
         [pltpu.VMEM((peers + 2, 2 * ch, 2 * cols), BF16)],
     )
     return x1, x2, g1, g2, space_share, time_share

time: 52 us -> 42.2 us (0.81)
  waiting for transfers between devices: 20.9 us -> 9.6 us
  local copies, waits for them, and re-layouts: 4.71 us -> 0.02 us
  starting transfers between devices: 19.5 us -> 23.9 us
  Pallas kernels: 5.88 us -> 7.65 us
    ppermute x12 -> x16, waiting for transfers between devices: 14.6 us -> 7.64 us  [swap(): lax.ppermute(x, axis, [(i, i ^ bit) for i in range(lax.axis_size(axis))])]
    unnamed x18 -> x6, local copies, waits for them, and re-layouts: 4.71 us -> 0.02 us
    ppermute x2, waiting for transfers between devices: 6.25 us -> 1.95 us  [the longest x1 1.95 us: per_device(): before = lax.ppermute(packed, 'tm', [(i, i + 1) for i in range(steps - 1)])]
    ppermute x12 -> x16, starting transfers between devices: 13.4 us -> 17.1 us  [swap(): lax.ppermute(x, axis, [(i, i ^ bit) for i in range(lax.axis_size(axis))])]
    pallas_call x7, Pallas kernels: 5.88 us -> 7.65 us  [on_device(): pl.pallas_call(body, out_shape=outs, in_specs=[pl.BlockSpec(memory_space=...]
    ppermute x2, starting transfers between devices: 6.17 us -> 6.8 us  [the longest x1 5.51 us: per_device(): before = lax.ppermute(packed, 'tm', [(i, i + 1) for i in range(steps - 1)])]
  transfers between devices with their start and end apart: 14 -> 18, of which waited for: 6 -> 9; matrix products, arithmetic and copies ran while one was open for 0% -> 0% of each run, Pallas kernels for 7% -> 11%
where the time goes in v2:
time: 42.2 us; the launch traced here: 41.9 us
  starting transfers between devices  23.9 us (57%)
  waiting for transfers between devices  9.6 us (23%)
  Pallas kernels  7.65 us (18%)
  between operations  0.74 us (2%)
    ppermute x16, starting transfers between devices, swap(): lax.ppermute(x, axis, [(i, i ^ bit) for i in range(lax.axis_size(axis))])  17.1 us
    pallas_call x7, Pallas kernels, on_device(): pl.pallas_call(body, out_shape=outs, in_specs=[pl.BlockSpec(memory_space=...  7.65 us
    ppermute x16, waiting for transfers between devices, swap(): lax.ppermute(x, axis, [(i, i ^ bit) for i in range(lax.axis_size(axis))])  7.64 us
    ppermute x1, starting transfers between devices, per_device(): before = lax.ppermute(packed, 'tm', [(i, i + 1) for i in range(steps - 1)])  5.51 us
    ppermute x1, waiting for transfers between devices, per_device(): before = lax.ppermute(packed, 'tm', [(i, i + 1) for i in range(steps - 1)])  1.95 us
    ppermute x1, starting transfers between devices, per_device(): after = lax.ppermute(packed, 'tm', [(i + 1, i) for i in range(steps - 1)])  1.29 us
  transfers between devices with their start and end apart: 18, of which 9 were waited for; matrix products, arithmetic and copies ran while one was open for 0% of the time, Pallas kernels for 11%

profile of v2, /device:TPU:0, one launch (start us, length us, event | category | flops | bytes accessed | tf_op | source)
XLA Modules:
  0.0 41.9 jit_solution(11920849095832075485)
XLA Ops:
  0.6 1.1 %shard_map.109.own.refs_0_ = bf16[128,640]{1,0:T(8,128)(2,1)S(1)} custom-call(bf16[2,1,64,320]{3,2,1,0:T(8,128)(2,1)} %refs_8_.1, bf16[2,1,64,320]{3,2,1,0:T(8,128)(2,1)} %refs_9_.1), custom_call_target="tpu_custom_call" | custom-call | bytes 327680 | tf_op jit(solution)/shard_map/pallas_call | solution.py:27
  1.7 1.3 %collective-permute-start.1 = (bf16[128,640]{1,0:T(8,128)(2,1)S(1)}, bf16[128,640]{1,0:T(8,128)(2,1)S(1)}, u32[]{:S(2)}, u32[]{:S(2)}) collective-permute-start(bf16[128,640]{1,0:T(8,128)(2,1)S(1)} %shard_map.109.own.refs_0_), channel_id=1, source_target_pairs={{4,0},{8,4},{12,8},{16,12},{20,16},{24,20},{28,24},{5,1},{9,5},{13... | collective-permute-start | bytes 491528 | tf_op jit(solution)/shard_map/ppermute | solution.py:344
  3.0 5.5 %collective-permute-start = (bf16[128,640]{1,0:T(8,128)(2,1)S(1)}, bf16[128,640]{1,0:T(8,128)(2,1)S(1)}, u32[]{:S(2)}, u32[]{:S(2)}) collective-permute-start(bf16[128,640]{1,0:T(8,128)(2,1)S(1)} %shard_map.109.own.refs_0_), channel_id=1, source_target_pairs={{0,4},{4,8},{8,12},{12,16},{16,20},{20,24},{24,28},{1,5},{5,9},{9,... | collective-permute-start | bytes 491528 | tf_op jit(solution)/shard_map/ppermute | solution.py:345
  8.5 2.1 %collective-permute-start.8 = (bf16[128,640]{1,0:T(8,128)(2,1)S(1)}, bf16[128,640]{1,0:T(8,128)(2,1)S(1)}, u32[]{:S(2)}, u32[]{:S(2)}) collective-permute-start(bf16[128,640]{1,0:T(8,128)(2,1)S(1)} %shard_map.109.own.refs_0_), channel_id=1, source_target_pairs={{0,2},{1,3},{2,0},{3,1},{4,6},{5,7},{6,4},{7,5},{8,10},{9,11},{10,... | collective-permute-start | bytes 491528 | tf_op jit(solution)/shard_map/ppermute | solution.py:319
  10.6 1.5 %shard_map.110 = (f32[64,640]{1,0:T(8,128)S(1)}, f32[64,640]{1,0:T(8,128)S(1)}, f32[64,640]{1,0:T(8,128)S(1)}, bf16[2,2,64,320]{3,2,1,0:T(8,128)(2,1)S(1)}, bf16[3,5,128,128]{3,2,1,0:T(8,128)(2,1)S(1)}) custom-call(bf16[2,1,64,320]{3,2,1,0:T(8,128)(2,1)} %refs_8_.1, bf16[2,1,64,320]{3,2,1,0:T(8,128)(2,1)} %y2_far.1, bf16[2,1,64,320]{3,2,1,0:T(8,128)(2,1)} %c1_far.1, ...), custom_call_target="tpu_custom_call" | custom-call | bytes 2048000 | tf_op jit(solution)/shard_map/pallas_call | solution.py:27
  12.5 1.9 %collective-permute-done.before = bf16[128,640]{1,0:T(8,128)(2,1)S(1)} collective-permute-done((bf16[128,640]{1,0:T(8,128)(2,1)S(1)}, bf16[128,640]{1,0:T(8,128)(2,1)S(1)}, u32[]{:S(2)}, u32[]{:S(2)}) %collective-permute-start) | collective-permute-done | bytes 163872 | tf_op jit(solution)/shard_map/ppermute | solution.py:345
  14.5 0.6 %shard_map.111 = (bf16[2,1,64,320]{3,2,1,0:T(8,128)(2,1)S(1)}, bf16[2,1,64,320]{3,2,1,0:T(8,128)(2,1)S(1)}, bf16[320,128]{1,0:T(8,128)(2,1)S(1)}, bf16[320,128]{1,0:T(8,128)(2,1)S(1)}) custom-call(bf16[128,640]{1,0:T(8,128)(2,1)S(1)} %collective-permute-done.before, bf16[128,640]{1,0:T(8,128)(2,1)S(1)} %collective-permute-done.1.after.refs_1_, ...), custom_call_target="tpu_custom_call" | custom-call | bytes 1802240 | tf_op jit(solution)/shard_map/pallas_call | solution.py:27
  15.1 1.6 %collective-permute-start.4 = (bf16[320,128]{1,0:T(8,128)(2,1)S(1)}, bf16[320,128]{1,0:T(8,128)(2,1)S(1)}, u32[]{:S(2)}, u32[]{:S(2)}) collective-permute-start(bf16[320,128]{1,0:T(8,128)(2,1)S(1)} %get-tuple-element.47.refs_0_), channel_id=1, source_target_pairs={{0,2},{1,3},{2,0},{3,1},{4,6},{5,7},{6,4},{7,5},{8,10},{9,11},{10,... | collective-permute-start | bytes 245768 | tf_op jit(solution)/shard_map/ppermute | solution.py:319
  16.6 0.5 %collective-permute-start.5 = (bf16[320,128]{1,0:T(8,128)(2,1)S(1)}, bf16[320,128]{1,0:T(8,128)(2,1)S(1)}, u32[]{:S(2)}, u32[]{:S(2)}) collective-permute-start(bf16[320,128]{1,0:T(8,128)(2,1)S(1)} %get-tuple-element.48.refs_1_), channel_id=1, source_target_pairs={{0,2},{1,3},{2,0},{3,1},{4,6},{5,7},{6,4},{7,5},{8,10},{9,11},{10,... | collective-permute-start | bytes 245768 | tf_op jit(solution)/shard_map/ppermute | solution.py:319
  17.2 0.6 %collective-permute-done.9.refs_3_ = bf16[128,640]{1,0:T(8,128)(2,1)S(1)} collective-permute-done((bf16[128,640]{1,0:T(8,128)(2,1)S(1)}, bf16[128,640]{1,0:T(8,128)(2,1)S(1)}, u32[]{:S(2)}, u32[]{:S(2)}) %collective-permute-start.9) | collective-permute-done | bytes 163872 | tf_op jit(solution)/shard_map/ppermute | solution.py:319
  18.8 1.3 %collective-permute-done.4.refs_4_ = bf16[320,128]{1,0:T(8,128)(2,1)S(1)} collective-permute-done((bf16[320,128]{1,0:T(8,128)(2,1)S(1)}, bf16[320,128]{1,0:T(8,128)(2,1)S(1)}, u32[]{:S(2)}, u32[]{:S(2)}) %collective-permute-start.4) | collective-permute-done | bytes 81952 | tf_op jit(solution)/shard_map/ppermute | solution.py:319
  20.2 1.1 %collective-permute-done.5.refs_5_ = bf16[320,128]{1,0:T(8,128)(2,1)S(1)} collective-permute-done((bf16[320,128]{1,0:T(8,128)(2,1)S(1)}, bf16[320,128]{1,0:T(8,128)(2,1)S(1)}, u32[]{:S(2)}, u32[]{:S(2)}) %collective-permute-start.5) | collective-permute-done | bytes 81952 | tf_op jit(solution)/shard_map/ppermute | solution.py:319
  21.5 1.1 %collective-permute-done.7.refs_7_ = bf16[320,128]{1,0:T(8,128)(2,1)S(1)} collective-permute-done((bf16[320,128]{1,0:T(8,128)(2,1)S(1)}, bf16[320,128]{1,0:T(8,128)(2,1)S(1)}, u32[]{:S(2)}, u32[]{:S(2)}) %collective-permute-start.7) | collective-permute-done | bytes 81952 | tf_op jit(solution)/shard_map/ppermute | solution.py:319
  22.6 1.2 %shard_map.114 = (f32[192,128]{1,0:T(8,128)S(1)}, bf16[192,128]{1,0:T(8,128)(2,1)S(1)}, bf16[192,128]{1,0:T(8,128)(2,1)S(1)}, bf16[192,128]{1,0:T(8,128)(2,1)S(1...) custom-call(bf16[320,128]{1,0:T(8,128)(2,1)S(1)} %get-tuple-element., ...), custom_call_target="tpu_custom_call" | custom-call | bytes 1490944 | tf_op jit(solution)/shard_map/pallas_call | solution.py:27
  23.8 2.7 %collective-permute-start.11 = (bf16[192,128]{1,0:T(8,128)(2,1)S(1)}, bf16[192,128]{1,0:T(8,128)(2,1)S(1)}, u32[]{:S(2)}, u32[]{:S(2)}) collective-permute-start(bf16[192,128]{1,0:T(8,128)(2,1)S(1)} %get-tuple-element.59), channel_id=1, source_target_pairs={{0,4},{4,0},{8,12},{12,8},{16,20},{20,16},{24,28},{28,24},{1,5},{5... | collective-permute-start | bytes 147464 | tf_op jit(solution)/shard_map/ppermute | solution.py:319
  26.5 1.6 %collective-permute-start.12 = (bf16[192,128]{1,0:T(8,128)(2,1)S(1)}, bf16[192,128]{1,0:T(8,128)(2,1)S(1)}, u32[]{:S(2)}, u32[]{:S(2)}) collective-permute-start(bf16[192,128]{1,0:T(8,128)(2,1)S(1)} %get-tuple-element.60), channel_id=1, source_target_pairs={{0,8},{4,12},{8,0},{12,4},{16,24},{20,28},{24,16},{28,20},{1,9},{5... | collective-permute-start | bytes 147464 | tf_op jit(solution)/shard_map/ppermute | solution.py:319
  28.1 2.6 %collective-permute-start.14 = (bf16[192,128]{1,0:T(8,128)(2,1)S(1)}, bf16[192,128]{1,0:T(8,128)(2,1)S(1)}, u32[]{:S(2)}, u32[]{:S(2)}) collective-permute-start(bf16[192,128]{1,0:T(8,128)(2,1)S(1)} %get-tuple-element.62), channel_id=1, source_target_pairs={{0,16},{4,20},{8,24},{12,28},{16,0},{20,4},{24,8},{28,12},{1,17},{... | collective-permute-start | bytes 147464 | tf_op jit(solution)/shard_map/ppermute | solution.py:319
  30.6 1.7 %collective-permute-start.15 = (bf16[192,128]{1,0:T(8,128)(2,1)S(1)}, bf16[192,128]{1,0:T(8,128)(2,1)S(1)}, u32[]{:S(2)}, u32[]{:S(2)}) collective-permute-start(bf16[192,128]{1,0:T(8,128)(2,1)S(1)} %get-tuple-element.63), channel_id=1, source_target_pairs={{0,20},{4,16},{8,28},{12,24},{16,4},{20,0},{24,12},{28,8},{1,21},{... | collective-permute-start | bytes 147464 | tf_op jit(solution)/shard_map/ppermute | solution.py:319
  32.3 2.0 %collective-permute-start.16 = (bf16[192,128]{1,0:T(8,128)(2,1)S(1)}, bf16[192,128]{1,0:T(8,128)(2,1)S(1)}, u32[]{:S(2)}, u32[]{:S(2)}) collective-permute-start(bf16[192,128]{1,0:T(8,128)(2,1)S(1)} %get-tuple-element.64), channel_id=1, source_target_pairs={{0,24},{4,28},{8,16},{12,20},{16,8},{20,12},{24,0},{28,4},{1,25},{... | collective-permute-start | bytes 147464 | tf_op jit(solution)/shard_map/ppermute | solution.py:319
  34.4 1.5 %collective-permute-start.17 = (bf16[192,128]{1,0:T(8,128)(2,1)S(1)}, bf16[192,128]{1,0:T(8,128)(2,1)S(1)}, u32[]{:S(2)}, u32[]{:S(2)}) collective-permute-start(bf16[192,128]{1,0:T(8,128)(2,1)S(1)} %get-tuple-element.65), channel_id=1, source_target_pairs={{0,28},{4,24},{8,20},{12,16},{16,12},{20,8},{24,4},{28,0},{1,29},{... | collective-permute-start | bytes 147464 | tf_op jit(solution)/shard_map/ppermute | solution.py:319
  35.9 2.1 %shard_map.112 = (bf16[2,1,64,320]{3,2,1,0:T(8,128)(2,1)}, bf16[2,1,64,320]{3,2,1,0:T(8,128)(2,1)}, bf16[2,1,64,320]{3,2,1,0:T(8,128)(2,1)}, bf16[2,1,64,320]{3,2,1,0:T(8,128)(2,1)}) custom-call(bf16[320,128]{1,0:T(8,128)(2,1)S(1)} %get-tuple-element.47.refs_0_, bf16[320,128]{1,0:T(8,128)(2,1)S(1)} %get-tuple-element.48.refs_1_, ...), custom_call_target="tpu_custom_call" | custom-call | bytes 2232320 | tf_op jit(solution)/shard_map/pallas_call | solution.py:27
  38.0 0.5 %collective-permute-done.15.refs_5_ = bf16[192,128]{1,0:T(8,128)(2,1)S(1)} collective-permute-done((bf16[192,128]{1,0:T(8,128)(2,1)S(1)}, bf16[192,128]{1,0:T(8,128)(2,1)S(1)}, u32[]{:S(2)}, u32[]{:S(2)}) %collective-permute-start.15) | collective-permute-done | bytes 49184 | tf_op jit(solution)/shard_map/ppermute | solution.py:319
  38.6 2.6 %collective-permute-done.17.refs_7_ = bf16[192,128]{1,0:T(8,128)(2,1)S(1)} collective-permute-done((bf16[192,128]{1,0:T(8,128)(2,1)S(1)}, bf16[192,128]{1,0:T(8,128)(2,1)S(1)}, u32[]{:S(2)}, u32[]{:S(2)}) %collective-permute-start.17) | collective-permute-done | bytes 49184 | tf_op jit(solution)/shard_map/ppermute | solution.py:319
  41.3 0.7 %shard_map.115 = (f32[115,128]{1,0:T(8,128)}, f32[60,128]{1,0:T(8,128)}) custom-call(f32[192,128]{1,0:T(8,128)S(1)} %get-tuple-element.58.refs_0_, bf16[192,128]{1,0:T(8,128)(2,1)S(1)} %collective-permute-done.11.refs_1_, bf16[192,128]{1,0:T(8,128)(2,1)S(1)} %collective-permute-done.12.refs_2_, bf16[192,128]{1,0:T(8,128)(2,1)S(1)} %collective-permute-done.13.refs_3_, ...), custom_call_target="tpu_custom_call" | custom-call | bytes 531968 | tf_op jit(solution)/shard_map/pallas_call | solution.py:27
  (25 shorter events, 1.7 us)
Async XLA Ops:
  1.7 10.4 %collective-permute-start.1 = (bf16[128,640]{1,0:T(8,128)(2,1)S(1)}, bf16[128,640]{1,0:T(8,128)(2,1)S(1)}, u32[]{:S(2)}, u32[]{:S(2)}) collective-permute-start(bf16[128,640]{1,0:T(8,128)(2,1)S(1)} %shard_map.109.own.refs_0_), channel_id=1, source_target_pairs={{4,0},{8,4},{12,8},{16,12},{20,16},{24,20},{28,24},{5,1},{9,5},{13... | collective-permute-start | bytes 491528 | tf_op jit(solution)/shard_map/ppermute | solution.py:344
  3.0 11.4 %collective-permute-start = (bf16[128,640]{1,0:T(8,128)(2,1)S(1)}, bf16[128,640]{1,0:T(8,128)(2,1)S(1)}, u32[]{:S(2)}, u32[]{:S(2)}) collective-permute-start(bf16[128,640]{1,0:T(8,128)(2,1)S(1)} %shard_map.109.own.refs_0_), channel_id=1, source_target_pairs={{0,4},{4,8},{8,12},{12,16},{16,20},{20,24},{24,28},{1,5},{5,9},{9,... | collective-permute-start | bytes 491528 | tf_op jit(solution)/shard_map/ppermute | solution.py:345
  8.5 8.6 %collective-permute-start.8 = (bf16[128,640]{1,0:T(8,128)(2,1)S(1)}, bf16[128,640]{1,0:T(8,128)(2,1)S(1)}, u32[]{:S(2)}, u32[]{:S(2)}) collective-permute-start(bf16[128,640]{1,0:T(8,128)(2,1)S(1)} %shard_map.109.own.refs_0_), channel_id=1, source_target_pairs={{0,2},{1,3},{2,0},{3,1},{4,6},{5,7},{6,4},{7,5},{8,10},{9,11},{10,... | collective-permute-start | bytes 491528 | tf_op jit(solution)/shard_map/ppermute | solution.py:319
  12.1 23.7 %copy-start = (bf16[3,3,2,160,160]{4,3,2,1,0:T(8,128)(2,1)S(1)}, bf16[3,3,2,160,160]{4,3,2,1,0:T(8,128)(2,1)}, u32[]{:S(2)}) copy-start(bf16[3,3,2,160,160]{4,3,2,1,0:T(8,128)(2,1)} %refs_12_.1) | copy-start | bytes 2764804
  12.1 23.7 %copy-start.1 = (bf16[2,1,64,320]{3,2,1,0:T(8,128)(2,1)S(1)}, bf16[2,1,64,320]{3,2,1,0:T(8,128)(2,1)}, u32[]{:S(2)}) copy-start(bf16[2,1,64,320]{3,2,1,0:T(8,128)(2,1)} %refs_8_.1) | copy-start | bytes 245764
  12.1 23.7 %copy-start.2 = (bf16[2,1,64,320]{3,2,1,0:T(8,128)(2,1)S(1)}, bf16[2,1,64,320]{3,2,1,0:T(8,128)(2,1)}, u32[]{:S(2)}) copy-start(bf16[2,1,64,320]{3,2,1,0:T(8,128)(2,1)} %refs_9_.1) | copy-start | bytes 245764
  12.2 5.6 %collective-permute-start.9 = (bf16[128,640]{1,0:T(8,128)(2,1)S(1)}, bf16[128,640]{1,0:T(8,128)(2,1)S(1)}, u32[]{:S(2)}, u32[]{:S(2)}) collective-permute-start(bf16[128,640]{1,0:T(8,128)(2,1)S(1)} %collective-permute-done.1.after.refs_1_), channel_id=1, source_target_pairs={{0,2},{1,3},{2,0},{3,1},{4,6},{5,7},{6,4},{7,5},{8,10},{9,11},{10,... | collective-permute-start | bytes 491528 | tf_op jit(solution)/shard_map/ppermute | solution.py:319
  15.1 5.1 %collective-permute-start.4 = (bf16[320,128]{1,0:T(8,128)(2,1)S(1)}, bf16[320,128]{1,0:T(8,128)(2,1)S(1)}, u32[]{:S(2)}, u32[]{:S(2)}) collective-permute-start(bf16[320,128]{1,0:T(8,128)(2,1)S(1)} %get-tuple-element.47.refs_0_), channel_id=1, source_target_pairs={{0,2},{1,3},{2,0},{3,1},{4,6},{5,7},{6,4},{7,5},{8,10},{9,11},{10,... | collective-permute-start | bytes 245768 | tf_op jit(solution)/shard_map/ppermute | solution.py:319
  16.6 4.7 %collective-permute-start.5 = (bf16[320,128]{1,0:T(8,128)(2,1)S(1)}, bf16[320,128]{1,0:T(8,128)(2,1)S(1)}, u32[]{:S(2)}, u32[]{:S(2)}) collective-permute-start(bf16[320,128]{1,0:T(8,128)(2,1)S(1)} %get-tuple-element.48.refs_1_), channel_id=1, source_target_pairs={{0,2},{1,3},{2,0},{3,1},{4,6},{5,7},{6,4},{7,5},{8,10},{9,11},{10,... | collective-permute-start | bytes 245768 | tf_op jit(solution)/shard_map/ppermute | solution.py:319
  18.2 4.4 %collective-permute-start.10 = (bf16[8,64,128]{2,1,0:T(8,128)(2,1)S(1)}, bf16[8,64,128]{2,1,0:T(8,128)(2,1)S(1)}, u32[]{:S(2)}, u32[]{:S(2)}) collective-permute-start(bf16[8,64,128]{2,1,0:T(8,128)(2,1)S(1)} %get-tuple-element.57), channel_id=1, source_target_pairs={{0,1},{1,0},{2,3},{3,2},{4,5},{5,4},{6,7},{7,6},{8,9},{9,8},{10,11... | collective-permute-start | bytes 393224 | tf_op jit(solution)/shard_map/ppermute | solution.py:319
  18.3 3.1 %collective-permute-start.2 = (bf16[320,128]{1,0:T(8,128)(2,1)S(1)}, bf16[320,128]{1,0:T(8,128)(2,1)S(1)}, u32[]{:S(2)}, u32[]{:S(2)}) collective-permute-start(bf16[320,128]{1,0:T(8,128)(2,1)S(1)} %get-tuple-element.47.refs_0_), channel_id=1, source_target_pairs={{0,1},{1,0},{2,3},{3,2},{4,5},{5,4},{6,7},{7,6},{8,9},{9,8},{10,11... | collective-permute-start | bytes 245768 | tf_op jit(solution)/shard_map/ppermute | solution.py:319
  18.8 2.6 %collective-permute-start.3 = (bf16[320,128]{1,0:T(8,128)(2,1)S(1)}, bf16[320,128]{1,0:T(8,128)(2,1)S(1)}, u32[]{:S(2)}, u32[]{:S(2)}) collective-permute-start(bf16[320,128]{1,0:T(8,128)(2,1)S(1)} %get-tuple-element.48.refs_1_), channel_id=1, source_target_pairs={{0,1},{1,0},{2,3},{3,2},{4,5},{5,4},{6,7},{7,6},{8,9},{9,8},{10,11... | collective-permute-start | bytes 245768 | tf_op jit(solution)/shard_map/ppermute | solution.py:319
  20.2 1.3 %collective-permute-start.6 = (bf16[320,128]{1,0:T(8,128)(2,1)S(1)}, bf16[320,128]{1,0:T(8,128)(2,1)S(1)}, u32[]{:S(2)}, u32[]{:S(2)}) collective-permute-start(bf16[320,128]{1,0:T(8,128)(2,1)S(1)} %collective-permute-done.4.refs_4_), channel_id=1, source_target_pairs={{0,1},{1,0},{2,3},{3,2},{4,5},{5,4},{6,7},{7,6},{8,9},{9,8},{10,11... | collective-permute-start | bytes 245768 | tf_op jit(solution)/shard_map/ppermute | solution.py:319
  21.3 1.3 %collective-permute-start.7 = (bf16[320,128]{1,0:T(8,128)(2,1)S(1)}, bf16[320,128]{1,0:T(8,128)(2,1)S(1)}, u32[]{:S(2)}, u32[]{:S(2)}) collective-permute-start(bf16[320,128]{1,0:T(8,128)(2,1)S(1)} %collective-permute-done.5.refs_5_), channel_id=1, source_target_pairs={{0,1},{1,0},{2,3},{3,2},{4,5},{5,4},{6,7},{7,6},{8,9},{9,8},{10,11... | collective-permute-start | bytes 245768 | tf_op jit(solution)/shard_map/ppermute | solution.py:319
  23.8 8.5 %collective-permute-start.11 = (bf16[192,128]{1,0:T(8,128)(2,1)S(1)}, bf16[192,128]{1,0:T(8,128)(2,1)S(1)}, u32[]{:S(2)}, u32[]{:S(2)}) collective-permute-start(bf16[192,128]{1,0:T(8,128)(2,1)S(1)} %get-tuple-element.59), channel_id=1, source_target_pairs={{0,4},{4,0},{8,12},{12,8},{16,20},{20,16},{24,28},{28,24},{1,5},{5... | collective-permute-start | bytes 147464 | tf_op jit(solution)/shard_map/ppermute | solution.py:319
  26.5 7.9 %collective-permute-start.12 = (bf16[192,128]{1,0:T(8,128)(2,1)S(1)}, bf16[192,128]{1,0:T(8,128)(2,1)S(1)}, u32[]{:S(2)}, u32[]{:S(2)}) collective-permute-start(bf16[192,128]{1,0:T(8,128)(2,1)S(1)} %get-tuple-element.60), channel_id=1, source_target_pairs={{0,8},{4,12},{8,0},{12,4},{16,24},{20,28},{24,16},{28,20},{1,9},{5... | collective-permute-start | bytes 147464 | tf_op jit(solution)/shard_map/ppermute | solution.py:319
  28.1 9.9 %collective-permute-start.13 = (bf16[192,128]{1,0:T(8,128)(2,1)S(1)}, bf16[192,128]{1,0:T(8,128)(2,1)S(1)}, u32[]{:S(2)}, u32[]{:S(2)}) collective-permute-start(bf16[192,128]{1,0:T(8,128)(2,1)S(1)} %get-tuple-element.61), channel_id=1, source_target_pairs={{0,12},{4,8},{8,4},{12,0},{16,28},{20,24},{24,20},{28,16},{1,13},{... | collective-permute-start | bytes 147464 | tf_op jit(solution)/shard_map/ppermute | solution.py:319
  28.1 9.9 %collective-permute-start.14 = (bf16[192,128]{1,0:T(8,128)(2,1)S(1)}, bf16[192,128]{1,0:T(8,128)(2,1)S(1)}, u32[]{:S(2)}, u32[]{:S(2)}) collective-permute-start(bf16[192,128]{1,0:T(8,128)(2,1)S(1)} %get-tuple-element.62), channel_id=1, source_target_pairs={{0,16},{4,20},{8,24},{12,28},{16,0},{20,4},{24,8},{28,12},{1,17},{... | collective-permute-start | bytes 147464 | tf_op jit(solution)/shard_map/ppermute | solution.py:319
  30.6 7.9 %collective-permute-start.15 = (bf16[192,128]{1,0:T(8,128)(2,1)S(1)}, bf16[192,128]{1,0:T(8,128)(2,1)S(1)}, u32[]{:S(2)}, u32[]{:S(2)}) collective-permute-start(bf16[192,128]{1,0:T(8,128)(2,1)S(1)} %get-tuple-element.63), channel_id=1, source_target_pairs={{0,20},{4,16},{8,28},{12,24},{16,4},{20,0},{24,12},{28,8},{1,21},{... | collective-permute-start | bytes 147464 | tf_op jit(solution)/shard_map/ppermute | solution.py:319
  32.3 6.3 %collective-permute-start.16 = (bf16[192,128]{1,0:T(8,128)(2,1)S(1)}, bf16[192,128]{1,0:T(8,128)(2,1)S(1)}, u32[]{:S(2)}, u32[]{:S(2)}) collective-permute-start(bf16[192,128]{1,0:T(8,128)(2,1)S(1)} %get-tuple-element.64), channel_id=1, source_target_pairs={{0,24},{4,28},{8,16},{12,20},{16,8},{20,12},{24,0},{28,4},{1,25},{... | collective-permute-start | bytes 147464 | tf_op jit(solution)/shard_map/ppermute | solution.py:319
  34.4 6.9 %collective-permute-start.17 = (bf16[192,128]{1,0:T(8,128)(2,1)S(1)}, bf16[192,128]{1,0:T(8,128)(2,1)S(1)}, u32[]{:S(2)}, u32[]{:S(2)}) collective-permute-start(bf16[192,128]{1,0:T(8,128)(2,1)S(1)} %get-tuple-element.65), channel_id=1, source_target_pairs={{0,28},{4,24},{8,20},{12,16},{16,12},{20,8},{24,4},{28,0},{1,29},{... | collective-permute-start | bytes 147464 | tf_op jit(solution)/shard_map/ppermute | solution.py:319

commit v3 on v2

--- a/solution.py
+++ b/solution.py
@@ -198,7 +198,7 @@
     return period, found
 
 
-def space_sum_body(groups, rows, *refs):
+def space_sum_body(groups, rows, time_rows, *refs):
     peers, steps = lax.axis_size("row"), lax.axis_size("tm")
     slots, (kept, came), refs = refs[: 2 * peers], refs[2 * peers : 2 * peers + 2], refs[2 * peers + 2 :]
     mine, sends, (rows_ref, main, rest) = refs[0], refs[1:steps], refs[steps:]
@@ -218,7 +218,7 @@
     held = round_up(-(-rows // period), 8)
     lane = lax.broadcasted_iota(jnp.int32, (held, LANES), 1)
     here, me = lax.axis_index("tm"), lax.axis_index("row")
-    early = kept.shape[1]
+    short = -(-rows // period)
     for k in range(steps):
         t = here ^ k
         start = (t * peers + me) * rows
@@ -231,14 +231,14 @@
                 rolled[j, tile, amount] = pltpu.roll(value, amount, 1) if amount else value
             return rolled[j, tile, amount]
 
-        parts = [kept[t] + came[t].astype(F32)]
+        parts = [(kept[t] + came[t].astype(F32))[:time_rows]]
         for row in layout:
             value = None
             for first, j, tile, amount in row:
                 piece = source(j, tile, amount)
                 value = piece if value is None else jnp.where(lane < first, value, piece)
-            parts.append(value)
-        blank = mine.shape[0] - early - held * len(layout)
+            parts.append(value[:short])
+        blank = mine.shape[0] - time_rows - short * len(layout)
         if blank:
             parts.append(jnp.zeros((blank, LANES), F32))
         piece = jnp.concatenate(parts, axis=0)
@@ -263,18 +263,16 @@
     space_terms(slots, rows_ref, LANES // 2, store)
 
 
-def final_body(factor, early, period, stride, *refs):
+def final_body(factor, stride, *refs):
     (mine, *came), (space_out, time_out) = refs[:-2], refs[-2:]
     total = mine[...]
     for ref in came:
         total = total + ref[...].astype(F32)
     total = total * factor
-    time_out[...] = total[: time_out.shape[0]]
-    held = space_out.shape[0] // stride
-    tall = (total.shape[0] - early) // stride // 8 * 8
+    first, short = time_out.shape[0], space_out.shape[0] // stride
+    time_out[...] = total[:first]
     for j in range(stride):
-        first = early + j * tall
-        space_out[pl.ds(j, held, stride=stride), :] = total[first : first + held]
+        space_out[pl.ds(j, short, stride=stride), :] = total[first + j * short : first + (j + 1) * short]
 
 
 def space_body(*refs):
@@ -378,19 +376,20 @@
     if even:
         rows = space_rows // devices
         period, layout = segments(width)
-        deep = round_up(tall + round_up(-(-rows // period), 8) * len(layout), 16)
+        full = -(-rows // period) * len(layout)
+        deep = round_up(time_rows // devices + full, 16)
         piece = (deep, LANES)
         scratch = (round_up(space_rows + 8 * period + rows, 8), LANES)
         mine, *sends = on_device(
-            functools.partial(space_sum_body, groups, rows),
+            functools.partial(space_sum_body, groups, rows, time_rows // devices),
             (*gathered, kept, came),
             [shape(piece, F32)] + [shape(piece, BF16)] * (steps - 1),
             [pltpu.VMEM((peers, 2 * ch, 2 * cols), BF16)] + [pltpu.VMEM(scratch, F32)] * 2,
         )
-        arrived = [swap(sends[k - 1], "tm", k) for k in range(1, steps)]
-        full = -(-rows // period) * len(layout)
+        order = sorted(range(1, steps), key=lambda k: (-k.bit_length(), k & 1, -k))
+        arrived = [swap(sends[k - 1], "tm", k) for k in order]
         space_share, time_share = on_device(
-            functools.partial(final_body, factor, tall, period, len(layout)),
+            functools.partial(final_body, factor, len(layout)),
             (mine, *arrived),
             [shape((full, LANES), F32), shape((time_rows // devices, time_width), F32)],
         )

time: 42.2 us -> 40 us (0.948)
  waiting for transfers between devices: 9.6 us -> 6.34 us
  starting transfers between devices: 23.9 us -> 25 us
    ppermute x16, waiting for transfers between devices: 7.64 us -> 4.39 us  [swap(): lax.ppermute(x, axis, [(i, i ^ bit) for i in range(lax.axis_size(axis))])]
    ppermute x16, starting transfers between devices: 17.1 us -> 18.2 us  [swap(): lax.ppermute(x, axis, [(i, i ^ bit) for i in range(lax.axis_size(axis))])]
  transfers between devices with their start and end apart: 18 -> 18, of which waited for: 9 -> 6; matrix products, arithmetic and copies ran while one was open for 0% -> 0% of each run, Pallas kernels for 11% -> 12%
where the time goes in v3:
time: 40 us; the launch traced here: 39.8 us
  starting transfers between devices  25 us (62%)
  Pallas kernels  7.67 us (19%)
  waiting for transfers between devices  6.34 us (16%)
  between operations  0.77 us (2%)
    ppermute x16, starting transfers between devices, swap(): lax.ppermute(x, axis, [(i, i ^ bit) for i in range(lax.axis_size(axis))])  18.2 us
    pallas_call x7, Pallas kernels, on_device(): pl.pallas_call(body, out_shape=outs, in_specs=[pl.BlockSpec(memory_space=...  7.67 us
    ppermute x1, starting transfers between devices, per_device(): before = lax.ppermute(packed, 'tm', [(i, i + 1) for i in range(steps - 1)])  5.51 us
    ppermute x16, waiting for transfers between devices, swap(): lax.ppermute(x, axis, [(i, i ^ bit) for i in range(lax.axis_size(axis))])  4.39 us
    ppermute x1, waiting for transfers between devices, per_device(): before = lax.ppermute(packed, 'tm', [(i, i + 1) for i in range(steps - 1)])  1.95 us
    ppermute x1, starting transfers between devices, per_device(): after = lax.ppermute(packed, 'tm', [(i + 1, i) for i in range(steps - 1)])  1.29 us
  transfers between devices with their start and end apart: 18, of which 6 were waited for; matrix products, arithmetic and copies ran while one was open for 0% of the time, Pallas kernels for 12%

profile of v3, /device:TPU:0, one launch (start us, length us, event | category | flops | bytes accessed | tf_op | source)
XLA Modules:
  0.0 39.8 jit_solution(16091409248305021024)
XLA Ops:
  0.6 1.1 %shard_map.109.own.refs_0_ = bf16[128,640]{1,0:T(8,128)(2,1)S(1)} custom-call(bf16[2,1,64,320]{3,2,1,0:T(8,128)(2,1)} %refs_8_.1, bf16[2,1,64,320]{3,2,1,0:T(8,128)(2,1)} %refs_9_.1), custom_call_target="tpu_custom_call" | custom-call | bytes 327680 | tf_op jit(solution)/shard_map/pallas_call | solution.py:27
  1.7 1.3 %collective-permute-start.1 = (bf16[128,640]{1,0:T(8,128)(2,1)S(1)}, bf16[128,640]{1,0:T(8,128)(2,1)S(1)}, u32[]{:S(2)}, u32[]{:S(2)}) collective-permute-start(bf16[128,640]{1,0:T(8,128)(2,1)S(1)} %shard_map.109.own.refs_0_), channel_id=1, source_target_pairs={{4,0},{8,4},{12,8},{16,12},{20,16},{24,20},{28,24},{5,1},{9,5},{13... | collective-permute-start | bytes 491528 | tf_op jit(solution)/shard_map/ppermute | solution.py:342
  3.0 5.5 %collective-permute-start = (bf16[128,640]{1,0:T(8,128)(2,1)S(1)}, bf16[128,640]{1,0:T(8,128)(2,1)S(1)}, u32[]{:S(2)}, u32[]{:S(2)}) collective-permute-start(bf16[128,640]{1,0:T(8,128)(2,1)S(1)} %shard_map.109.own.refs_0_), channel_id=1, source_target_pairs={{0,4},{4,8},{8,12},{12,16},{16,20},{20,24},{24,28},{1,5},{5,9},{9,... | collective-permute-start | bytes 491528 | tf_op jit(solution)/shard_map/ppermute | solution.py:343
  8.5 2.1 %collective-permute-start.8 = (bf16[128,640]{1,0:T(8,128)(2,1)S(1)}, bf16[128,640]{1,0:T(8,128)(2,1)S(1)}, u32[]{:S(2)}, u32[]{:S(2)}) collective-permute-start(bf16[128,640]{1,0:T(8,128)(2,1)S(1)} %shard_map.109.own.refs_0_), channel_id=1, source_target_pairs={{0,2},{1,3},{2,0},{3,1},{4,6},{5,7},{6,4},{7,5},{8,10},{9,11},{10,... | collective-permute-start | bytes 491528 | tf_op jit(solution)/shard_map/ppermute | solution.py:317
  10.6 1.5 %shard_map.110 = (f32[64,640]{1,0:T(8,128)S(1)}, f32[64,640]{1,0:T(8,128)S(1)}, f32[64,640]{1,0:T(8,128)S(1)}, bf16[2,2,64,320]{3,2,1,0:T(8,128)(2,1)S(1)}, bf16[3,5,128,128]{3,2,1,0:T(8,128)(2,1)S(1)}) custom-call(bf16[2,1,64,320]{3,2,1,0:T(8,128)(2,1)} %refs_8_.1, bf16[2,1,64,320]{3,2,1,0:T(8,128)(2,1)} %y2_far.1, bf16[2,1,64,320]{3,2,1,0:T(8,128)(2,1)} %c1_far.1, ...), custom_call_target="tpu_custom_call" | custom-call | bytes 2048000 | tf_op jit(solution)/shard_map/pallas_call | solution.py:27
  12.2 0.3 collective-permute-start.9
  12.5 1.9 %collective-permute-done.before = bf16[128,640]{1,0:T(8,128)(2,1)S(1)} collective-permute-done((bf16[128,640]{1,0:T(8,128)(2,1)S(1)}, bf16[128,640]{1,0:T(8,128)(2,1)S(1)}, u32[]{:S(2)}, u32[]{:S(2)}) %collective-permute-start) | collective-permute-done | bytes 163872 | tf_op jit(solution)/shard_map/ppermute | solution.py:343
  14.5 0.6 %shard_map.111 = (bf16[2,1,64,320]{3,2,1,0:T(8,128)(2,1)S(1)}, bf16[2,1,64,320]{3,2,1,0:T(8,128)(2,1)S(1)}, bf16[320,128]{1,0:T(8,128)(2,1)S(1)}, bf16[320,128]{1,0:T(8,128)(2,1)S(1)}) custom-call(bf16[128,640]{1,0:T(8,128)(2,1)S(1)} %collective-permute-done.before, bf16[128,640]{1,0:T(8,128)(2,1)S(1)} %collective-permute-done.1.after.refs_1_, ...), custom_call_target="tpu_custom_call" | custom-call | bytes 1802240 | tf_op jit(solution)/shard_map/pallas_call | solution.py:27
  15.1 1.6 %collective-permute-start.4 = (bf16[320,128]{1,0:T(8,128)(2,1)S(1)}, bf16[320,128]{1,0:T(8,128)(2,1)S(1)}, u32[]{:S(2)}, u32[]{:S(2)}) collective-permute-start(bf16[320,128]{1,0:T(8,128)(2,1)S(1)} %get-tuple-element.47.refs_0_), channel_id=1, source_target_pairs={{0,2},{1,3},{2,0},{3,1},{4,6},{5,7},{6,4},{7,5},{8,10},{9,11},{10,... | collective-permute-start | bytes 245768 | tf_op jit(solution)/shard_map/ppermute | solution.py:317
  16.6 0.5 %collective-permute-start.5 = (bf16[320,128]{1,0:T(8,128)(2,1)S(1)}, bf16[320,128]{1,0:T(8,128)(2,1)S(1)}, u32[]{:S(2)}, u32[]{:S(2)}) collective-permute-start(bf16[320,128]{1,0:T(8,128)(2,1)S(1)} %get-tuple-element.48.refs_1_), channel_id=1, source_target_pairs={{0,2},{1,3},{2,0},{3,1},{4,6},{5,7},{6,4},{7,5},{8,10},{9,11},{10,... | collective-permute-start | bytes 245768 | tf_op jit(solution)/shard_map/ppermute | solution.py:317
  17.2 0.6 %collective-permute-done.9.refs_3_ = bf16[128,640]{1,0:T(8,128)(2,1)S(1)} collective-permute-done((bf16[128,640]{1,0:T(8,128)(2,1)S(1)}, bf16[128,640]{1,0:T(8,128)(2,1)S(1)}, u32[]{:S(2)}, u32[]{:S(2)}) %collective-permute-start.9) | collective-permute-done | bytes 163872 | tf_op jit(solution)/shard_map/ppermute | solution.py:317
  17.8 0.4 %shard_map.113 = (f32[8,64,128]{2,1,0:T(8,128)S(1)}, bf16[8,64,128]{2,1,0:T(8,128)(2,1)S(1)}) custom-call(bf16[128,640]{1,0:T(8,128)(2,1)S(1)} %shard_map.109.own.refs_0_, bf16[128,640]{1,0:T(8,128)(2,1)S(1)} %collective-permute-done.1.after.refs_1_, bf16[128,640]{1,0:T(8,128)(2,1)S(1)} %collective-permute-done.8.refs_2_, ...), custom_call_target="tpu_custom_call" | custom-call | bytes 1048576 | tf_op jit(solution)/shard_map/pallas_call | solution.py:27
  18.3 0.5 %collective-permute-start.2 = (bf16[320,128]{1,0:T(8,128)(2,1)S(1)}, bf16[320,128]{1,0:T(8,128)(2,1)S(1)}, u32[]{:S(2)}, u32[]{:S(2)}) collective-permute-start(bf16[320,128]{1,0:T(8,128)(2,1)S(1)} %get-tuple-element.47.refs_0_), channel_id=1, source_target_pairs={{0,1},{1,0},{2,3},{3,2},{4,5},{5,4},{6,7},{7,6},{8,9},{9,8},{10,11... | collective-permute-start | bytes 245768 | tf_op jit(solution)/shard_map/ppermute | solution.py:317
  18.8 1.3 %collective-permute-done.4.refs_4_ = bf16[320,128]{1,0:T(8,128)(2,1)S(1)} collective-permute-done((bf16[320,128]{1,0:T(8,128)(2,1)S(1)}, bf16[320,128]{1,0:T(8,128)(2,1)S(1)}, u32[]{:S(2)}, u32[]{:S(2)}) %collective-permute-start.4) | collective-permute-done | bytes 81952 | tf_op jit(solution)/shard_map/ppermute | solution.py:317
  20.2 1.1 %collective-permute-done.5.refs_5_ = bf16[320,128]{1,0:T(8,128)(2,1)S(1)} collective-permute-done((bf16[320,128]{1,0:T(8,128)(2,1)S(1)}, bf16[320,128]{1,0:T(8,128)(2,1)S(1)}, u32[]{:S(2)}, u32[]{:S(2)}) %collective-permute-start.5) | collective-permute-done | bytes 81952 | tf_op jit(solution)/shard_map/ppermute | solution.py:317
  21.5 1.1 %collective-permute-done.7.refs_7_ = bf16[320,128]{1,0:T(8,128)(2,1)S(1)} collective-permute-done((bf16[320,128]{1,0:T(8,128)(2,1)S(1)}, bf16[320,128]{1,0:T(8,128)(2,1)S(1)}, u32[]{:S(2)}, u32[]{:S(2)}) %collective-permute-start.7) | collective-permute-done | bytes 81952 | tf_op jit(solution)/shard_map/ppermute | solution.py:317
  22.6 1.2 %shard_map.114 = (f32[176,128]{1,0:T(8,128)S(1)}, bf16[176,128]{1,0:T(8,128)(2,1)S(1)}, bf16[176,128]{1,0:T(8,128)(2,1)S(1)}, bf16[176,128]{1,0:T(8,128)(2,1)S(1...) custom-call(bf16[320,128]{1,0:T(8,128)(2,1)S(1)} %get-tuple-element., ...), custom_call_target="tpu_custom_call" | custom-call | bytes 1454080 | tf_op jit(solution)/shard_map/pallas_call | solution.py:27
  23.8 3.9 %collective-permute-start.11 = (bf16[176,128]{1,0:T(8,128)(2,1)S(1)}, bf16[176,128]{1,0:T(8,128)(2,1)S(1)}, u32[]{:S(2)}, u32[]{:S(2)}) collective-permute-start(bf16[176,128]{1,0:T(8,128)(2,1)S(1)} %get-tuple-element.59), channel_id=1, source_target_pairs={{0,24},{4,28},{8,16},{12,20},{16,8},{20,12},{24,0},{28,4},{1,25},{... | collective-permute-start | bytes 135176 | tf_op jit(solution)/shard_map/ppermute | solution.py:317
  27.7 3.7 %collective-permute-start.13 = (bf16[176,128]{1,0:T(8,128)(2,1)S(1)}, bf16[176,128]{1,0:T(8,128)(2,1)S(1)}, u32[]{:S(2)}, u32[]{:S(2)}) collective-permute-start(bf16[176,128]{1,0:T(8,128)(2,1)S(1)} %get-tuple-element.61), channel_id=1, source_target_pairs={{0,28},{4,24},{8,20},{12,16},{16,12},{20,8},{24,4},{28,0},{1,29},{... | collective-permute-start | bytes 135176 | tf_op jit(solution)/shard_map/ppermute | solution.py:317
  31.5 1.6 %collective-permute-start.15 = (bf16[176,128]{1,0:T(8,128)(2,1)S(1)}, bf16[176,128]{1,0:T(8,128)(2,1)S(1)}, u32[]{:S(2)}, u32[]{:S(2)}) collective-permute-start(bf16[176,128]{1,0:T(8,128)(2,1)S(1)} %get-tuple-element.63), channel_id=1, source_target_pairs={{0,8},{4,12},{8,0},{12,4},{16,24},{20,28},{24,16},{28,20},{1,9},{5... | collective-permute-start | bytes 135176 | tf_op jit(solution)/shard_map/ppermute | solution.py:317
  33.0 1.7 %collective-permute-start.16 = (bf16[176,128]{1,0:T(8,128)(2,1)S(1)}, bf16[176,128]{1,0:T(8,128)(2,1)S(1)}, u32[]{:S(2)}, u32[]{:S(2)}) collective-permute-start(bf16[176,128]{1,0:T(8,128)(2,1)S(1)} %get-tuple-element.64), channel_id=1, source_target_pairs={{0,12},{4,8},{8,4},{12,0},{16,28},{20,24},{24,20},{28,16},{1,13},{... | collective-permute-start | bytes 135176 | tf_op jit(solution)/shard_map/ppermute | solution.py:317
  34.7 2.2 %collective-permute-start.17 = (bf16[176,128]{1,0:T(8,128)(2,1)S(1)}, bf16[176,128]{1,0:T(8,128)(2,1)S(1)}, u32[]{:S(2)}, u32[]{:S(2)}) collective-permute-start(bf16[176,128]{1,0:T(8,128)(2,1)S(1)} %get-tuple-element.65), channel_id=1, source_target_pairs={{0,4},{4,0},{8,12},{12,8},{16,20},{20,16},{24,28},{28,24},{1,5},{5... | collective-permute-start | bytes 135176 | tf_op jit(solution)/shard_map/ppermute | solution.py:317
  37.0 2.1 %shard_map.112 = (bf16[2,1,64,320]{3,2,1,0:T(8,128)(2,1)}, bf16[2,1,64,320]{3,2,1,0:T(8,128)(2,1)}, bf16[2,1,64,320]{3,2,1,0:T(8,128)(2,1)}, bf16[2,1,64,320]{3,2,1,0:T(8,128)(2,1)}) custom-call(bf16[320,128]{1,0:T(8,128)(2,1)S(1)} %get-tuple-element.47.refs_0_, bf16[320,128]{1,0:T(8,128)(2,1)S(1)} %get-tuple-element.48.refs_1_, ...), custom_call_target="tpu_custom_call" | custom-call | bytes 2232320 | tf_op jit(solution)/shard_map/pallas_call | solution.py:27
  39.1 0.7 %shard_map.115 = (f32[115,128]{1,0:T(8,128)}, f32[60,128]{1,0:T(8,128)}) custom-call(f32[176,128]{1,0:T(8,128)S(1)} %get-tuple-element.58.refs_0_, bf16[176,128]{1,0:T(8,128)(2,1)S(1)} %collective-permute-done.11.refs_1_, bf16[176,128]{1,0:T(8,128)(2,1)S(1)} %collective-permute-done.12.refs_2_, bf16[176,128]{1,0:T(8,128)(2,1)S(1)} %collective-permute-done.13.refs_3_, ...), custom_call_target="tpu_custom_call" | custom-call | bytes 495104 | tf_op jit(solution)/shard_map/pallas_call | solution.py:27
  (25 shorter events, 0.3 us)
Async XLA Ops:
  1.7 10.4 %collective-permute-start.1 = (bf16[128,640]{1,0:T(8,128)(2,1)S(1)}, bf16[128,640]{1,0:T(8,128)(2,1)S(1)}, u32[]{:S(2)}, u32[]{:S(2)}) collective-permute-start(bf16[128,640]{1,0:T(8,128)(2,1)S(1)} %shard_map.109.own.refs_0_), channel_id=1, source_target_pairs={{4,0},{8,4},{12,8},{16,12},{20,16},{24,20},{28,24},{5,1},{9,5},{13... | collective-permute-start | bytes 491528 | tf_op jit(solution)/shard_map/ppermute | solution.py:342
  3.0 11.4 %collective-permute-start = (bf16[128,640]{1,0:T(8,128)(2,1)S(1)}, bf16[128,640]{1,0:T(8,128)(2,1)S(1)}, u32[]{:S(2)}, u32[]{:S(2)}) collective-permute-start(bf16[128,640]{1,0:T(8,128)(2,1)S(1)} %shard_map.109.own.refs_0_), channel_id=1, source_target_pairs={{0,4},{4,8},{8,12},{12,16},{16,20},{20,24},{24,28},{1,5},{5,9},{9,... | collective-permute-start | bytes 491528 | tf_op jit(solution)/shard_map/ppermute | solution.py:343
  8.5 8.6 %collective-permute-start.8 = (bf16[128,640]{1,0:T(8,128)(2,1)S(1)}, bf16[128,640]{1,0:T(8,128)(2,1)S(1)}, u32[]{:S(2)}, u32[]{:S(2)}) collective-permute-start(bf16[128,640]{1,0:T(8,128)(2,1)S(1)} %shard_map.109.own.refs_0_), channel_id=1, source_target_pairs={{0,2},{1,3},{2,0},{3,1},{4,6},{5,7},{6,4},{7,5},{8,10},{9,11},{10,... | collective-permute-start | bytes 491528 | tf_op jit(solution)/shard_map/ppermute | solution.py:317
  12.1 24.8 %copy-start = (bf16[3,3,2,160,160]{4,3,2,1,0:T(8,128)(2,1)S(1)}, bf16[3,3,2,160,160]{4,3,2,1,0:T(8,128)(2,1)}, u32[]{:S(2)}) copy-start(bf16[3,3,2,160,160]{4,3,2,1,0:T(8,128)(2,1)} %refs_12_.1) | copy-start | bytes 2764804
  12.1 24.8 %copy-start.1 = (bf16[2,1,64,320]{3,2,1,0:T(8,128)(2,1)S(1)}, bf16[2,1,64,320]{3,2,1,0:T(8,128)(2,1)}, u32[]{:S(2)}) copy-start(bf16[2,1,64,320]{3,2,1,0:T(8,128)(2,1)} %refs_8_.1) | copy-start | bytes 245764
  12.1 24.8 %copy-start.2 = (bf16[2,1,64,320]{3,2,1,0:T(8,128)(2,1)S(1)}, bf16[2,1,64,320]{3,2,1,0:T(8,128)(2,1)}, u32[]{:S(2)}) copy-start(bf16[2,1,64,320]{3,2,1,0:T(8,128)(2,1)} %refs_9_.1) | copy-start | bytes 245764
  12.2 5.6 %collective-permute-start.9 = (bf16[128,640]{1,0:T(8,128)(2,1)S(1)}, bf16[128,640]{1,0:T(8,128)(2,1)S(1)}, u32[]{:S(2)}, u32[]{:S(2)}) collective-permute-start(bf16[128,640]{1,0:T(8,128)(2,1)S(1)} %collective-permute-done.1.after.refs_1_), channel_id=1, source_target_pairs={{0,2},{1,3},{2,0},{3,1},{4,6},{5,7},{6,4},{7,5},{8,10},{9,11},{10,... | collective-permute-start | bytes 491528 | tf_op jit(solution)/shard_map/ppermute | solution.py:317
  15.1 5.1 %collective-permute-start.4 = (bf16[320,128]{1,0:T(8,128)(2,1)S(1)}, bf16[320,128]{1,0:T(8,128)(2,1)S(1)}, u32[]{:S(2)}, u32[]{:S(2)}) collective-permute-start(bf16[320,128]{1,0:T(8,128)(2,1)S(1)} %get-tuple-element.47.refs_0_), channel_id=1, source_target_pairs={{0,2},{1,3},{2,0},{3,1},{4,6},{5,7},{6,4},{7,5},{8,10},{9,11},{10,... | collective-permute-start | bytes 245768 | tf_op jit(solution)/shard_map/ppermute | solution.py:317
  16.6 4.7 %collective-permute-start.5 = (bf16[320,128]{1,0:T(8,128)(2,1)S(1)}, bf16[320,128]{1,0:T(8,128)(2,1)S(1)}, u32[]{:S(2)}, u32[]{:S(2)}) collective-permute-start(bf16[320,128]{1,0:T(8,128)(2,1)S(1)} %get-tuple-element.48.refs_1_), channel_id=1, source_target_pairs={{0,2},{1,3},{2,0},{3,1},{4,6},{5,7},{6,4},{7,5},{8,10},{9,11},{10,... | collective-permute-start | bytes 245768 | tf_op jit(solution)/shard_map/ppermute | solution.py:317
  18.2 4.4 %collective-permute-start.10 = (bf16[8,64,128]{2,1,0:T(8,128)(2,1)S(1)}, bf16[8,64,128]{2,1,0:T(8,128)(2,1)S(1)}, u32[]{:S(2)}, u32[]{:S(2)}) collective-permute-start(bf16[8,64,128]{2,1,0:T(8,128)(2,1)S(1)} %get-tuple-element.57), channel_id=1, source_target_pairs={{0,1},{1,0},{2,3},{3,2},{4,5},{5,4},{6,7},{7,6},{8,9},{9,8},{10,11... | collective-permute-start | bytes 393224 | tf_op jit(solution)/shard_map/ppermute | solution.py:317
  18.3 3.1 %collective-permute-start.2 = (bf16[320,128]{1,0:T(8,128)(2,1)S(1)}, bf16[320,128]{1,0:T(8,128)(2,1)S(1)}, u32[]{:S(2)}, u32[]{:S(2)}) collective-permute-start(bf16[320,128]{1,0:T(8,128)(2,1)S(1)} %get-tuple-element.47.refs_0_), channel_id=1, source_target_pairs={{0,1},{1,0},{2,3},{3,2},{4,5},{5,4},{6,7},{7,6},{8,9},{9,8},{10,11... | collective-permute-start | bytes 245768 | tf_op jit(solution)/shard_map/ppermute | solution.py:317
  18.8 2.6 %collective-permute-start.3 = (bf16[320,128]{1,0:T(8,128)(2,1)S(1)}, bf16[320,128]{1,0:T(8,128)(2,1)S(1)}, u32[]{:S(2)}, u32[]{:S(2)}) collective-permute-start(bf16[320,128]{1,0:T(8,128)(2,1)S(1)} %get-tuple-element.48.refs_1_), channel_id=1, source_target_pairs={{0,1},{1,0},{2,3},{3,2},{4,5},{5,4},{6,7},{7,6},{8,9},{9,8},{10,11... | collective-permute-start | bytes 245768 | tf_op jit(solution)/shard_map/ppermute | solution.py:317
  20.2 1.3 %collective-permute-start.6 = (bf16[320,128]{1,0:T(8,128)(2,1)S(1)}, bf16[320,128]{1,0:T(8,128)(2,1)S(1)}, u32[]{:S(2)}, u32[]{:S(2)}) collective-permute-start(bf16[320,128]{1,0:T(8,128)(2,1)S(1)} %collective-permute-done.4.refs_4_), channel_id=1, source_target_pairs={{0,1},{1,0},{2,3},{3,2},{4,5},{5,4},{6,7},{7,6},{8,9},{9,8},{10,11... | collective-permute-start | bytes 245768 | tf_op jit(solution)/shard_map/ppermute | solution.py:317
  21.3 1.3 %collective-permute-start.7 = (bf16[320,128]{1,0:T(8,128)(2,1)S(1)}, bf16[320,128]{1,0:T(8,128)(2,1)S(1)}, u32[]{:S(2)}, u32[]{:S(2)}) collective-permute-start(bf16[320,128]{1,0:T(8,128)(2,1)S(1)} %collective-permute-done.5.refs_5_), channel_id=1, source_target_pairs={{0,1},{1,0},{2,3},{3,2},{4,5},{5,4},{6,7},{7,6},{8,9},{9,8},{10,11... | collective-permute-start | bytes 245768 | tf_op jit(solution)/shard_map/ppermute | solution.py:317
  23.8 9.2 %collective-permute-start.11 = (bf16[176,128]{1,0:T(8,128)(2,1)S(1)}, bf16[176,128]{1,0:T(8,128)(2,1)S(1)}, u32[]{:S(2)}, u32[]{:S(2)}) collective-permute-start(bf16[176,128]{1,0:T(8,128)(2,1)S(1)} %get-tuple-element.59), channel_id=1, source_target_pairs={{0,24},{4,28},{8,16},{12,20},{16,8},{20,12},{24,0},{28,4},{1,25},{... | collective-permute-start | bytes 135176 | tf_op jit(solution)/shard_map/ppermute | solution.py:317
  27.7 7.0 %collective-permute-start.12 = (bf16[176,128]{1,0:T(8,128)(2,1)S(1)}, bf16[176,128]{1,0:T(8,128)(2,1)S(1)}, u32[]{:S(2)}, u32[]{:S(2)}) collective-permute-start(bf16[176,128]{1,0:T(8,128)(2,1)S(1)} %get-tuple-element.60), channel_id=1, source_target_pairs={{0,16},{4,20},{8,24},{12,28},{16,0},{20,4},{24,8},{28,12},{1,17},{... | collective-permute-start | bytes 135176 | tf_op jit(solution)/shard_map/ppermute | solution.py:317
  27.7 11.4 %collective-permute-start.13 = (bf16[176,128]{1,0:T(8,128)(2,1)S(1)}, bf16[176,128]{1,0:T(8,128)(2,1)S(1)}, u32[]{:S(2)}, u32[]{:S(2)}) collective-permute-start(bf16[176,128]{1,0:T(8,128)(2,1)S(1)} %get-tuple-element.61), channel_id=1, source_target_pairs={{0,28},{4,24},{8,20},{12,16},{16,12},{20,8},{24,4},{28,0},{1,29},{... | collective-permute-start | bytes 135176 | tf_op jit(solution)/shard_map/ppermute | solution.py:317
  31.5 7.7 %collective-permute-start.14 = (bf16[176,128]{1,0:T(8,128)(2,1)S(1)}, bf16[176,128]{1,0:T(8,128)(2,1)S(1)}, u32[]{:S(2)}, u32[]{:S(2)}) collective-permute-start(bf16[176,128]{1,0:T(8,128)(2,1)S(1)} %get-tuple-element.62), channel_id=1, source_target_pairs={{0,20},{4,16},{8,28},{12,24},{16,4},{20,0},{24,12},{28,8},{1,21},{... | collective-permute-start | bytes 135176 | tf_op jit(solution)/shard_map/ppermute | solution.py:317
  31.5 7.7 %collective-permute-start.15 = (bf16[176,128]{1,0:T(8,128)(2,1)S(1)}, bf16[176,128]{1,0:T(8,128)(2,1)S(1)}, u32[]{:S(2)}, u32[]{:S(2)}) collective-permute-start(bf16[176,128]{1,0:T(8,128)(2,1)S(1)} %get-tuple-element.63), channel_id=1, source_target_pairs={{0,8},{4,12},{8,0},{12,4},{16,24},{20,28},{24,16},{28,20},{1,9},{5... | collective-permute-start | bytes 135176 | tf_op jit(solution)/shard_map/ppermute | solution.py:317
  33.0 6.1 %collective-permute-start.16 = (bf16[176,128]{1,0:T(8,128)(2,1)S(1)}, bf16[176,128]{1,0:T(8,128)(2,1)S(1)}, u32[]{:S(2)}, u32[]{:S(2)}) collective-permute-start(bf16[176,128]{1,0:T(8,128)(2,1)S(1)} %get-tuple-element.64), channel_id=1, source_target_pairs={{0,12},{4,8},{8,4},{12,0},{16,28},{20,24},{24,20},{28,16},{1,13},{... | collective-permute-start | bytes 135176 | tf_op jit(solution)/shard_map/ppermute | solution.py:317
  34.7 4.4 %collective-permute-start.17 = (bf16[176,128]{1,0:T(8,128)(2,1)S(1)}, bf16[176,128]{1,0:T(8,128)(2,1)S(1)}, u32[]{:S(2)}, u32[]{:S(2)}) collective-permute-start(bf16[176,128]{1,0:T(8,128)(2,1)S(1)} %get-tuple-element.65), channel_id=1, source_target_pairs={{0,4},{4,0},{8,12},{12,8},{16,20},{20,16},{24,28},{28,24},{1,5},{5... | collective-permute-start | bytes 135176 | tf_op jit(solution)/shard_map/ppermute | solution.py:317

commit v4 on v3

--- a/solution.py
+++ b/solution.py
@@ -97,21 +97,22 @@
     weight_out[...] = weight[...]
 
 
-def time_body(before, after, forth0, back0, slope, base, weight, x2_out, g1_out, act_out, cot_out):
+def time_body(near, far, forth0, back0, slope, base, weight, x2_out, g1_out, held_out):
     cols = forth0.shape[0]
     groups, width = weight.shape[1:3]
+    tap = jnp.where(lax.axis_index("tm") % 2 == 0, 2, 0)
     forth, back = [], []
     for q in range(groups):
         lanes = slice(q * width, (q + 1) * width)
         forth.append(
-            dot(before[:cols, lanes], weight[0, q], 1, 0)
-            + forth0[:, lanes]
-            + dot(after[:cols, lanes], weight[2, q], 1, 0)
+            forth0[:, lanes]
+            + dot(near[:cols, lanes], weight[tap, q], 1, 0)
+            + dot(far[:cols, lanes], weight[2 - tap, q], 1, 0)
         )
         back.append(
-            dot(after[cols:, lanes], weight[0, q], 1, 1)
-            + back0[:, lanes]
-            + dot(before[cols:, lanes], weight[2, q], 1, 1)
+            back0[:, lanes]
+            + dot(near[cols:, lanes], weight[2 - tap, q], 1, 1)
+            + dot(far[cols:, lanes], weight[tap, q], 1, 1)
         )
     branch = unsqueezed(jnp.concatenate(forth, axis=-1))
     back = unsqueezed(jnp.concatenate(back, axis=-1) * slope[...])
@@ -124,47 +125,84 @@
         v = x2.astype(F32)
         acts.append(v * sigmoid(v))
         cots.append(g1.astype(F32))
-    act_out[...] = jnp.concatenate(acts, axis=0).T.astype(BF16)
-    cot_out[...] = jnp.concatenate(cots, axis=0).T.astype(BF16)
-
-
-def time_terms(owns, afters, total):
-    cols = owns[0].shape[0] // 2
+    ch = held_out.shape[0] // 2
+    held_out[:ch] = jnp.concatenate(acts, axis=0).T.astype(BF16)
+    held_out[ch:] = jnp.concatenate(cots, axis=0).T.astype(BF16)
+
+
+def time_terms(own, pairs, total):
+    cols = own.shape[0] // 2
     width = total.shape[1]
-    groups = owns[0].shape[1] // width
-    acts, cots = [], []
-    for refs in (owns, afters):
-        act = jnp.concatenate([ref[:cols] for ref in refs], axis=0)
-        acts.append(act.astype(F32).T.astype(BF16))
-        cots.append(jnp.concatenate([ref[cols:] for ref in refs], axis=0))
-    for k, (act, cot) in enumerate(((acts[0], cots[1]), (acts[0], cots[0]), (acts[1], cots[0]))):
+    groups = own.shape[1] // width
+    act = own[:cols].astype(F32).T.astype(BF16)
+    for k, cot in pairs:
         for q in range(groups):
             part = slice(q * width, (q + 1) * width)
-            term = dot(act[part], cot[:, part], 1, 0)
-            total[pl.ds((k * groups + q) * width, width), :] = term
-
-
-def time_sum_body(rows, *refs):
-    (keep, send, total), refs = refs[-3:], refs[:-3]
-    time_terms(refs[0::2], refs[1::2], total)
+            at = pl.multiple_of((k * groups + q) * width, width)
+            total[pl.ds(at, width), :] = dot(act[part], cot[cols:, part], 1, 0)
+
+
+def near_tap():
+    return jnp.where(lax.axis_index("tm") % 2 == 0, 0, 2)
+
+
+def time_near_body(own, near, total):
+    total[...] = jnp.zeros_like(total)
+    time_terms(own, ((1, own), (near_tap(), near)), total)
+
+
+def time_sum_body(offsets, rows, own, far, early, keep, *refs):
+    sends, total = refs[:-1], refs[-1]
+    total[: early.shape[0]] = early[...]
+    time_terms(own, ((2 - near_tap(), far),), total)
     me, peers, steps = lax.axis_index("row"), lax.axis_size("row"), lax.axis_size("tm")
-    held = keep.shape[1]
-    for t in range(steps):
-        keep[t] = total[pl.ds((t * peers + me) * rows, held), :]
-        send[t] = total[pl.ds((t * peers + (me ^ 1)) * rows, held), :].astype(BF16)
-
-
-def time_sum_whole_body(own, after, total):
-    time_terms((own,), (after,), total)
+    held, size = keep.shape[2], sends[0].shape[0]
+    for u, offset in enumerate(offsets):
+        for t in range(steps):
+            mine = (t * peers + (me ^ offset)) * rows
+            other = (t * peers + (me ^ offset ^ 1)) * rows
+            keep[u, t] = total[pl.ds(mine, held), :]
+            part = sends[(u * steps + t) // size]
+            part[t % size] = total[pl.ds(other, held), :].astype(BF16)
+
+
+def time_sum_whole_body(own, far, early, total):
+    total[...] = early[...]
+    time_terms(own, ((2 - near_tap(), far),), total)
+
+
+def fold_body(kept, *refs):
+    *came, keep, send = refs
+    steps, size = kept.shape[1], came[0].shape[0]
+    half = keep.shape[0]
+    for i, ref in enumerate(came):
+        u, t = divmod(i * size, steps)
+        total = kept[u, t : t + size] + ref[...].astype(F32)
+        if u < half:
+            keep[u, t : t + size] = total
+        else:
+            send[u - half, t : t + size] = total.astype(BF16)
+
+
+def place(slots, rows_ref, lead):
+    me, ch = lax.axis_index("row"), rows_ref.shape[1]
+    peers = lax.axis_size("row")
+    whole = peers // 2 + 1
+    rest = slots[whole:]
+    parts = len(rest) // (peers - whole) if rest else 1
+    slots = [(v,) for v in slots[:whole]] + [
+        rest[i : i + parts] for i in range(0, len(rest), parts)
+    ]
+    for k, refs in zip(slot_order(peers), slots):
+        for j, ref in enumerate(refs):
+            size = ch // len(refs)
+            rows_ref[(me ^ k) + lead, j * size : (j + 1) * size] = ref[...]
 
 
 def space_terms(slots, rows_ref, cols, store):
-    peers = len(slots) // 2
-    me = lax.axis_index("row")
+    peers = lax.axis_size("row")
     ch = rows_ref.shape[1] // 2
-    for k in range(peers):
-        rows_ref[me ^ k, :ch] = slots[2 * k][...]
-        rows_ref[me ^ k, ch:] = slots[2 * k + 1][...]
+    place(slots, rows_ref, 0)
     column = lax.broadcasted_iota(jnp.int32, (ch, LANES), 1) % cols
     act, shifts = [], ([], [], [])
     for r in range(peers):
@@ -198,10 +236,10 @@
     return period, found
 
 
-def space_sum_body(groups, rows, time_rows, *refs):
+def space_sum_body(count, groups, rows, time_rows, *refs):
     peers, steps = lax.axis_size("row"), lax.axis_size("tm")
-    slots, (kept, came), refs = refs[: 2 * peers], refs[2 * peers : 2 * peers + 2], refs[2 * peers + 2 :]
-    mine, sends, (rows_ref, main, rest) = refs[0], refs[1:steps], refs[steps:]
+    slots, refs = refs[:count], refs[count:]
+    out, rows_ref, main, rest = refs
     ch = rows_ref.shape[1] // 2
     width = ch // groups
 
@@ -231,26 +269,34 @@
                 rolled[j, tile, amount] = pltpu.roll(value, amount, 1) if amount else value
             return rolled[j, tile, amount]
 
-        parts = [(kept[t] + came[t].astype(F32))[:time_rows]]
+        parts = [jnp.zeros((time_rows, LANES), F32)]
         for row in layout:
             value = None
             for first, j, tile, amount in row:
                 piece = source(j, tile, amount)
                 value = piece if value is None else jnp.where(lane < first, value, piece)
             parts.append(value[:short])
-        blank = mine.shape[0] - time_rows - short * len(layout)
+        blank = out.shape[1] - time_rows - short * len(layout)
         if blank:
             parts.append(jnp.zeros((blank, LANES), F32))
-        piece = jnp.concatenate(parts, axis=0)
+        out[k] = jnp.concatenate(parts, axis=0)
+
+
+def join_body(time_rows, pieces, kept, came, mine, *sends):
+    tall = kept.shape[2]
+    row = lax.broadcasted_iota(jnp.int32, (tall, LANES), 0)
+    for k in range(pieces.shape[0]):
+        t = lax.axis_index("tm") ^ k
+        terms = jnp.where(row < time_rows, kept[0, t] + came[0, t].astype(F32), 0.0)
+        piece = jnp.concatenate([pieces[k, :tall] + terms, pieces[k, tall:]], axis=0)
         if k == 0:
             mine[...] = piece
         else:
             sends[k - 1][...] = piece.astype(BF16)
 
 
-def space_sum_whole_body(groups, *refs):
-    peers = lax.axis_size("row")
-    slots, (total, rows_ref) = refs[: 2 * peers], refs[2 * peers :]
+def space_sum_whole_body(count, groups, *refs):
+    slots, (total, rows_ref) = refs[:count], refs[count:]
     ch = rows_ref.shape[1] // 2
     width = ch // groups
 
@@ -275,9 +321,9 @@
         space_out[pl.ds(j, short, stride=stride), :] = total[first + j * short : first + (j + 1) * short]
 
 
-def space_body(*refs):
+def space_body(count, *refs):
     peers = lax.axis_size("row")
-    slots, refs = refs[: 2 * peers], refs[2 * peers :]
+    slots, refs = refs[:count], refs[count:]
     y1, c2, x2, g1, weight, x1_out, x2_out, g1_out, g2_out, rows_ref = refs
     x2_out[...] = x2[...]
     g1_out[...] = g1[...]
@@ -286,9 +332,7 @@
     groups, width = weight.shape[2:4]
     rows_ref[0] = jnp.zeros(rows_ref.shape[1:], BF16)
     rows_ref[peers + 1] = jnp.zeros(rows_ref.shape[1:], BF16)
-    for k in range(peers):
-        rows_ref[(me ^ k) + 1, :ch] = slots[2 * k][...]
-        rows_ref[(me ^ k) + 1, ch:] = slots[2 * k + 1][...]
+    place(slots, rows_ref, 1)
     column = lax.broadcasted_iota(jnp.int32, (LANES, width), 0) % cols
     forth, back = [None] * groups, [None] * groups
     for a in range(3):
@@ -322,7 +366,24 @@
     for bit in reversed(bits):
         for k in list(slots):
             slots[k ^ bit] = swap(slots[k], axis, bit)
-    return [slots[k] for k in sorted(slots)]
+    return slots
+
+
+def slot_order(peers):
+    last = [k for k in range(peers) if k & 1 and k > 1]
+    return [k for k in range(peers) if k not in last] + last
+
+
+def row_offsets(bits):
+    if not bits:
+        return [0]
+    rest = row_offsets(bits[1:])
+    return rest + [o ^ bits[0] for o in rest]
+
+
+def neighbours(x, axis, first):
+    lower = range(first, lax.axis_size(axis) - 1, 2)
+    return lax.ppermute(x, axis, [p for i in lower for p in ((i, i + 1), (i + 1, i))])
 
 
 def per_device(y1, y2, c1, c2, weight_space, temporal_weight):
@@ -339,8 +400,7 @@
 
     packed = on_device(open_body, (y1, c2), [shape((2 * cols, 2 * ch), BF16)], far=2)[0]
     up = [(i, i + 1) for i in range(steps - 1)]
-    after = lax.ppermute(packed, "tm", [(i + 1, i) for i in range(steps - 1)])
-    before = lax.ppermute(packed, "tm", [(i, i + 1) for i in range(steps - 1)])
+    near, far = neighbours(packed, "tm", 0), neighbours(packed, "tm", 1)
     wide = shape((cols, 2 * ch), F32)
     centre = on_device(
         centre_body,
@@ -351,27 +411,41 @@
 
     even = time_rows % devices == 0 and space_rows % devices == 0
     bits = [1 << i for i in range(peers.bit_length() - 1)]
+    near, centre = lax.optimization_barrier((near, centre))
+    early = on_device(time_near_body, (packed, near), [shape((time_rows, time_width), F32)])[0]
     if even:
         rows = time_rows // devices
         tall = round_up(rows, 16)
-        part = (steps, tall, time_width)
-        held, centre = lax.optimization_barrier((after, centre))
-        owns, afters = gather(packed, "row", bits[1:]), gather(held, "row", bits[1:])
-        kept, sent = on_device(
-            functools.partial(time_sum_body, rows),
-            [v for pair in zip(owns, afters) for v in pair],
-            [shape(part, F32), shape(part, BF16)],
+        offsets = row_offsets(bits[1:])
+        block = (len(offsets), steps, tall, time_width)
+        pieces = len(offsets)
+        share = (len(offsets) * steps // pieces, *block[2:])
+        kept, *sent = on_device(
+            functools.partial(time_sum_body, offsets, rows),
+            (packed, far, early),
+            [shape(block, F32)] + [shape(share, BF16)] * pieces,
             [pltpu.VMEM((round_up(time_rows + tall, 8), time_width), F32)],
         )
-        came = swap(sent, "row", 1)
-
-    x2, g1, act, cot = on_device(
+        came = [swap(v, "row", 1) for v in sent]
+        for bit in bits[1:]:
+            block = (block[0] // 2, *block[1:])
+            kept, sent = on_device(
+                fold_body, (kept, *came), [shape(block, F32), shape(block, BF16)]
+            )
+            came = [swap(sent, "row", bit)]
+    x2, g1, held = on_device(
         time_body,
-        (before, after, *centre),
-        [shape(y1.shape, BF16)] * 2 + [shape((ch, 2 * cols), BF16)] * 2,
+        (near, far, *centre),
+        [shape(y1.shape, BF16)] * 2 + [shape((2 * ch, 2 * cols), BF16)],
     )
-    pairs = zip(gather(act, "row", bits), gather(cot, "row", bits))
-    gathered = [v for pair in pairs for v in pair]
+    slots = {k: (v,) for k, v in gather(held, "row", bits[1:]).items()}
+    slots[1] = (swap(held, "row", 1),)
+    for k in list(slots):
+        if k > 1:
+            halves = (slots[k][0][:ch], slots[k][0][ch:])
+            slots[k ^ 1] = tuple(swap(v, "row", 1) for v in halves)
+    gathered = [v for k in slot_order(peers) for v in slots[k]]
+    count = len(gathered)
 
     if even:
         rows = space_rows // devices
@@ -380,13 +454,18 @@
         deep = round_up(time_rows // devices + full, 16)
         piece = (deep, LANES)
         scratch = (round_up(space_rows + 8 * period + rows, 8), LANES)
+        pieces = on_device(
+            functools.partial(space_sum_body, count, groups, rows, time_rows // devices),
+            gathered,
+            [shape((steps, *piece), F32)],
+            [pltpu.VMEM((peers, 2 * ch, 2 * cols), BF16)] + [pltpu.VMEM(scratch, F32)] * 2,
+        )
         mine, *sends = on_device(
-            functools.partial(space_sum_body, groups, rows, time_rows // devices),
-            (*gathered, kept, came),
+            functools.partial(join_body, time_rows // devices),
+            (*pieces, kept, *came),
             [shape(piece, F32)] + [shape(piece, BF16)] * (steps - 1),
-            [pltpu.VMEM((peers, 2 * ch, 2 * cols), BF16)] + [pltpu.VMEM(scratch, F32)] * 2,
-        )
-        order = sorted(range(1, steps), key=lambda k: (-k.bit_length(), k & 1, -k))
+        )
+        order = sorted(range(1, steps), key=lambda k: (k < steps // 2, k >= steps // 2 and k & 1, -k))
         arrived = [swap(sends[k - 1], "tm", k) for k in order]
         space_share, time_share = on_device(
             functools.partial(final_body, factor, len(layout)),
@@ -397,13 +476,13 @@
         time_share = time_share.reshape(-1)
     else:
         total = on_device(
-            time_sum_whole_body, (packed, after), [shape((time_rows, time_width), F32)]
+            time_sum_whole_body, (packed, far, early), [shape((time_rows, time_width), F32)]
         )[0]
         time_share = factor * lax.psum_scatter(
             total.reshape(-1), ("tm", "row"), scatter_dimension=0, tiled=True
         )
         total = on_device(
-            functools.partial(space_sum_whole_body, groups),
+            functools.partial(space_sum_whole_body, count, groups),
             gathered,
             [shape((space_rows, width), F32)],
             [pltpu.VMEM((peers, 2 * ch, 2 * cols), BF16)],
@@ -415,7 +494,7 @@
         )
 
     x1, x2, g1, g2 = on_device(
-        space_body,
+        functools.partial(space_body, count),
         (*gathered, y1, c2, x2, g1, weight_space),
         [shape(y1.shape, BF16)] * 4,
         [pltpu.VMEM((peers + 2, 2 * ch, 2 * cols), BF16)],

time: 40 us -> 38 us (0.950)
  starting transfers between devices: 25 us -> 19 us
  waiting for transfers between devices: 6.34 us -> 9.95 us
  Pallas kernels: 7.67 us -> 8.13 us
    ppermute x2, starting transfers between devices: 6.8 us -> 3.69 us  [neighbours(): lax.ppermute(x, axis, [p for i in lower for p in ((i, i + 1), (i + 1, i))])]
    ppermute x16 -> x14, starting transfers between devices: 18.2 us -> 15.3 us  [swap(): lax.ppermute(x, axis, [(i, i ^ bit) for i in range(lax.axis_size(axis))])]
    ppermute x2, waiting for transfers between devices: 1.95 us -> 4.81 us  [neighbours(): lax.ppermute(x, axis, [p for i in lower for p in ((i, i + 1), (i + 1, i))])]
    ppermute x16 -> x14, waiting for transfers between devices: 4.39 us -> 5.14 us  [swap(): lax.ppermute(x, axis, [(i, i ^ bit) for i in range(lax.axis_size(axis))])]
    pallas_call x7 -> x10, Pallas kernels: 7.67 us -> 8.13 us  [on_device(): pl.pallas_call(body, out_shape=outs, in_specs=[pl.BlockSpec(memory_space=...]
  transfers between devices with their start and end apart: 18 -> 16, of which waited for: 6 -> 9; matrix products, arithmetic and copies ran while one was open for 0% -> 0% of each run, Pallas kernels for 12% -> 15%
where the time goes in v4:
time: 38 us; the launch traced here: 37.8 us
  starting transfers between devices  19 us (50%)
  waiting for transfers between devices  9.95 us (26%)
  Pallas kernels  8.13 us (21%)
  between operations  0.76 us (2%)
    ppermute x14, starting transfers between devices, swap(): lax.ppermute(x, axis, [(i, i ^ bit) for i in range(lax.axis_size(axis))])  15.3 us
    pallas_call x10, Pallas kernels, on_device(): pl.pallas_call(body, out_shape=outs, in_specs=[pl.BlockSpec(memory_space=...  8.13 us
    ppermute x14, waiting for transfers between devices, swap(): lax.ppermute(x, axis, [(i, i ^ bit) for i in range(lax.axis_size(axis))])  5.14 us
    ppermute x2, waiting for transfers between devices, neighbours(): lax.ppermute(x, axis, [p for i in lower for p in ((i, i + 1), (i + 1, i))])  4.81 us
    ppermute x2, starting transfers between devices, neighbours(): lax.ppermute(x, axis, [p for i in lower for p in ((i, i + 1), (i + 1, i))])  3.69 us
  transfers between devices with their start and end apart: 16, of which 9 were waited for; matrix products, arithmetic and copies ran while one was open for 0% of the time, Pallas kernels for 15%

profile of v4, /device:TPU:0, one launch (start us, length us, event | category | flops | bytes accessed | tf_op | source)
XLA Modules:
  0.0 37.8 jit_solution(625966385419120966)
XLA Ops:
  0.6 1.1 %shard_map.109.own = bf16[128,640]{1,0:T(8,128)(2,1)S(1)} custom-call(bf16[2,1,64,320]{3,2,1,0:T(8,128)(2,1)} %refs_5_.1, bf16[2,1,64,320]{3,2,1,0:T(8,128)(2,1)} %refs_6_.1), custom_call_target="tpu_custom_call" | custom-call | bytes 327680 | tf_op jit(solution)/shard_map/pallas_call | solution.py:27
  1.7 3.0 %collective-permute-start = (bf16[128,640]{1,0:T(8,128)(2,1)S(1)}, bf16[128,640]{1,0:T(8,128)(2,1)S(1)}, u32[]{:S(2)}, u32[]{:S(2)}) collective-permute-start(bf16[128,640]{1,0:T(8,128)(2,1)S(1)} %shard_map.109.own), channel_id=1, source_target_pairs={{0,4},{4,0},{8,12},{12,8},{16,20},{20,16},{24,28},{28,24},{1,5},{5... | collective-permute-start | bytes 491528 | tf_op jit(solution)/shard_map/ppermute | solution.py:386
  4.8 0.7 %collective-permute-start.1 = (bf16[128,640]{1,0:T(8,128)(2,1)S(1)}, bf16[128,640]{1,0:T(8,128)(2,1)S(1)}, u32[]{:S(2)}, u32[]{:S(2)}) collective-permute-start(bf16[128,640]{1,0:T(8,128)(2,1)S(1)} %shard_map.109.own), channel_id=1, source_target_pairs={{4,8},{8,4},{12,16},{16,12},{20,24},{24,20},{5,9},{9,5},{13,17},{1... | collective-permute-start | bytes 491528 | tf_op jit(solution)/shard_map/ppermute | solution.py:386
  5.4 1.5 %shard_map.110 = (f32[64,640]{1,0:T(8,128)S(1)}, f32[64,640]{1,0:T(8,128)S(1)}, f32[64,640]{1,0:T(8,128)S(1)}, bf16[2,2,64,320]{3,2,1,0:T(8,128)(2,1)S(1)}, bf16[3,5,128,128]{3,2,1,0:T(8,128)(2,1)S(1)}) custom-call(bf16[2,1,64,320]{3,2,1,0:T(8,128)(2,1)} %refs_5_.1, bf16[2,1,64,320]{3,2,1,0:T(8,128)(2,1)} %y2_far.1, bf16[2,1,64,320]{3,2,1,0:T(8,128)(2,1)} %c1_far.1, ...), custom_call_target="tpu_custom_call" | custom-call | bytes 2048000 | tf_op jit(solution)/shard_map/pallas_call | solution.py:27
  7.0 4.8 %collective-permute-done.near = bf16[128,640]{1,0:T(8,128)(2,1)S(1)} collective-permute-done((bf16[128,640]{1,0:T(8,128)(2,1)S(1)}, bf16[128,640]{1,0:T(8,128)(2,1)S(1)}, u32[]{:S(2)}, u32[]{:S(2)}) %collective-permute-start) | collective-permute-done | bytes 163872 | tf_op jit(solution)/shard_map/ppermute | solution.py:386
  11.8 0.6 %shard_map.111 = (bf16[2,1,64,320]{3,2,1,0:T(8,128)(2,1)S(1)}, bf16[2,1,64,320]{3,2,1,0:T(8,128)(2,1)S(1)}, bf16[640,128]{1,0:T(8,128)(2,1)S(1)}) custom-call(bf16[128,640]{1,0:T(8,128)(2,1)S(1)} %collective-permute-done.near, bf16[128,640]{1,0:T(8,128)(2,1)S(1)} %collective-permute-done.1.far, f32[64,640]{1,0:T(8,128)S(1)} %get-tuple-element.45.forth0, ...), custom_call_target="tpu_custom_call" | custom-call | bytes 1802240 | tf_op jit(solution)/shard_map/pallas_call | solution.py:27
  12.4 1.6 %collective-permute-start.3 = (bf16[640,128]{1,0:T(8,128)(2,1)S(1)}, bf16[640,128]{1,0:T(8,128)(2,1)S(1)}, u32[]{:S(2)}, u32[]{:S(2)}) collective-permute-start(bf16[640,128]{1,0:T(8,128)(2,1)S(1)} %get-tuple-element.50.refs_0_), channel_id=1, source_target_pairs={{0,2},{1,3},{2,0},{3,1},{4,6},{5,7},{6,4},{7,5},{8,10},{9,11},{10,... | collective-permute-start | bytes 491528 | tf_op jit(solution)/shard_map/ppermute | solution.py:361
  14.7 0.5 %collective-permute-start.7 = (bf16[8,64,128]{2,1,0:T(8,128)(2,1)S(1)}, bf16[8,64,128]{2,1,0:T(8,128)(2,1)S(1)}, u32[]{:S(2)}, u32[]{:S(2)}) collective-permute-start(bf16[8,64,128]{2,1,0:T(8,128)(2,1)S(1)} %get-tuple-element.59), channel_id=1, source_target_pairs={{0,1},{1,0},{2,3},{3,2},{4,5},{5,4},{6,7},{7,6},{8,9},{9,8},{10,11... | collective-permute-start | bytes 393224 | tf_op jit(solution)/shard_map/ppermute | solution.py:361
  15.3 0.8 %collective-permute-done.6.refs_0_ = bf16[8,64,128]{2,1,0:T(8,128)(2,1)S(1)} collective-permute-done((bf16[8,64,128]{2,1,0:T(8,128)(2,1)S(1)}, bf16[8,64,128]{2,1,0:T(8,128)(2,1)S(1)}, u32[]{:S(2)}, u32[]{:S(2)}) %collective-permute-start.6) | collective-permute-done | bytes 131104 | tf_op jit(solution)/shard_map/ppermute | solution.py:361
  16.3 0.6 %collective-permute-start.8 = (bf16[1,8,64,128]{3,2,1,0:T(8,128)(2,1)S(1)}, bf16[1,8,64,128]{3,2,1,0:T(8,128)(2,1)S(1)}, u32[]{:S(2)}, u32[]{:S(2)}) collective-permute-start(bf16[1,8,64,128]{3,2,1,0:T(8,128)(2,1)S(1)} %get-tuple-element.61), channel_id=1, source_target_pairs={{0,2},{1,3},{2,0},{3,1},{4,6},{5,7},{6,4},{7,5},{8,10},{9,11},{10,... | collective-permute-start | bytes 393224 | tf_op jit(solution)/shard_map/ppermute | solution.py:361
  16.9 0.9 %collective-permute-done.3.refs_2_ = bf16[640,128]{1,0:T(8,128)(2,1)S(1)} collective-permute-done((bf16[640,128]{1,0:T(8,128)(2,1)S(1)}, bf16[640,128]{1,0:T(8,128)(2,1)S(1)}, u32[]{:S(2)}, u32[]{:S(2)}) %collective-permute-start.3) | collective-permute-done | bytes 163872 | tf_op jit(solution)/shard_map/ppermute | solution.py:361
  17.9 0.5 %collective-permute-start.4 = (bf16[320,128]{1,0:T(8,128)(2,1)S(1)}, bf16[320,128]{1,0:T(8,128)(2,1)S(1)}, u32[]{:S(2)}, u32[]{:S(2)}) collective-permute-start(bf16[320,128]{1,0:T(8,128)(2,1)S(1)} %get-tuple-element.73), channel_id=1, source_target_pairs={{0,1},{1,0},{2,3},{3,2},{4,5},{5,4},{6,7},{7,6},{8,9},{9,8},{10,11... | collective-permute-start | bytes 245768 | tf_op jit(solution)/shard_map/ppermute | solution.py:361
  18.4 0.8 %collective-permute-done.5.refs_4_ = bf16[320,128]{1,0:T(8,128)(2,1)S(1)} collective-permute-done((bf16[320,128]{1,0:T(8,128)(2,1)S(1)}, bf16[320,128]{1,0:T(8,128)(2,1)S(1)}, u32[]{:S(2)}, u32[]{:S(2)}) %collective-permute-start.5) | collective-permute-done | bytes 81952 | tf_op jit(solution)/shard_map/ppermute | solution.py:361
  19.3 1.3 %shard_map.113.pieces = f32[8,176,128]{2,1,0:T(8,128)S(1)} custom-call(bf16[640,128]{1,0:T(8,128)(2,1)S(1)} %get-tuple-element.50.refs_0_, bf16[640,128]{1,0:T(8,128)(2,1)S(1)} %collective-permute-done.2.refs_1_, bf16[640,128]{1,0:T(8,128)(2,1)S(1)} %collective-permute-done.3.refs_2_, bf16[320,128]{1,0:T(8,128)(2,1)S(1)} %collective-permute-done.4.refs_3_, ...), custom_call_target="tpu_custom_call" | custom-call | bytes 1376256 | tf_op jit(solution)/shard_map/pallas_call | solution.py:27
  20.6 1.5 %collective-permute-done.8.came = bf16[1,8,64,128]{3,2,1,0:T(8,128)(2,1)S(1)} collective-permute-done((bf16[1,8,64,128]{3,2,1,0:T(8,128)(2,1)S(1)}, bf16[1,8,64,128]{3,2,1,0:T(8,128)(2,1)S(1)}, u32[]{:S(2)}, u32[]{:S(2)}) %collective-permute-start.8) | collective-permute-done | bytes 131104 | tf_op jit(solution)/shard_map/ppermute | solution.py:361
  22.2 5.1 %collective-permute-start.9 = (bf16[176,128]{1,0:T(8,128)(2,1)S(1)}, bf16[176,128]{1,0:T(8,128)(2,1)S(1)}, u32[]{:S(2)}, u32[]{:S(2)}) collective-permute-start(bf16[176,128]{1,0:T(8,128)(2,1)S(1)} %get-tuple-element.63), channel_id=1, source_target_pairs={{0,24},{4,28},{8,16},{12,20},{16,8},{20,12},{24,0},{28,4},{1,25},{... | collective-permute-start | bytes 135176 | tf_op jit(solution)/shard_map/ppermute | solution.py:361
  27.2 2.4 %collective-permute-start.11 = (bf16[176,128]{1,0:T(8,128)(2,1)S(1)}, bf16[176,128]{1,0:T(8,128)(2,1)S(1)}, u32[]{:S(2)}, u32[]{:S(2)}) collective-permute-start(bf16[176,128]{1,0:T(8,128)(2,1)S(1)} %get-tuple-element.65), channel_id=1, source_target_pairs={{0,28},{4,24},{8,20},{12,16},{16,12},{20,8},{24,4},{28,0},{1,29},{... | collective-permute-start | bytes 135176 | tf_op jit(solution)/shard_map/ppermute | solution.py:361
  29.6 0.6 %collective-permute-start.12 = (bf16[176,128]{1,0:T(8,128)(2,1)S(1)}, bf16[176,128]{1,0:T(8,128)(2,1)S(1)}, u32[]{:S(2)}, u32[]{:S(2)}) collective-permute-start(bf16[176,128]{1,0:T(8,128)(2,1)S(1)} %get-tuple-element.66), channel_id=1, source_target_pairs={{0,20},{4,16},{8,28},{12,24},{16,4},{20,0},{24,12},{28,8},{1,21},{... | collective-permute-start | bytes 135176 | tf_op jit(solution)/shard_map/ppermute | solution.py:361
  30.3 2.2 %collective-permute-start.13 = (bf16[176,128]{1,0:T(8,128)(2,1)S(1)}, bf16[176,128]{1,0:T(8,128)(2,1)S(1)}, u32[]{:S(2)}, u32[]{:S(2)}) collective-permute-start(bf16[176,128]{1,0:T(8,128)(2,1)S(1)} %get-tuple-element.67), channel_id=1, source_target_pairs={{0,12},{4,8},{8,4},{12,0},{16,28},{20,24},{24,20},{28,16},{1,13},{... | collective-permute-start | bytes 135176 | tf_op jit(solution)/shard_map/ppermute | solution.py:361
  32.4 0.7 %collective-permute-start.14 = (bf16[176,128]{1,0:T(8,128)(2,1)S(1)}, bf16[176,128]{1,0:T(8,128)(2,1)S(1)}, u32[]{:S(2)}, u32[]{:S(2)}) collective-permute-start(bf16[176,128]{1,0:T(8,128)(2,1)S(1)} %get-tuple-element.68), channel_id=1, source_target_pairs={{0,8},{4,12},{8,0},{12,4},{16,24},{20,28},{24,16},{28,20},{1,9},{5... | collective-permute-start | bytes 135176 | tf_op jit(solution)/shard_map/ppermute | solution.py:361
  33.1 1.0 %collective-permute-start.15 = (bf16[176,128]{1,0:T(8,128)(2,1)S(1)}, bf16[176,128]{1,0:T(8,128)(2,1)S(1)}, u32[]{:S(2)}, u32[]{:S(2)}) collective-permute-start(bf16[176,128]{1,0:T(8,128)(2,1)S(1)} %get-tuple-element.69), channel_id=1, source_target_pairs={{0,4},{4,0},{8,12},{12,8},{16,20},{20,16},{24,28},{28,24},{1,5},{5... | collective-permute-start | bytes 135176 | tf_op jit(solution)/shard_map/ppermute | solution.py:361
  34.1 2.2 %shard_map.112 = (bf16[2,1,64,320]{3,2,1,0:T(8,128)(2,1)}, bf16[2,1,64,320]{3,2,1,0:T(8,128)(2,1)}, bf16[2,1,64,320]{3,2,1,0:T(8,128)(2,1)}, bf16[2,1,64,320]{3,2,1,0:T(8,128)(2,1)}) custom-call(bf16[640,128]{1,0:T(8,128)(2,1)S(1)} %get-tuple-element.50.refs_0_, bf16[640,128]{1,0:T(8,128)(2,1)S(1)} %collective-permute-done.2.refs_1_, ...), custom_call_target="tpu_custom_call" | custom-call | bytes 2232320 | tf_op jit(solution)/shard_map/pallas_call | solution.py:27
  36.5 0.7 %collective-permute-done.15.refs_7_ = bf16[176,128]{1,0:T(8,128)(2,1)S(1)} collective-permute-done((bf16[176,128]{1,0:T(8,128)(2,1)S(1)}, bf16[176,128]{1,0:T(8,128)(2,1)S(1)}, u32[]{:S(2)}, u32[]{:S(2)}) %collective-permute-start.15) | collective-permute-done | bytes 45088 | tf_op jit(solution)/shard_map/ppermute | solution.py:361
  37.2 0.7 %shard_map.118 = (f32[115,128]{1,0:T(8,128)}, f32[60,128]{1,0:T(8,128)}) custom-call(f32[176,128]{1,0:T(8,128)S(1)} %get-tuple-element.62.refs_0_, bf16[176,128]{1,0:T(8,128)(2,1)S(1)} %collective-permute-done.9.refs_1_, bf16[176,128]{1,0:T(8,128)(2,1)S(1)} %collective-permute-done.10.refs_2_, bf16[176,128]{1,0:T(8,128)(2,1)S(1)} %collective-permute-done.11.refs_3_, ...), custom_call_target="tpu_custom_call" | custom-call | bytes 495104 | tf_op jit(solution)/shard_map/pallas_call | solution.py:27
  (25 shorter events, 1.6 us)
Async XLA Ops:
  1.7 10.0 %collective-permute-start = (bf16[128,640]{1,0:T(8,128)(2,1)S(1)}, bf16[128,640]{1,0:T(8,128)(2,1)S(1)}, u32[]{:S(2)}, u32[]{:S(2)}) collective-permute-start(bf16[128,640]{1,0:T(8,128)(2,1)S(1)} %shard_map.109.own), channel_id=1, source_target_pairs={{0,4},{4,0},{8,12},{12,8},{16,20},{20,16},{24,28},{28,24},{1,5},{5... | collective-permute-start | bytes 491528 | tf_op jit(solution)/shard_map/ppermute | solution.py:386
  4.8 7.0 %collective-permute-start.1 = (bf16[128,640]{1,0:T(8,128)(2,1)S(1)}, bf16[128,640]{1,0:T(8,128)(2,1)S(1)}, u32[]{:S(2)}, u32[]{:S(2)}) collective-permute-start(bf16[128,640]{1,0:T(8,128)(2,1)S(1)} %shard_map.109.own), channel_id=1, source_target_pairs={{4,8},{8,4},{12,16},{16,12},{20,24},{24,20},{5,9},{9,5},{13,17},{1... | collective-permute-start | bytes 491528 | tf_op jit(solution)/shard_map/ppermute | solution.py:386
  12.4 5.4 %collective-permute-start.3 = (bf16[640,128]{1,0:T(8,128)(2,1)S(1)}, bf16[640,128]{1,0:T(8,128)(2,1)S(1)}, u32[]{:S(2)}, u32[]{:S(2)}) collective-permute-start(bf16[640,128]{1,0:T(8,128)(2,1)S(1)} %get-tuple-element.50.refs_0_), channel_id=1, source_target_pairs={{0,2},{1,3},{2,0},{3,1},{4,6},{5,7},{6,4},{7,5},{8,10},{9,11},{10,... | collective-permute-start | bytes 491528 | tf_op jit(solution)/shard_map/ppermute | solution.py:361
  14.6 1.4 %collective-permute-start.6 = (bf16[8,64,128]{2,1,0:T(8,128)(2,1)S(1)}, bf16[8,64,128]{2,1,0:T(8,128)(2,1)S(1)}, u32[]{:S(2)}, u32[]{:S(2)}) collective-permute-start(bf16[8,64,128]{2,1,0:T(8,128)(2,1)S(1)} %get-tuple-element.58), channel_id=1, source_target_pairs={{0,1},{1,0},{2,3},{3,2},{4,5},{5,4},{6,7},{7,6},{8,9},{9,8},{10,11... | collective-permute-start | bytes 393224 | tf_op jit(solution)/shard_map/ppermute | solution.py:361
  14.7 1.5 %collective-permute-start.7 = (bf16[8,64,128]{2,1,0:T(8,128)(2,1)S(1)}, bf16[8,64,128]{2,1,0:T(8,128)(2,1)S(1)}, u32[]{:S(2)}, u32[]{:S(2)}) collective-permute-start(bf16[8,64,128]{2,1,0:T(8,128)(2,1)S(1)} %get-tuple-element.59), channel_id=1, source_target_pairs={{0,1},{1,0},{2,3},{3,2},{4,5},{5,4},{6,7},{7,6},{8,9},{9,8},{10,11... | collective-permute-start | bytes 393224 | tf_op jit(solution)/shard_map/ppermute | solution.py:361
  15.2 3.2 %collective-permute-start.2 = (bf16[640,128]{1,0:T(8,128)(2,1)S(1)}, bf16[640,128]{1,0:T(8,128)(2,1)S(1)}, u32[]{:S(2)}, u32[]{:S(2)}) collective-permute-start(bf16[640,128]{1,0:T(8,128)(2,1)S(1)} %get-tuple-element.50.refs_0_), channel_id=1, source_target_pairs={{0,1},{1,0},{2,3},{3,2},{4,5},{5,4},{6,7},{7,6},{8,9},{9,8},{10,11... | collective-permute-start | bytes 491528 | tf_op jit(solution)/shard_map/ppermute | solution.py:361
  16.3 17.8 %copy-start = (bf16[3,3,2,160,160]{4,3,2,1,0:T(8,128)(2,1)S(1)}, bf16[3,3,2,160,160]{4,3,2,1,0:T(8,128)(2,1)}, u32[]{:S(2)}) copy-start(bf16[3,3,2,160,160]{4,3,2,1,0:T(8,128)(2,1)} %refs_9_.1) | copy-start | bytes 2764804
  16.3 17.8 %copy-start.1 = (bf16[2,1,64,320]{3,2,1,0:T(8,128)(2,1)S(1)}, bf16[2,1,64,320]{3,2,1,0:T(8,128)(2,1)}, u32[]{:S(2)}) copy-start(bf16[2,1,64,320]{3,2,1,0:T(8,128)(2,1)} %refs_5_.1) | copy-start | bytes 245764
  16.3 17.8 %copy-start.2 = (bf16[2,1,64,320]{3,2,1,0:T(8,128)(2,1)S(1)}, bf16[2,1,64,320]{3,2,1,0:T(8,128)(2,1)}, u32[]{:S(2)}) copy-start(bf16[2,1,64,320]{3,2,1,0:T(8,128)(2,1)} %refs_6_.1) | copy-start | bytes 245764
  16.3 5.8 %collective-permute-start.8 = (bf16[1,8,64,128]{3,2,1,0:T(8,128)(2,1)S(1)}, bf16[1,8,64,128]{3,2,1,0:T(8,128)(2,1)S(1)}, u32[]{:S(2)}, u32[]{:S(2)}) collective-permute-start(bf16[1,8,64,128]{3,2,1,0:T(8,128)(2,1)S(1)} %get-tuple-element.61), channel_id=1, source_target_pairs={{0,2},{1,3},{2,0},{3,1},{4,6},{5,7},{6,4},{7,5},{8,10},{9,11},{10,... | collective-permute-start | bytes 393224 | tf_op jit(solution)/shard_map/ppermute | solution.py:361
  17.8 1.3 %collective-permute-start.5 = (bf16[320,128]{1,0:T(8,128)(2,1)S(1)}, bf16[320,128]{1,0:T(8,128)(2,1)S(1)}, u32[]{:S(2)}, u32[]{:S(2)}) collective-permute-start(bf16[320,128]{1,0:T(8,128)(2,1)S(1)} %get-tuple-element.72), channel_id=1, source_target_pairs={{0,1},{1,0},{2,3},{3,2},{4,5},{5,4},{6,7},{7,6},{8,9},{9,8},{10,11... | collective-permute-start | bytes 245768 | tf_op jit(solution)/shard_map/ppermute | solution.py:361
  17.9 1.4 %collective-permute-start.4 = (bf16[320,128]{1,0:T(8,128)(2,1)S(1)}, bf16[320,128]{1,0:T(8,128)(2,1)S(1)}, u32[]{:S(2)}, u32[]{:S(2)}) collective-permute-start(bf16[320,128]{1,0:T(8,128)(2,1)S(1)} %get-tuple-element.73), channel_id=1, source_target_pairs={{0,1},{1,0},{2,3},{3,2},{4,5},{5,4},{6,7},{7,6},{8,9},{9,8},{10,11... | collective-permute-start | bytes 245768 | tf_op jit(solution)/shard_map/ppermute | solution.py:361
  22.2 10.3 %collective-permute-start.9 = (bf16[176,128]{1,0:T(8,128)(2,1)S(1)}, bf16[176,128]{1,0:T(8,128)(2,1)S(1)}, u32[]{:S(2)}, u32[]{:S(2)}) collective-permute-start(bf16[176,128]{1,0:T(8,128)(2,1)S(1)} %get-tuple-element.63), channel_id=1, source_target_pairs={{0,24},{4,28},{8,16},{12,20},{16,8},{20,12},{24,0},{28,4},{1,25},{... | collective-permute-start | bytes 135176 | tf_op jit(solution)/shard_map/ppermute | solution.py:361
  27.2 5.9 %collective-permute-start.10 = (bf16[176,128]{1,0:T(8,128)(2,1)S(1)}, bf16[176,128]{1,0:T(8,128)(2,1)S(1)}, u32[]{:S(2)}, u32[]{:S(2)}) collective-permute-start(bf16[176,128]{1,0:T(8,128)(2,1)S(1)} %get-tuple-element.64), channel_id=1, source_target_pairs={{0,16},{4,20},{8,24},{12,28},{16,0},{20,4},{24,8},{28,12},{1,17},{... | collective-permute-start | bytes 135176 | tf_op jit(solution)/shard_map/ppermute | solution.py:361
  27.2 9.0 %collective-permute-start.11 = (bf16[176,128]{1,0:T(8,128)(2,1)S(1)}, bf16[176,128]{1,0:T(8,128)(2,1)S(1)}, u32[]{:S(2)}, u32[]{:S(2)}) collective-permute-start(bf16[176,128]{1,0:T(8,128)(2,1)S(1)} %get-tuple-element.65), channel_id=1, source_target_pairs={{0,28},{4,24},{8,20},{12,16},{16,12},{20,8},{24,4},{28,0},{1,29},{... | collective-permute-start | bytes 135176 | tf_op jit(solution)/shard_map/ppermute | solution.py:361
  29.6 6.6 %collective-permute-start.12 = (bf16[176,128]{1,0:T(8,128)(2,1)S(1)}, bf16[176,128]{1,0:T(8,128)(2,1)S(1)}, u32[]{:S(2)}, u32[]{:S(2)}) collective-permute-start(bf16[176,128]{1,0:T(8,128)(2,1)S(1)} %get-tuple-element.66), channel_id=1, source_target_pairs={{0,20},{4,16},{8,28},{12,24},{16,4},{20,0},{24,12},{28,8},{1,21},{... | collective-permute-start | bytes 135176 | tf_op jit(solution)/shard_map/ppermute | solution.py:361
  30.3 6.0 %collective-permute-start.13 = (bf16[176,128]{1,0:T(8,128)(2,1)S(1)}, bf16[176,128]{1,0:T(8,128)(2,1)S(1)}, u32[]{:S(2)}, u32[]{:S(2)}) collective-permute-start(bf16[176,128]{1,0:T(8,128)(2,1)S(1)} %get-tuple-element.67), channel_id=1, source_target_pairs={{0,12},{4,8},{8,4},{12,0},{16,28},{20,24},{24,20},{28,16},{1,13},{... | collective-permute-start | bytes 135176 | tf_op jit(solution)/shard_map/ppermute | solution.py:361
  32.4 4.0 %collective-permute-start.14 = (bf16[176,128]{1,0:T(8,128)(2,1)S(1)}, bf16[176,128]{1,0:T(8,128)(2,1)S(1)}, u32[]{:S(2)}, u32[]{:S(2)}) collective-permute-start(bf16[176,128]{1,0:T(8,128)(2,1)S(1)} %get-tuple-element.68), channel_id=1, source_target_pairs={{0,8},{4,12},{8,0},{12,4},{16,24},{20,28},{24,16},{28,20},{1,9},{5... | collective-permute-start | bytes 135176 | tf_op jit(solution)/shard_map/ppermute | solution.py:361
  33.1 4.0 %collective-permute-start.15 = (bf16[176,128]{1,0:T(8,128)(2,1)S(1)}, bf16[176,128]{1,0:T(8,128)(2,1)S(1)}, u32[]{:S(2)}, u32[]{:S(2)}) collective-permute-start(bf16[176,128]{1,0:T(8,128)(2,1)S(1)} %get-tuple-element.69), channel_id=1, source_target_pairs={{0,4},{4,0},{8,12},{12,8},{16,20},{20,16},{24,28},{28,24},{1,5},{5... | collective-permute-start | bytes 135176 | tf_op jit(solution)/shard_map/ppermute | solution.py:361

commit v5 on v4

--- a/solution.py
+++ b/solution.py
@@ -146,9 +146,27 @@
     return jnp.where(lax.axis_index("tm") % 2 == 0, 0, 2)
 
 
-def time_near_body(own, near, total):
+def time_near_body(near, *refs):
+    owns, total = refs[:-1], refs[-1]
+    cols = near.shape[0] // 2
+    width = total.shape[1]
+    groups = near.shape[1] // width
     total[...] = jnp.zeros_like(total)
-    time_terms(own, ((1, own), (near_tap(), near)), total)
+    time_terms(owns[0], ((near_tap(), near),), total)
+    act = jnp.concatenate([v[:cols] for v in owns], axis=0).astype(F32).T.astype(BF16)
+    cot = jnp.concatenate([v[cols:] for v in owns], axis=0)
+    for q in range(groups):
+        part = slice(q * width, (q + 1) * width)
+        total[pl.ds((groups + q) * width, width), :] = dot(act[part], cot[:, part], 1, 0)
+
+
+def outer_steps(steps, peers, taps, rows):
+    size = steps * peers * rows // taps
+    return [
+        t
+        for t in range(steps)
+        if t * peers * rows < size or (t + 1) * peers * rows > (taps - 1) * size
+    ]
 
 
 def time_sum_body(offsets, rows, own, far, early, keep, *refs):
@@ -156,14 +174,15 @@
     total[: early.shape[0]] = early[...]
     time_terms(own, ((2 - near_tap(), far),), total)
     me, peers, steps = lax.axis_index("row"), lax.axis_size("row"), lax.axis_size("tm")
-    held, size = keep.shape[2], sends[0].shape[0]
+    held, third = keep.shape[2], early.shape[0] // 3
     for u, offset in enumerate(offsets):
-        for t in range(steps):
+        if u == 1:
+            total[third : 2 * third] = jnp.zeros((third, total.shape[1]), F32)
+        for i, t in enumerate(range(steps) if u == 0 else outer_steps(steps, peers, 3, rows)):
             mine = (t * peers + (me ^ offset)) * rows
             other = (t * peers + (me ^ offset ^ 1)) * rows
-            keep[u, t] = total[pl.ds(mine, held), :]
-            part = sends[(u * steps + t) // size]
-            part[t % size] = total[pl.ds(other, held), :].astype(BF16)
+            keep[u, i] = total[pl.ds(mine, held), :]
+            sends[u][i] = total[pl.ds(other, held), :].astype(BF16)
 
 
 def time_sum_whole_body(own, far, early, total):
@@ -171,17 +190,9 @@
     time_terms(own, ((2 - near_tap(), far),), total)
 
 
-def fold_body(kept, *refs):
-    *came, keep, send = refs
-    steps, size = kept.shape[1], came[0].shape[0]
-    half = keep.shape[0]
-    for i, ref in enumerate(came):
-        u, t = divmod(i * size, steps)
-        total = kept[u, t : t + size] + ref[...].astype(F32)
-        if u < half:
-            keep[u, t : t + size] = total
-        else:
-            send[u - half, t : t + size] = total.astype(BF16)
+def fold_body(kept, own_came, other_came, keep, send):
+    keep[...] = kept[0] + own_came[...].astype(F32)
+    send[...] = (kept[1, : send.shape[0]] + other_came[...].astype(F32)).astype(BF16)
 
 
 def place(slots, rows_ref, lead):
@@ -282,13 +293,19 @@
         out[k] = jnp.concatenate(parts, axis=0)
 
 
-def join_body(time_rows, pieces, kept, came, mine, *sends):
-    tall = kept.shape[2]
+def join_body(time_rows, outer, pieces, kept, came, mine, *sends):
+    tall, steps = kept.shape[1], kept.shape[0]
     row = lax.broadcasted_iota(jnp.int32, (tall, LANES), 0)
+    gap = steps - len(outer)
     for k in range(pieces.shape[0]):
         t = lax.axis_index("tm") ^ k
-        terms = jnp.where(row < time_rows, kept[0, t] + came[0, t].astype(F32), 0.0)
-        piece = jnp.concatenate([pieces[k, :tall] + terms, pieces[k, tall:]], axis=0)
+        first = next((i for i, v in enumerate(outer) if v != i), len(outer))
+        over = t >= first + gap
+        sent = jnp.logical_or(t < first, over)
+        terms = came[jnp.where(over, t - gap, jnp.minimum(t, len(outer) - 1))].astype(F32)
+        terms = kept[t] + jnp.where(sent, terms, 0.0)
+        head = pieces[k, :tall] + jnp.where(row < time_rows, terms, 0.0)
+        piece = jnp.concatenate([head, pieces[k, tall:]], axis=0)
         if k == 0:
             mine[...] = piece
         else:
@@ -409,30 +426,28 @@
         far=4,
     )
 
-    even = time_rows % devices == 0 and space_rows % devices == 0
+    near, centre = lax.optimization_barrier((near, centre))
     bits = [1 << i for i in range(peers.bit_length() - 1)]
-    near, centre = lax.optimization_barrier((near, centre))
-    early = on_device(time_near_body, (packed, near), [shape((time_rows, time_width), F32)])[0]
+    even = time_rows % devices == 0 and space_rows % devices == 0 and peers == 4
+    owns = gather(packed, "row", bits[1:]) if even else {0: packed}
+    owns = [owns[k] for k in sorted(owns)]
+    early = on_device(time_near_body, (near, *owns), [shape((time_rows, time_width), F32)])[0]
     if even:
         rows = time_rows // devices
         tall = round_up(rows, 16)
         offsets = row_offsets(bits[1:])
-        block = (len(offsets), steps, tall, time_width)
-        pieces = len(offsets)
-        share = (len(offsets) * steps // pieces, *block[2:])
+        block = (steps, tall, time_width)
+        outer = outer_steps(steps, peers, 3, rows)
+        rest = (len(outer), *block[1:])
         kept, *sent = on_device(
             functools.partial(time_sum_body, offsets, rows),
             (packed, far, early),
-            [shape(block, F32)] + [shape(share, BF16)] * pieces,
+            [shape((2, *block), F32), shape(block, BF16), shape(rest, BF16)],
             [pltpu.VMEM((round_up(time_rows + tall, 8), time_width), F32)],
         )
         came = [swap(v, "row", 1) for v in sent]
-        for bit in bits[1:]:
-            block = (block[0] // 2, *block[1:])
-            kept, sent = on_device(
-                fold_body, (kept, *came), [shape(block, F32), shape(block, BF16)]
-            )
-            came = [swap(sent, "row", bit)]
+        kept, sent = on_device(fold_body, (kept, *came), [shape(block, F32), shape(rest, BF16)])
+        came = [swap(sent, "row", bits[1])]
     x2, g1, held = on_device(
         time_body,
         (near, far, *centre),
@@ -461,7 +476,7 @@
             [pltpu.VMEM((peers, 2 * ch, 2 * cols), BF16)] + [pltpu.VMEM(scratch, F32)] * 2,
         )
         mine, *sends = on_device(
-            functools.partial(join_body, time_rows // devices),
+            functools.partial(join_body, time_rows // devices, outer),
             (*pieces, kept, *came),
             [shape(piece, F32)] + [shape(piece, BF16)] * (steps - 1),
         )

time: 38 us -> 37.4 us (0.984)
  waiting for transfers between devices: 9.95 us -> 7.77 us
  starting transfers between devices: 19 us -> 20.5 us
    ppermute x2, waiting for transfers between devices: 4.81 us -> 3.26 us  [neighbours(): lax.ppermute(x, axis, [p for i in lower for p in ((i, i + 1), (i + 1, i))])]
    ppermute x14 -> x15, starting transfers between devices: 15.3 us -> 16.8 us  [swap(): lax.ppermute(x, axis, [(i, i ^ bit) for i in range(lax.axis_size(axis))])]
    ppermute x14 -> x15, waiting for transfers between devices: 5.14 us -> 4.52 us  [swap(): lax.ppermute(x, axis, [(i, i ^ bit) for i in range(lax.axis_size(axis))])]
  transfers between devices with their start and end apart: 16 -> 17, of which waited for: 9 -> 9; matrix products, arithmetic and copies ran while one was open for 0% -> 0% of each run, Pallas kernels for 15% -> 17%
where the time goes in v5:
time: 37.4 us; the launch traced here: 37.2 us
  starting transfers between devices  20.5 us (55%)
  Pallas kernels  8.17 us (22%)
  waiting for transfers between devices  7.77 us (21%)
  between operations  0.75 us (2%)
    ppermute x15, starting transfers between devices, swap(): lax.ppermute(x, axis, [(i, i ^ bit) for i in range(lax.axis_size(axis))])  16.8 us
    pallas_call x10, Pallas kernels, on_device(): pl.pallas_call(body, out_shape=outs, in_specs=[pl.BlockSpec(memory_space=...  8.17 us
    ppermute x15, waiting for transfers between devices, swap(): lax.ppermute(x, axis, [(i, i ^ bit) for i in range(lax.axis_size(axis))])  4.52 us
    ppermute x2, starting transfers between devices, neighbours(): lax.ppermute(x, axis, [p for i in lower for p in ((i, i + 1), (i + 1, i))])  3.69 us
    ppermute x2, waiting for transfers between devices, neighbours(): lax.ppermute(x, axis, [p for i in lower for p in ((i, i + 1), (i + 1, i))])  3.26 us
  transfers between devices with their start and end apart: 17, of which 9 were waited for; matrix products, arithmetic and copies ran while one was open for 0% of the time, Pallas kernels for 17%

profile of v5, /device:TPU:0, one launch (start us, length us, event | category | flops | bytes accessed | tf_op | source)
XLA Modules:
  0.0 37.2 jit_solution(3356065640875539730)
XLA Ops:
  0.6 1.1 %shard_map.109.own.refs_0_ = bf16[128,640]{1,0:T(8,128)(2,1)S(1)} custom-call(bf16[2,1,64,320]{3,2,1,0:T(8,128)(2,1)} %refs_5_.1, bf16[2,1,64,320]{3,2,1,0:T(8,128)(2,1)} %refs_6_.1), custom_call_target="tpu_custom_call" | custom-call | bytes 327680 | tf_op jit(solution)/shard_map/pallas_call | solution.py:27
  1.7 3.0 %collective-permute-start = (bf16[128,640]{1,0:T(8,128)(2,1)S(1)}, bf16[128,640]{1,0:T(8,128)(2,1)S(1)}, u32[]{:S(2)}, u32[]{:S(2)}) collective-permute-start(bf16[128,640]{1,0:T(8,128)(2,1)S(1)} %shard_map.109.own.refs_0_), channel_id=1, source_target_pairs={{0,4},{4,0},{8,12},{12,8},{16,20},{20,16},{24,28},{28,24},{1,5},{5... | collective-permute-start | bytes 491528 | tf_op jit(solution)/shard_map/ppermute | solution.py:403
  4.8 0.7 %collective-permute-start.1 = (bf16[128,640]{1,0:T(8,128)(2,1)S(1)}, bf16[128,640]{1,0:T(8,128)(2,1)S(1)}, u32[]{:S(2)}, u32[]{:S(2)}) collective-permute-start(bf16[128,640]{1,0:T(8,128)(2,1)S(1)} %shard_map.109.own.refs_0_), channel_id=1, source_target_pairs={{4,8},{8,4},{12,16},{16,12},{20,24},{24,20},{5,9},{9,5},{13,17},{1... | collective-permute-start | bytes 491528 | tf_op jit(solution)/shard_map/ppermute | solution.py:403
  5.4 1.6 %collective-permute-start.6 = (bf16[128,640]{1,0:T(8,128)(2,1)S(1)}, bf16[128,640]{1,0:T(8,128)(2,1)S(1)}, u32[]{:S(2)}, u32[]{:S(2)}) collective-permute-start(bf16[128,640]{1,0:T(8,128)(2,1)S(1)} %shard_map.109.own.refs_0_), channel_id=1, source_target_pairs={{0,2},{1,3},{2,0},{3,1},{4,6},{5,7},{6,4},{7,5},{8,10},{9,11},{10,... | collective-permute-start | bytes 491528 | tf_op jit(solution)/shard_map/ppermute | solution.py:378
  7.0 1.5 %shard_map.110 = (f32[64,640]{1,0:T(8,128)S(1)}, f32[64,640]{1,0:T(8,128)S(1)}, f32[64,640]{1,0:T(8,128)S(1)}, bf16[2,2,64,320]{3,2,1,0:T(8,128)(2,1)S(1)}, bf16[3,5,128,128]{3,2,1,0:T(8,128)(2,1)S(1)}) custom-call(bf16[2,1,64,320]{3,2,1,0:T(8,128)(2,1)} %refs_5_.1, bf16[2,1,64,320]{3,2,1,0:T(8,128)(2,1)} %y2_far.1, bf16[2,1,64,320]{3,2,1,0:T(8,128)(2,1)} %c1_far.1, ...), custom_call_target="tpu_custom_call" | custom-call | bytes 2048000 | tf_op jit(solution)/shard_map/pallas_call | solution.py:27
  8.5 3.3 %collective-permute-done.near = bf16[128,640]{1,0:T(8,128)(2,1)S(1)} collective-permute-done((bf16[128,640]{1,0:T(8,128)(2,1)S(1)}, bf16[128,640]{1,0:T(8,128)(2,1)S(1)}, u32[]{:S(2)}, u32[]{:S(2)}) %collective-permute-start) | collective-permute-done | bytes 163872 | tf_op jit(solution)/shard_map/ppermute | solution.py:403
  11.8 0.6 %shard_map.111 = (bf16[2,1,64,320]{3,2,1,0:T(8,128)(2,1)S(1)}, bf16[2,1,64,320]{3,2,1,0:T(8,128)(2,1)S(1)}, bf16[640,128]{1,0:T(8,128)(2,1)S(1)}) custom-call(bf16[128,640]{1,0:T(8,128)(2,1)S(1)} %collective-permute-done.near, bf16[128,640]{1,0:T(8,128)(2,1)S(1)} %collective-permute-done.1.far, f32[64,640]{1,0:T(8,128)S(1)} %get-tuple-element.45.forth0, ...), custom_call_target="tpu_custom_call" | custom-call | bytes 1802240 | tf_op jit(solution)/shard_map/pallas_call | solution.py:27
  12.4 1.6 %collective-permute-start.3 = (bf16[640,128]{1,0:T(8,128)(2,1)S(1)}, bf16[640,128]{1,0:T(8,128)(2,1)S(1)}, u32[]{:S(2)}, u32[]{:S(2)}) collective-permute-start(bf16[640,128]{1,0:T(8,128)(2,1)S(1)} %get-tuple-element.50.refs_0_), channel_id=1, source_target_pairs={{0,2},{1,3},{2,0},{3,1},{4,6},{5,7},{6,4},{7,5},{8,10},{9,11},{10,... | collective-permute-start | bytes 491528 | tf_op jit(solution)/shard_map/ppermute | solution.py:378
  14.7 0.5 %collective-permute-start.8 = (bf16[6,64,128]{2,1,0:T(8,128)(2,1)S(1)}, bf16[6,64,128]{2,1,0:T(8,128)(2,1)S(1)}, u32[]{:S(2)}, u32[]{:S(2)}) collective-permute-start(bf16[6,64,128]{2,1,0:T(8,128)(2,1)S(1)} %get-tuple-element.59), channel_id=1, source_target_pairs={{0,1},{1,0},{2,3},{3,2},{4,5},{5,4},{6,7},{7,6},{8,9},{9,8},{10,11... | collective-permute-start | bytes 294920 | tf_op jit(solution)/shard_map/ppermute | solution.py:378
  15.3 0.9 %collective-permute-done.8.other_came = bf16[6,64,128]{2,1,0:T(8,128)(2,1)S(1)} collective-permute-done((bf16[6,64,128]{2,1,0:T(8,128)(2,1)S(1)}, bf16[6,64,128]{2,1,0:T(8,128)(2,1)S(1)}, u32[]{:S(2)}, u32[]{:S(2)}) %collective-permute-start.8) | collective-permute-done | bytes 98336 | tf_op jit(solution)/shard_map/ppermute | solution.py:378
  16.3 0.6 %collective-permute-start.9 = (bf16[6,64,128]{2,1,0:T(8,128)(2,1)S(1)}, bf16[6,64,128]{2,1,0:T(8,128)(2,1)S(1)}, u32[]{:S(2)}, u32[]{:S(2)}) collective-permute-start(bf16[6,64,128]{2,1,0:T(8,128)(2,1)S(1)} %get-tuple-element.61), channel_id=1, source_target_pairs={{0,2},{1,3},{2,0},{3,1},{4,6},{5,7},{6,4},{7,5},{8,10},{9,11},{10,... | collective-permute-start | bytes 294920 | tf_op jit(solution)/shard_map/ppermute | solution.py:378
  16.9 0.9 %collective-permute-done.3.refs_2_ = bf16[640,128]{1,0:T(8,128)(2,1)S(1)} collective-permute-done((bf16[640,128]{1,0:T(8,128)(2,1)S(1)}, bf16[640,128]{1,0:T(8,128)(2,1)S(1)}, u32[]{:S(2)}, u32[]{:S(2)}) %collective-permute-start.3) | collective-permute-done | bytes 163872 | tf_op jit(solution)/shard_map/ppermute | solution.py:378
  18.4 0.8 %collective-permute-done.5.refs_4_ = bf16[320,128]{1,0:T(8,128)(2,1)S(1)} collective-permute-done((bf16[320,128]{1,0:T(8,128)(2,1)S(1)}, bf16[320,128]{1,0:T(8,128)(2,1)S(1)}, u32[]{:S(2)}, u32[]{:S(2)}) %collective-permute-start.5) | collective-permute-done | bytes 81952 | tf_op jit(solution)/shard_map/ppermute | solution.py:378
  19.3 1.3 %shard_map.113.pieces = f32[8,176,128]{2,1,0:T(8,128)S(1)} custom-call(bf16[640,128]{1,0:T(8,128)(2,1)S(1)} %get-tuple-element.50.refs_0_, bf16[640,128]{1,0:T(8,128)(2,1)S(1)} %collective-permute-done.2.refs_1_, bf16[640,128]{1,0:T(8,128)(2,1)S(1)} %collective-permute-done.3.refs_2_, bf16[320,128]{1,0:T(8,128)(2,1)S(1)} %collective-permute-done.4.refs_3_, ...), custom_call_target="tpu_custom_call" | custom-call | bytes 1376256 | tf_op jit(solution)/shard_map/pallas_call | solution.py:27
  20.6 0.8 %collective-permute-done.9.came = bf16[6,64,128]{2,1,0:T(8,128)(2,1)S(1)} collective-permute-done((bf16[6,64,128]{2,1,0:T(8,128)(2,1)S(1)}, bf16[6,64,128]{2,1,0:T(8,128)(2,1)S(1)}, u32[]{:S(2)}, u32[]{:S(2)}) %collective-permute-start.9) | collective-permute-done | bytes 98336 | tf_op jit(solution)/shard_map/ppermute | solution.py:378
  21.4 5.1 %collective-permute-start.10 = (bf16[176,128]{1,0:T(8,128)(2,1)S(1)}, bf16[176,128]{1,0:T(8,128)(2,1)S(1)}, u32[]{:S(2)}, u32[]{:S(2)}) collective-permute-start(bf16[176,128]{1,0:T(8,128)(2,1)S(1)} %get-tuple-element.63), channel_id=1, source_target_pairs={{0,24},{4,28},{8,16},{12,20},{16,8},{20,12},{24,0},{28,4},{1,25},{... | collective-permute-start | bytes 135176 | tf_op jit(solution)/shard_map/ppermute | solution.py:378
  26.5 2.4 %collective-permute-start.12 = (bf16[176,128]{1,0:T(8,128)(2,1)S(1)}, bf16[176,128]{1,0:T(8,128)(2,1)S(1)}, u32[]{:S(2)}, u32[]{:S(2)}) collective-permute-start(bf16[176,128]{1,0:T(8,128)(2,1)S(1)} %get-tuple-element.65), channel_id=1, source_target_pairs={{0,28},{4,24},{8,20},{12,16},{16,12},{20,8},{24,4},{28,0},{1,29},{... | collective-permute-start | bytes 135176 | tf_op jit(solution)/shard_map/ppermute | solution.py:378
  28.9 0.6 %collective-permute-start.13 = (bf16[176,128]{1,0:T(8,128)(2,1)S(1)}, bf16[176,128]{1,0:T(8,128)(2,1)S(1)}, u32[]{:S(2)}, u32[]{:S(2)}) collective-permute-start(bf16[176,128]{1,0:T(8,128)(2,1)S(1)} %get-tuple-element.66), channel_id=1, source_target_pairs={{0,20},{4,16},{8,28},{12,24},{16,4},{20,0},{24,12},{28,8},{1,21},{... | collective-permute-start | bytes 135176 | tf_op jit(solution)/shard_map/ppermute | solution.py:378
  29.5 2.2 %collective-permute-start.14 = (bf16[176,128]{1,0:T(8,128)(2,1)S(1)}, bf16[176,128]{1,0:T(8,128)(2,1)S(1)}, u32[]{:S(2)}, u32[]{:S(2)}) collective-permute-start(bf16[176,128]{1,0:T(8,128)(2,1)S(1)} %get-tuple-element.67), channel_id=1, source_target_pairs={{0,12},{4,8},{8,4},{12,0},{16,28},{20,24},{24,20},{28,16},{1,13},{... | collective-permute-start | bytes 135176 | tf_op jit(solution)/shard_map/ppermute | solution.py:378
  31.7 0.7 %collective-permute-start.15 = (bf16[176,128]{1,0:T(8,128)(2,1)S(1)}, bf16[176,128]{1,0:T(8,128)(2,1)S(1)}, u32[]{:S(2)}, u32[]{:S(2)}) collective-permute-start(bf16[176,128]{1,0:T(8,128)(2,1)S(1)} %get-tuple-element.68), channel_id=1, source_target_pairs={{0,8},{4,12},{8,0},{12,4},{16,24},{20,28},{24,16},{28,20},{1,9},{5... | collective-permute-start | bytes 135176 | tf_op jit(solution)/shard_map/ppermute | solution.py:378
  32.5 0.9 %collective-permute-start.16 = (bf16[176,128]{1,0:T(8,128)(2,1)S(1)}, bf16[176,128]{1,0:T(8,128)(2,1)S(1)}, u32[]{:S(2)}, u32[]{:S(2)}) collective-permute-start(bf16[176,128]{1,0:T(8,128)(2,1)S(1)} %get-tuple-element.69), channel_id=1, source_target_pairs={{0,4},{4,0},{8,12},{12,8},{16,20},{20,16},{24,28},{28,24},{1,5},{5... | collective-permute-start | bytes 135176 | tf_op jit(solution)/shard_map/ppermute | solution.py:378
  33.4 2.2 %shard_map.112 = (bf16[2,1,64,320]{3,2,1,0:T(8,128)(2,1)}, bf16[2,1,64,320]{3,2,1,0:T(8,128)(2,1)}, bf16[2,1,64,320]{3,2,1,0:T(8,128)(2,1)}, bf16[2,1,64,320]{3,2,1,0:T(8,128)(2,1)}) custom-call(bf16[640,128]{1,0:T(8,128)(2,1)S(1)} %get-tuple-element.50.refs_0_, bf16[640,128]{1,0:T(8,128)(2,1)S(1)} %collective-permute-done.2.refs_1_, ...), custom_call_target="tpu_custom_call" | custom-call | bytes 2232320 | tf_op jit(solution)/shard_map/pallas_call | solution.py:27
  35.8 0.7 %collective-permute-done.16.refs_7_ = bf16[176,128]{1,0:T(8,128)(2,1)S(1)} collective-permute-done((bf16[176,128]{1,0:T(8,128)(2,1)S(1)}, bf16[176,128]{1,0:T(8,128)(2,1)S(1)}, u32[]{:S(2)}, u32[]{:S(2)}) %collective-permute-start.16) | collective-permute-done | bytes 45088 | tf_op jit(solution)/shard_map/ppermute | solution.py:378
  36.5 0.7 %shard_map.118 = (f32[115,128]{1,0:T(8,128)}, f32[60,128]{1,0:T(8,128)}) custom-call(f32[176,128]{1,0:T(8,128)S(1)} %get-tuple-element.62.refs_0_, bf16[176,128]{1,0:T(8,128)(2,1)S(1)} %collective-permute-done.10.refs_1_, bf16[176,128]{1,0:T(8,128)(2,1)S(1)} %collective-permute-done.11.refs_2_, bf16[176,128]{1,0:T(8,128)(2,1)S(1)} %collective-permute-done.12.refs_3_, ...), custom_call_target="tpu_custom_call" | custom-call | bytes 495104 | tf_op jit(solution)/shard_map/pallas_call | solution.py:27
  (27 shorter events, 2.0 us)
Async XLA Ops:
  1.7 10.0 %collective-permute-start = (bf16[128,640]{1,0:T(8,128)(2,1)S(1)}, bf16[128,640]{1,0:T(8,128)(2,1)S(1)}, u32[]{:S(2)}, u32[]{:S(2)}) collective-permute-start(bf16[128,640]{1,0:T(8,128)(2,1)S(1)} %shard_map.109.own.refs_0_), channel_id=1, source_target_pairs={{0,4},{4,0},{8,12},{12,8},{16,20},{20,16},{24,28},{28,24},{1,5},{5... | collective-permute-start | bytes 491528 | tf_op jit(solution)/shard_map/ppermute | solution.py:403
  4.8 7.0 %collective-permute-start.1 = (bf16[128,640]{1,0:T(8,128)(2,1)S(1)}, bf16[128,640]{1,0:T(8,128)(2,1)S(1)}, u32[]{:S(2)}, u32[]{:S(2)}) collective-permute-start(bf16[128,640]{1,0:T(8,128)(2,1)S(1)} %shard_map.109.own.refs_0_), channel_id=1, source_target_pairs={{4,8},{8,4},{12,16},{16,12},{20,24},{24,20},{5,9},{9,5},{13,17},{1... | collective-permute-start | bytes 491528 | tf_op jit(solution)/shard_map/ppermute | solution.py:403
  5.4 8.5 %collective-permute-start.6 = (bf16[128,640]{1,0:T(8,128)(2,1)S(1)}, bf16[128,640]{1,0:T(8,128)(2,1)S(1)}, u32[]{:S(2)}, u32[]{:S(2)}) collective-permute-start(bf16[128,640]{1,0:T(8,128)(2,1)S(1)} %shard_map.109.own.refs_0_), channel_id=1, source_target_pairs={{0,2},{1,3},{2,0},{3,1},{4,6},{5,7},{6,4},{7,5},{8,10},{9,11},{10,... | collective-permute-start | bytes 491528 | tf_op jit(solution)/shard_map/ppermute | solution.py:378
  12.4 5.4 %collective-permute-start.3 = (bf16[640,128]{1,0:T(8,128)(2,1)S(1)}, bf16[640,128]{1,0:T(8,128)(2,1)S(1)}, u32[]{:S(2)}, u32[]{:S(2)}) collective-permute-start(bf16[640,128]{1,0:T(8,128)(2,1)S(1)} %get-tuple-element.50.refs_0_), channel_id=1, source_target_pairs={{0,2},{1,3},{2,0},{3,1},{4,6},{5,7},{6,4},{7,5},{8,10},{9,11},{10,... | collective-permute-start | bytes 491528 | tf_op jit(solution)/shard_map/ppermute | solution.py:378
  14.6 1.6 %collective-permute-start.7 = (bf16[8,64,128]{2,1,0:T(8,128)(2,1)S(1)}, bf16[8,64,128]{2,1,0:T(8,128)(2,1)S(1)}, u32[]{:S(2)}, u32[]{:S(2)}) collective-permute-start(bf16[8,64,128]{2,1,0:T(8,128)(2,1)S(1)} %get-tuple-element.58), channel_id=1, source_target_pairs={{0,1},{1,0},{2,3},{3,2},{4,5},{5,4},{6,7},{7,6},{8,9},{9,8},{10,11... | collective-permute-start | bytes 393224 | tf_op jit(solution)/shard_map/ppermute | solution.py:378
  14.7 1.5 %collective-permute-start.8 = (bf16[6,64,128]{2,1,0:T(8,128)(2,1)S(1)}, bf16[6,64,128]{2,1,0:T(8,128)(2,1)S(1)}, u32[]{:S(2)}, u32[]{:S(2)}) collective-permute-start(bf16[6,64,128]{2,1,0:T(8,128)(2,1)S(1)} %get-tuple-element.59), channel_id=1, source_target_pairs={{0,1},{1,0},{2,3},{3,2},{4,5},{5,4},{6,7},{7,6},{8,9},{9,8},{10,11... | collective-permute-start | bytes 294920 | tf_op jit(solution)/shard_map/ppermute | solution.py:378
  15.2 3.1 %collective-permute-start.2 = (bf16[640,128]{1,0:T(8,128)(2,1)S(1)}, bf16[640,128]{1,0:T(8,128)(2,1)S(1)}, u32[]{:S(2)}, u32[]{:S(2)}) collective-permute-start(bf16[640,128]{1,0:T(8,128)(2,1)S(1)} %get-tuple-element.50.refs_0_), channel_id=1, source_target_pairs={{0,1},{1,0},{2,3},{3,2},{4,5},{5,4},{6,7},{7,6},{8,9},{9,8},{10,11... | collective-permute-start | bytes 491528 | tf_op jit(solution)/shard_map/ppermute | solution.py:378
  16.3 17.1 %copy-start = (bf16[3,3,2,160,160]{4,3,2,1,0:T(8,128)(2,1)S(1)}, bf16[3,3,2,160,160]{4,3,2,1,0:T(8,128)(2,1)}, u32[]{:S(2)}) copy-start(bf16[3,3,2,160,160]{4,3,2,1,0:T(8,128)(2,1)} %refs_9_.1) | copy-start | bytes 2764804
  16.3 17.1 %copy-start.1 = (bf16[2,1,64,320]{3,2,1,0:T(8,128)(2,1)S(1)}, bf16[2,1,64,320]{3,2,1,0:T(8,128)(2,1)}, u32[]{:S(2)}) copy-start(bf16[2,1,64,320]{3,2,1,0:T(8,128)(2,1)} %refs_5_.1) | copy-start | bytes 245764
  16.3 17.1 %copy-start.2 = (bf16[2,1,64,320]{3,2,1,0:T(8,128)(2,1)S(1)}, bf16[2,1,64,320]{3,2,1,0:T(8,128)(2,1)}, u32[]{:S(2)}) copy-start(bf16[2,1,64,320]{3,2,1,0:T(8,128)(2,1)} %refs_6_.1) | copy-start | bytes 245764
  16.3 5.1 %collective-permute-start.9 = (bf16[6,64,128]{2,1,0:T(8,128)(2,1)S(1)}, bf16[6,64,128]{2,1,0:T(8,128)(2,1)S(1)}, u32[]{:S(2)}, u32[]{:S(2)}) collective-permute-start(bf16[6,64,128]{2,1,0:T(8,128)(2,1)S(1)} %get-tuple-element.61), channel_id=1, source_target_pairs={{0,2},{1,3},{2,0},{3,1},{4,6},{5,7},{6,4},{7,5},{8,10},{9,11},{10,... | collective-permute-start | bytes 294920 | tf_op jit(solution)/shard_map/ppermute | solution.py:378
  17.8 1.3 %collective-permute-start.5 = (bf16[320,128]{1,0:T(8,128)(2,1)S(1)}, bf16[320,128]{1,0:T(8,128)(2,1)S(1)}, u32[]{:S(2)}, u32[]{:S(2)}) collective-permute-start(bf16[320,128]{1,0:T(8,128)(2,1)S(1)} %get-tuple-element.72), channel_id=1, source_target_pairs={{0,1},{1,0},{2,3},{3,2},{4,5},{5,4},{6,7},{7,6},{8,9},{9,8},{10,11... | collective-permute-start | bytes 245768 | tf_op jit(solution)/shard_map/ppermute | solution.py:378
  17.9 1.4 %collective-permute-start.4 = (bf16[320,128]{1,0:T(8,128)(2,1)S(1)}, bf16[320,128]{1,0:T(8,128)(2,1)S(1)}, u32[]{:S(2)}, u32[]{:S(2)}) collective-permute-start(bf16[320,128]{1,0:T(8,128)(2,1)S(1)} %get-tuple-element.73), channel_id=1, source_target_pairs={{0,1},{1,0},{2,3},{3,2},{4,5},{5,4},{6,7},{7,6},{8,9},{9,8},{10,11... | collective-permute-start | bytes 245768 | tf_op jit(solution)/shard_map/ppermute | solution.py:378
  21.4 10.3 %collective-permute-start.10 = (bf16[176,128]{1,0:T(8,128)(2,1)S(1)}, bf16[176,128]{1,0:T(8,128)(2,1)S(1)}, u32[]{:S(2)}, u32[]{:S(2)}) collective-permute-start(bf16[176,128]{1,0:T(8,128)(2,1)S(1)} %get-tuple-element.63), channel_id=1, source_target_pairs={{0,24},{4,28},{8,16},{12,20},{16,8},{20,12},{24,0},{28,4},{1,25},{... | collective-permute-start | bytes 135176 | tf_op jit(solution)/shard_map/ppermute | solution.py:378
  26.5 5.9 %collective-permute-start.11 = (bf16[176,128]{1,0:T(8,128)(2,1)S(1)}, bf16[176,128]{1,0:T(8,128)(2,1)S(1)}, u32[]{:S(2)}, u32[]{:S(2)}) collective-permute-start(bf16[176,128]{1,0:T(8,128)(2,1)S(1)} %get-tuple-element.64), channel_id=1, source_target_pairs={{0,16},{4,20},{8,24},{12,28},{16,0},{20,4},{24,8},{28,12},{1,17},{... | collective-permute-start | bytes 135176 | tf_op jit(solution)/shard_map/ppermute | solution.py:378
  26.5 9.0 %collective-permute-start.12 = (bf16[176,128]{1,0:T(8,128)(2,1)S(1)}, bf16[176,128]{1,0:T(8,128)(2,1)S(1)}, u32[]{:S(2)}, u32[]{:S(2)}) collective-permute-start(bf16[176,128]{1,0:T(8,128)(2,1)S(1)} %get-tuple-element.65), channel_id=1, source_target_pairs={{0,28},{4,24},{8,20},{12,16},{16,12},{20,8},{24,4},{28,0},{1,29},{... | collective-permute-start | bytes 135176 | tf_op jit(solution)/shard_map/ppermute | solution.py:378
  28.9 6.6 %collective-permute-start.13 = (bf16[176,128]{1,0:T(8,128)(2,1)S(1)}, bf16[176,128]{1,0:T(8,128)(2,1)S(1)}, u32[]{:S(2)}, u32[]{:S(2)}) collective-permute-start(bf16[176,128]{1,0:T(8,128)(2,1)S(1)} %get-tuple-element.66), channel_id=1, source_target_pairs={{0,20},{4,16},{8,28},{12,24},{16,4},{20,0},{24,12},{28,8},{1,21},{... | collective-permute-start | bytes 135176 | tf_op jit(solution)/shard_map/ppermute | solution.py:378
  29.5 6.0 %collective-permute-start.14 = (bf16[176,128]{1,0:T(8,128)(2,1)S(1)}, bf16[176,128]{1,0:T(8,128)(2,1)S(1)}, u32[]{:S(2)}, u32[]{:S(2)}) collective-permute-start(bf16[176,128]{1,0:T(8,128)(2,1)S(1)} %get-tuple-element.67), channel_id=1, source_target_pairs={{0,12},{4,8},{8,4},{12,0},{16,28},{20,24},{24,20},{28,16},{1,13},{... | collective-permute-start | bytes 135176 | tf_op jit(solution)/shard_map/ppermute | solution.py:378
  31.7 4.0 %collective-permute-start.15 = (bf16[176,128]{1,0:T(8,128)(2,1)S(1)}, bf16[176,128]{1,0:T(8,128)(2,1)S(1)}, u32[]{:S(2)}, u32[]{:S(2)}) collective-permute-start(bf16[176,128]{1,0:T(8,128)(2,1)S(1)} %get-tuple-element.68), channel_id=1, source_target_pairs={{0,8},{4,12},{8,0},{12,4},{16,24},{20,28},{24,16},{28,20},{1,9},{5... | collective-permute-start | bytes 135176 | tf_op jit(solution)/shard_map/ppermute | solution.py:378
  32.5 4.0 %collective-permute-start.16 = (bf16[176,128]{1,0:T(8,128)(2,1)S(1)}, bf16[176,128]{1,0:T(8,128)(2,1)S(1)}, u32[]{:S(2)}, u32[]{:S(2)}) collective-permute-start(bf16[176,128]{1,0:T(8,128)(2,1)S(1)} %get-tuple-element.69), channel_id=1, source_target_pairs={{0,4},{4,0},{8,12},{12,8},{16,20},{20,16},{24,28},{28,24},{1,5},{5... | collective-permute-start | bytes 135176 | tf_op jit(solution)/shard_map/ppermute | solution.py:378

commit v6 on v5

--- a/solution.py
+++ b/solution.py
@@ -97,23 +97,19 @@
     weight_out[...] = weight[...]
 
 
-def time_body(near, far, forth0, back0, slope, base, weight, x2_out, g1_out, held_out):
+def time_body(near, near_cot, far, forth0, back0, slope, base, weight, x2_out, g1_out, held_out):
     cols = forth0.shape[0]
     groups, width = weight.shape[1:3]
     tap = jnp.where(lax.axis_index("tm") % 2 == 0, 2, 0)
     forth, back = [], []
     for q in range(groups):
         lanes = slice(q * width, (q + 1) * width)
-        forth.append(
-            forth0[:, lanes]
-            + dot(near[:cols, lanes], weight[tap, q], 1, 0)
-            + dot(far[:cols, lanes], weight[2 - tap, q], 1, 0)
-        )
-        back.append(
-            back0[:, lanes]
-            + dot(near[cols:, lanes], weight[2 - tap, q], 1, 1)
-            + dot(far[cols:, lanes], weight[tap, q], 1, 1)
-        )
+        sides = jnp.concatenate([near[:cols, lanes], far[:cols, lanes]], axis=1)
+        taps = jnp.concatenate([weight[tap, q], weight[2 - tap, q]], axis=0)
+        forth.append(forth0[:, lanes] + dot(sides, taps, 1, 0))
+        sides = jnp.concatenate([near_cot[:, lanes], far[cols:, lanes]], axis=1)
+        taps = jnp.concatenate([weight[2 - tap, q], weight[tap, q]], axis=1)
+        back.append(back0[:, lanes] + dot(sides, taps, 1, 1))
     branch = unsqueezed(jnp.concatenate(forth, axis=-1))
     back = unsqueezed(jnp.concatenate(back, axis=-1) * slope[...])
     acts, cots = [], []
@@ -126,38 +122,22 @@
         acts.append(v * sigmoid(v))
         cots.append(g1.astype(F32))
     ch = held_out.shape[0] // 2
-    held_out[:ch] = jnp.concatenate(acts, axis=0).T.astype(BF16)
-    held_out[ch:] = jnp.concatenate(cots, axis=0).T.astype(BF16)
-
-
-def time_terms(own, pairs, total):
-    cols = own.shape[0] // 2
+    held_out[:ch] = jnp.concatenate(acts, axis=0).astype(BF16).T
+    held_out[ch:] = jnp.concatenate(cots, axis=0).astype(BF16).T
+
+
+def time_terms(near_cot, far, owns, total):
+    cols = far.shape[0] // 2
     width = total.shape[1]
-    groups = own.shape[1] // width
-    act = own[:cols].astype(F32).T.astype(BF16)
-    for k, cot in pairs:
+    groups = far.shape[1] // width
+    act = jnp.concatenate([v[:cols] for v in owns], axis=0).T
+    own = jnp.concatenate([v[cols:] for v in owns], axis=0)
+    tap = jnp.where(lax.axis_index("tm") % 2 == 0, 0, 2)
+    for k, cot in ((1, own), (tap, near_cot[...]), (2 - tap, far[cols:])):
         for q in range(groups):
             part = slice(q * width, (q + 1) * width)
             at = pl.multiple_of((k * groups + q) * width, width)
-            total[pl.ds(at, width), :] = dot(act[part], cot[cols:, part], 1, 0)
-
-
-def near_tap():
-    return jnp.where(lax.axis_index("tm") % 2 == 0, 0, 2)
-
-
-def time_near_body(near, *refs):
-    owns, total = refs[:-1], refs[-1]
-    cols = near.shape[0] // 2
-    width = total.shape[1]
-    groups = near.shape[1] // width
-    total[...] = jnp.zeros_like(total)
-    time_terms(owns[0], ((near_tap(), near),), total)
-    act = jnp.concatenate([v[:cols] for v in owns], axis=0).astype(F32).T.astype(BF16)
-    cot = jnp.concatenate([v[cols:] for v in owns], axis=0)
-    for q in range(groups):
-        part = slice(q * width, (q + 1) * width)
-        total[pl.ds((groups + q) * width, width), :] = dot(act[part], cot[:, part], 1, 0)
+            total[pl.ds(at, width), :] = dot(act[part, : cot.shape[0]], cot[:, part], 1, 0)
 
 
 def outer_steps(steps, peers, taps, rows):
@@ -169,30 +149,28 @@
     ]
 
 
-def time_sum_body(offsets, rows, own, far, early, keep, *refs):
-    sends, total = refs[:-1], refs[-1]
-    total[: early.shape[0]] = early[...]
-    time_terms(own, ((2 - near_tap(), far),), total)
+def time_sum_body(offsets, rows, near_cot, far, *refs):
+    owns, refs, total = refs[: len(offsets)], refs[len(offsets) : -1], refs[-1]
+    keeps, sends = refs[: len(offsets)], refs[len(offsets) :]
+    time_terms(near_cot, far, owns, total)
     me, peers, steps = lax.axis_index("row"), lax.axis_size("row"), lax.axis_size("tm")
-    held, third = keep.shape[2], early.shape[0] // 3
+    held, third = keeps[0].shape[1], steps * peers * rows // 3
     for u, offset in enumerate(offsets):
         if u == 1:
             total[third : 2 * third] = jnp.zeros((third, total.shape[1]), F32)
         for i, t in enumerate(range(steps) if u == 0 else outer_steps(steps, peers, 3, rows)):
             mine = (t * peers + (me ^ offset)) * rows
             other = (t * peers + (me ^ offset ^ 1)) * rows
-            keep[u, i] = total[pl.ds(mine, held), :]
+            keeps[u][i] = total[pl.ds(mine, held), :]
             sends[u][i] = total[pl.ds(other, held), :].astype(BF16)
 
 
-def time_sum_whole_body(own, far, early, total):
-    total[...] = early[...]
-    time_terms(own, ((2 - near_tap(), far),), total)
-
-
-def fold_body(kept, own_came, other_came, keep, send):
-    keep[...] = kept[0] + own_came[...].astype(F32)
-    send[...] = (kept[1, : send.shape[0]] + other_came[...].astype(F32)).astype(BF16)
+def time_sum_whole_body(near_cot, far, own, total):
+    time_terms(near_cot, far, (own,), total)
+
+
+def fold_body(kept, came, send):
+    send[...] = (kept[...] + came[...].astype(F32)).astype(BF16)
 
 
 def place(slots, rows_ref, lead):
@@ -293,7 +271,7 @@
         out[k] = jnp.concatenate(parts, axis=0)
 
 
-def join_body(time_rows, outer, pieces, kept, came, mine, *sends):
+def join_body(time_rows, outer, pieces, kept, core_came, came, mine, *sends):
     tall, steps = kept.shape[1], kept.shape[0]
     row = lax.broadcasted_iota(jnp.int32, (tall, LANES), 0)
     gap = steps - len(outer)
@@ -303,7 +281,7 @@
         over = t >= first + gap
         sent = jnp.logical_or(t < first, over)
         terms = came[jnp.where(over, t - gap, jnp.minimum(t, len(outer) - 1))].astype(F32)
-        terms = kept[t] + jnp.where(sent, terms, 0.0)
+        terms = kept[t] + core_came[t].astype(F32) + jnp.where(sent, terms, 0.0)
         head = pieces[k, :tall] + jnp.where(row < time_rows, terms, 0.0)
         piece = jnp.concatenate([head, pieces[k, tall:]], axis=0)
         if k == 0:
@@ -427,11 +405,11 @@
     )
 
     near, centre = lax.optimization_barrier((near, centre))
+    near_cot = near[cols:]
     bits = [1 << i for i in range(peers.bit_length() - 1)]
     even = time_rows % devices == 0 and space_rows % devices == 0 and peers == 4
     owns = gather(packed, "row", bits[1:]) if even else {0: packed}
     owns = [owns[k] for k in sorted(owns)]
-    early = on_device(time_near_body, (near, *owns), [shape((time_rows, time_width), F32)])[0]
     if even:
         rows = time_rows // devices
         tall = round_up(rows, 16)
@@ -439,18 +417,17 @@
         block = (steps, tall, time_width)
         outer = outer_steps(steps, peers, 3, rows)
         rest = (len(outer), *block[1:])
-        kept, *sent = on_device(
+        kept, other, sent_own, core_sent = on_device(
             functools.partial(time_sum_body, offsets, rows),
-            (packed, far, early),
-            [shape((2, *block), F32), shape(block, BF16), shape(rest, BF16)],
+            (near_cot, far, *owns),
+            [shape(block, F32), shape(rest, F32), shape(block, BF16), shape(rest, BF16)],
             [pltpu.VMEM((round_up(time_rows + tall, 8), time_width), F32)],
         )
-        came = [swap(v, "row", 1) for v in sent]
-        kept, sent = on_device(fold_body, (kept, *came), [shape(block, F32), shape(rest, BF16)])
-        came = [swap(sent, "row", bits[1])]
+        sent = on_device(fold_body, (other, swap(core_sent, "row", 1)), [shape(rest, BF16)])[0]
+        came = [swap(sent_own, "row", 1), swap(sent, "row", bits[1])]
     x2, g1, held = on_device(
         time_body,
-        (near, far, *centre),
+        (near, near_cot, far, *centre),
         [shape(y1.shape, BF16)] * 2 + [shape((2 * ch, 2 * cols), BF16)],
     )
     slots = {k: (v,) for k, v in gather(held, "row", bits[1:]).items()}
@@ -491,7 +468,7 @@
         time_share = time_share.reshape(-1)
     else:
         total = on_device(
-            time_sum_whole_body, (packed, far, early), [shape((time_rows, time_width), F32)]
+            time_sum_whole_body, (near_cot, far, packed), [shape((time_rows, time_width), F32)]
         )[0]
         time_share = factor * lax.psum_scatter(
             total.reshape(-1), ("tm", "row"), scatter_dimension=0, tiled=True

time: 37.4 us -> 36.7 us (0.981)
    pallas_call x10 -> x9, Pallas kernels: 8.17 us -> 7.8 us  [on_device(): pl.pallas_call(body, out_shape=outs, in_specs=[pl.BlockSpec(memory_space=...]
  transfers between devices with their start and end apart: 17 -> 17, of which waited for: 9 -> 10; matrix products, arithmetic and copies ran while one was open for 0% -> 0% of each run, Pallas kernels for 17% -> 16%
where the time goes in v6:
time: 36.7 us; the launch traced here: 36.5 us
  starting transfers between devices  20.4 us (56%)
  Pallas kernels  7.8 us (21%)
  waiting for transfers between devices  7.49 us (20%)
  between operations  0.76 us (2%)
    ppermute x15, starting transfers between devices, swap(): lax.ppermute(x, axis, [(i, i ^ bit) for i in range(lax.axis_size(axis))])  16.7 us
    pallas_call x9, Pallas kernels, on_device(): pl.pallas_call(body, out_shape=outs, in_specs=[pl.BlockSpec(memory_space=...  7.8 us
    ppermute x15, waiting for transfers between devices, swap(): lax.ppermute(x, axis, [(i, i ^ bit) for i in range(lax.axis_size(axis))])  4.24 us
    ppermute x2, starting transfers between devices, neighbours(): lax.ppermute(x, axis, [p for i in lower for p in ((i, i + 1), (i + 1, i))])  3.69 us
    ppermute x2, waiting for transfers between devices, neighbours(): lax.ppermute(x, axis, [p for i in lower for p in ((i, i + 1), (i + 1, i))])  3.26 us
  transfers between devices with their start and end apart: 17, of which 10 were waited for; matrix products, arithmetic and copies ran while one was open for 0% of the time, Pallas kernels for 16%

profile of v6, /device:TPU:0, one launch (start us, length us, event | category | flops | bytes accessed | tf_op | source)
XLA Modules:
  0.0 36.5 jit_solution(10598973670007162145)
XLA Ops:
  0.6 1.1 %shard_map.109.own.refs_0_ = bf16[128,640]{1,0:T(8,128)(2,1)S(1)} custom-call(bf16[2,1,64,320]{3,2,1,0:T(8,128)(2,1)} %refs_5_.1, bf16[2,1,64,320]{3,2,1,0:T(8,128)(2,1)} %refs_6_.1), custom_call_target="tpu_custom_call" | custom-call | bytes 327680 | tf_op jit(solution)/shard_map/pallas_call | solution.py:27
  1.7 3.0 %collective-permute-start = (bf16[128,640]{1,0:T(8,128)(2,1)S(1)}, bf16[128,640]{1,0:T(8,128)(2,1)S(1)}, u32[]{:S(2)}, u32[]{:S(2)}) collective-permute-start(bf16[128,640]{1,0:T(8,128)(2,1)S(1)} %shard_map.109.own.refs_0_), channel_id=1, source_target_pairs={{0,4},{4,0},{8,12},{12,8},{16,20},{20,16},{24,28},{28,24},{1,5},{5... | collective-permute-start | bytes 491528 | tf_op jit(solution)/shard_map/ppermute | solution.py:381
  4.8 0.7 %collective-permute-start.1 = (bf16[128,640]{1,0:T(8,128)(2,1)S(1)}, bf16[128,640]{1,0:T(8,128)(2,1)S(1)}, u32[]{:S(2)}, u32[]{:S(2)}) collective-permute-start(bf16[128,640]{1,0:T(8,128)(2,1)S(1)} %shard_map.109.own.refs_0_), channel_id=1, source_target_pairs={{4,8},{8,4},{12,16},{16,12},{20,24},{24,20},{5,9},{9,5},{13,17},{1... | collective-permute-start | bytes 491528 | tf_op jit(solution)/shard_map/ppermute | solution.py:381
  5.4 1.6 %collective-permute-start.6 = (bf16[128,640]{1,0:T(8,128)(2,1)S(1)}, bf16[128,640]{1,0:T(8,128)(2,1)S(1)}, u32[]{:S(2)}, u32[]{:S(2)}) collective-permute-start(bf16[128,640]{1,0:T(8,128)(2,1)S(1)} %shard_map.109.own.refs_0_), channel_id=1, source_target_pairs={{0,2},{1,3},{2,0},{3,1},{4,6},{5,7},{6,4},{7,5},{8,10},{9,11},{10,... | collective-permute-start | bytes 491528 | tf_op jit(solution)/shard_map/ppermute | solution.py:356
  7.0 1.5 %shard_map.110 = (f32[64,640]{1,0:T(8,128)S(1)}, f32[64,640]{1,0:T(8,128)S(1)}, f32[64,640]{1,0:T(8,128)S(1)}, bf16[2,2,64,320]{3,2,1,0:T(8,128)(2,1)S(1)}, bf16[3,5,128,128]{3,2,1,0:T(8,128)(2,1)S(1)}) custom-call(bf16[2,1,64,320]{3,2,1,0:T(8,128)(2,1)} %refs_5_.1, bf16[2,1,64,320]{3,2,1,0:T(8,128)(2,1)} %y2_far.1, bf16[2,1,64,320]{3,2,1,0:T(8,128)(2,1)} %c1_far.1, ...), custom_call_target="tpu_custom_call" | custom-call | bytes 2048000 | tf_op jit(solution)/shard_map/pallas_call | solution.py:27
  8.5 3.3 %collective-permute-done.near = bf16[128,640]{1,0:T(8,128)(2,1)S(1)} collective-permute-done((bf16[128,640]{1,0:T(8,128)(2,1)S(1)}, bf16[128,640]{1,0:T(8,128)(2,1)S(1)}, u32[]{:S(2)}, u32[]{:S(2)}) %collective-permute-start) | collective-permute-done | bytes 163872 | tf_op jit(solution)/shard_map/ppermute | solution.py:381
  11.8 0.5 %shard_map.111 = (bf16[2,1,64,320]{3,2,1,0:T(8,128)(2,1)S(1)}, bf16[2,1,64,320]{3,2,1,0:T(8,128)(2,1)S(1)}, bf16[640,128]{1,0:T(8,128)(2,1)S(1)}) custom-call(bf16[128,640]{1,0:T(8,128)(2,1)S(1)} %collective-permute-done.near, bf16[64,640]{1,0:T(8,128)(2,1)S(1)} %slice.12.near_cot, bf16[128,640]{1,0:T(8,128)(2,1)S(1)} %collective-permute-done.1.far, ...), custom_call_target="tpu_custom_call" | custom-call | bytes 1884160 | tf_op jit(solution)/shard_map/pallas_call | solution.py:27
  12.3 1.6 %collective-permute-start.3 = (bf16[640,128]{1,0:T(8,128)(2,1)S(1)}, bf16[640,128]{1,0:T(8,128)(2,1)S(1)}, u32[]{:S(2)}, u32[]{:S(2)}) collective-permute-start(bf16[640,128]{1,0:T(8,128)(2,1)S(1)} %get-tuple-element.49.refs_0_), channel_id=1, source_target_pairs={{0,2},{1,3},{2,0},{3,1},{4,6},{5,7},{6,4},{7,5},{8,10},{9,11},{10,... | collective-permute-start | bytes 491528 | tf_op jit(solution)/shard_map/ppermute | solution.py:356
  14.4 0.5 %collective-permute-start.2 = (bf16[640,128]{1,0:T(8,128)(2,1)S(1)}, bf16[640,128]{1,0:T(8,128)(2,1)S(1)}, u32[]{:S(2)}, u32[]{:S(2)}) collective-permute-start(bf16[640,128]{1,0:T(8,128)(2,1)S(1)} %get-tuple-element.49.refs_0_), channel_id=1, source_target_pairs={{0,1},{1,0},{2,3},{3,2},{4,5},{5,4},{6,7},{7,6},{8,9},{9,8},{10,11... | collective-permute-start | bytes 491528 | tf_op jit(solution)/shard_map/ppermute | solution.py:356
  14.9 0.7 %collective-permute-done.8.came = bf16[6,64,128]{2,1,0:T(8,128)(2,1)S(1)} collective-permute-done((bf16[6,64,128]{2,1,0:T(8,128)(2,1)S(1)}, bf16[6,64,128]{2,1,0:T(8,128)(2,1)S(1)}, u32[]{:S(2)}, u32[]{:S(2)}) %collective-permute-start.8) | collective-permute-done | bytes 98336 | tf_op jit(solution)/shard_map/ppermute | solution.py:356
  15.7 0.6 %collective-permute-start.9 = (bf16[6,64,128]{2,1,0:T(8,128)(2,1)S(1)}, bf16[6,64,128]{2,1,0:T(8,128)(2,1)S(1)}, u32[]{:S(2)}, u32[]{:S(2)}) collective-permute-start(bf16[6,64,128]{2,1,0:T(8,128)(2,1)S(1)} %shard_map.115), channel_id=1, source_target_pairs={{0,2},{1,3},{2,0},{3,1},{4,6},{5,7},{6,4},{7,5},{8,10},{9,11},{10,... | collective-permute-start | bytes 294920 | tf_op jit(solution)/shard_map/ppermute | solution.py:356
  16.3 1.4 %collective-permute-done.3.refs_2_ = bf16[640,128]{1,0:T(8,128)(2,1)S(1)} collective-permute-done((bf16[640,128]{1,0:T(8,128)(2,1)S(1)}, bf16[640,128]{1,0:T(8,128)(2,1)S(1)}, u32[]{:S(2)}, u32[]{:S(2)}) %collective-permute-start.3) | collective-permute-done | bytes 163872 | tf_op jit(solution)/shard_map/ppermute | solution.py:356
  17.8 0.5 %collective-permute-start.4 = (bf16[320,128]{1,0:T(8,128)(2,1)S(1)}, bf16[320,128]{1,0:T(8,128)(2,1)S(1)}, u32[]{:S(2)}, u32[]{:S(2)}) collective-permute-start(bf16[320,128]{1,0:T(8,128)(2,1)S(1)} %get-tuple-element.71), channel_id=1, source_target_pairs={{0,1},{1,0},{2,3},{3,2},{4,5},{5,4},{6,7},{7,6},{8,9},{9,8},{10,11... | collective-permute-start | bytes 245768 | tf_op jit(solution)/shard_map/ppermute | solution.py:356
  18.3 0.8 %collective-permute-done.5.refs_4_ = bf16[320,128]{1,0:T(8,128)(2,1)S(1)} collective-permute-done((bf16[320,128]{1,0:T(8,128)(2,1)S(1)}, bf16[320,128]{1,0:T(8,128)(2,1)S(1)}, u32[]{:S(2)}, u32[]{:S(2)}) %collective-permute-start.5) | collective-permute-done | bytes 81952 | tf_op jit(solution)/shard_map/ppermute | solution.py:356
  19.2 1.3 %shard_map.113.pieces = f32[8,176,128]{2,1,0:T(8,128)S(1)} custom-call(bf16[640,128]{1,0:T(8,128)(2,1)S(1)} %get-tuple-element.49.refs_0_, bf16[640,128]{1,0:T(8,128)(2,1)S(1)} %collective-permute-done.2.refs_1_, bf16[640,128]{1,0:T(8,128)(2,1)S(1)} %collective-permute-done.3.refs_2_, bf16[320,128]{1,0:T(8,128)(2,1)S(1)} %collective-permute-done.4.refs_3_, ...), custom_call_target="tpu_custom_call" | custom-call | bytes 1376256 | tf_op jit(solution)/shard_map/pallas_call | solution.py:27
  20.7 5.1 %collective-permute-start.10 = (bf16[176,128]{1,0:T(8,128)(2,1)S(1)}, bf16[176,128]{1,0:T(8,128)(2,1)S(1)}, u32[]{:S(2)}, u32[]{:S(2)}) collective-permute-start(bf16[176,128]{1,0:T(8,128)(2,1)S(1)} %get-tuple-element.61), channel_id=1, source_target_pairs={{0,24},{4,28},{8,16},{12,20},{16,8},{20,12},{24,0},{28,4},{1,25},{... | collective-permute-start | bytes 135176 | tf_op jit(solution)/shard_map/ppermute | solution.py:356
  25.8 2.4 %collective-permute-start.12 = (bf16[176,128]{1,0:T(8,128)(2,1)S(1)}, bf16[176,128]{1,0:T(8,128)(2,1)S(1)}, u32[]{:S(2)}, u32[]{:S(2)}) collective-permute-start(bf16[176,128]{1,0:T(8,128)(2,1)S(1)} %get-tuple-element.63), channel_id=1, source_target_pairs={{0,28},{4,24},{8,20},{12,16},{16,12},{20,8},{24,4},{28,0},{1,29},{... | collective-permute-start | bytes 135176 | tf_op jit(solution)/shard_map/ppermute | solution.py:356
  28.2 0.6 %collective-permute-start.13 = (bf16[176,128]{1,0:T(8,128)(2,1)S(1)}, bf16[176,128]{1,0:T(8,128)(2,1)S(1)}, u32[]{:S(2)}, u32[]{:S(2)}) collective-permute-start(bf16[176,128]{1,0:T(8,128)(2,1)S(1)} %get-tuple-element.64), channel_id=1, source_target_pairs={{0,20},{4,16},{8,28},{12,24},{16,4},{20,0},{24,12},{28,8},{1,21},{... | collective-permute-start | bytes 135176 | tf_op jit(solution)/shard_map/ppermute | solution.py:356
  28.8 2.2 %collective-permute-start.14 = (bf16[176,128]{1,0:T(8,128)(2,1)S(1)}, bf16[176,128]{1,0:T(8,128)(2,1)S(1)}, u32[]{:S(2)}, u32[]{:S(2)}) collective-permute-start(bf16[176,128]{1,0:T(8,128)(2,1)S(1)} %get-tuple-element.65), channel_id=1, source_target_pairs={{0,12},{4,8},{8,4},{12,0},{16,28},{20,24},{24,20},{28,16},{1,13},{... | collective-permute-start | bytes 135176 | tf_op jit(solution)/shard_map/ppermute | solution.py:356
  31.0 0.6 %collective-permute-start.15 = (bf16[176,128]{1,0:T(8,128)(2,1)S(1)}, bf16[176,128]{1,0:T(8,128)(2,1)S(1)}, u32[]{:S(2)}, u32[]{:S(2)}) collective-permute-start(bf16[176,128]{1,0:T(8,128)(2,1)S(1)} %get-tuple-element.66), channel_id=1, source_target_pairs={{0,8},{4,12},{8,0},{12,4},{16,24},{20,28},{24,16},{28,20},{1,9},{5... | collective-permute-start | bytes 135176 | tf_op jit(solution)/shard_map/ppermute | solution.py:356
  31.8 0.9 %collective-permute-start.16 = (bf16[176,128]{1,0:T(8,128)(2,1)S(1)}, bf16[176,128]{1,0:T(8,128)(2,1)S(1)}, u32[]{:S(2)}, u32[]{:S(2)}) collective-permute-start(bf16[176,128]{1,0:T(8,128)(2,1)S(1)} %get-tuple-element.67), channel_id=1, source_target_pairs={{0,4},{4,0},{8,12},{12,8},{16,20},{20,16},{24,28},{28,24},{1,5},{5... | collective-permute-start | bytes 135176 | tf_op jit(solution)/shard_map/ppermute | solution.py:356
  32.7 2.2 %shard_map.112 = (bf16[2,1,64,320]{3,2,1,0:T(8,128)(2,1)}, bf16[2,1,64,320]{3,2,1,0:T(8,128)(2,1)}, bf16[2,1,64,320]{3,2,1,0:T(8,128)(2,1)}, bf16[2,1,64,320]{3,2,1,0:T(8,128)(2,1)}) custom-call(bf16[640,128]{1,0:T(8,128)(2,1)S(1)} %get-tuple-element.49.refs_0_, bf16[640,128]{1,0:T(8,128)(2,1)S(1)} %collective-permute-done.2.refs_1_, ...), custom_call_target="tpu_custom_call" | custom-call | bytes 2232320 | tf_op jit(solution)/shard_map/pallas_call | solution.py:27
  35.1 0.7 %collective-permute-done.16.refs_7_ = bf16[176,128]{1,0:T(8,128)(2,1)S(1)} collective-permute-done((bf16[176,128]{1,0:T(8,128)(2,1)S(1)}, bf16[176,128]{1,0:T(8,128)(2,1)S(1)}, u32[]{:S(2)}, u32[]{:S(2)}) %collective-permute-start.16) | collective-permute-done | bytes 45088 | tf_op jit(solution)/shard_map/ppermute | solution.py:356
  35.8 0.7 %shard_map.117 = (f32[115,128]{1,0:T(8,128)}, f32[60,128]{1,0:T(8,128)}) custom-call(f32[176,128]{1,0:T(8,128)S(1)} %get-tuple-element.60.refs_0_, bf16[176,128]{1,0:T(8,128)(2,1)S(1)} %collective-permute-done.10.refs_1_, bf16[176,128]{1,0:T(8,128)(2,1)S(1)} %collective-permute-done.11.refs_2_, bf16[176,128]{1,0:T(8,128)(2,1)S(1)} %collective-permute-done.12.refs_3_, ...), custom_call_target="tpu_custom_call" | custom-call | bytes 495104 | tf_op jit(solution)/shard_map/pallas_call | solution.py:27
  (27 shorter events, 1.5 us)
Async XLA Ops:
  1.7 10.0 %collective-permute-start = (bf16[128,640]{1,0:T(8,128)(2,1)S(1)}, bf16[128,640]{1,0:T(8,128)(2,1)S(1)}, u32[]{:S(2)}, u32[]{:S(2)}) collective-permute-start(bf16[128,640]{1,0:T(8,128)(2,1)S(1)} %shard_map.109.own.refs_0_), channel_id=1, source_target_pairs={{0,4},{4,0},{8,12},{12,8},{16,20},{20,16},{24,28},{28,24},{1,5},{5... | collective-permute-start | bytes 491528 | tf_op jit(solution)/shard_map/ppermute | solution.py:381
  4.8 7.0 %collective-permute-start.1 = (bf16[128,640]{1,0:T(8,128)(2,1)S(1)}, bf16[128,640]{1,0:T(8,128)(2,1)S(1)}, u32[]{:S(2)}, u32[]{:S(2)}) collective-permute-start(bf16[128,640]{1,0:T(8,128)(2,1)S(1)} %shard_map.109.own.refs_0_), channel_id=1, source_target_pairs={{4,8},{8,4},{12,16},{16,12},{20,24},{24,20},{5,9},{9,5},{13,17},{1... | collective-permute-start | bytes 491528 | tf_op jit(solution)/shard_map/ppermute | solution.py:381
  5.4 8.4 %collective-permute-start.6 = (bf16[128,640]{1,0:T(8,128)(2,1)S(1)}, bf16[128,640]{1,0:T(8,128)(2,1)S(1)}, u32[]{:S(2)}, u32[]{:S(2)}) collective-permute-start(bf16[128,640]{1,0:T(8,128)(2,1)S(1)} %shard_map.109.own.refs_0_), channel_id=1, source_target_pairs={{0,2},{1,3},{2,0},{3,1},{4,6},{5,7},{6,4},{7,5},{8,10},{9,11},{10,... | collective-permute-start | bytes 491528 | tf_op jit(solution)/shard_map/ppermute | solution.py:356
  12.3 5.4 %collective-permute-start.3 = (bf16[640,128]{1,0:T(8,128)(2,1)S(1)}, bf16[640,128]{1,0:T(8,128)(2,1)S(1)}, u32[]{:S(2)}, u32[]{:S(2)}) collective-permute-start(bf16[640,128]{1,0:T(8,128)(2,1)S(1)} %get-tuple-element.49.refs_0_), channel_id=1, source_target_pairs={{0,2},{1,3},{2,0},{3,1},{4,6},{5,7},{6,4},{7,5},{8,10},{9,11},{10,... | collective-permute-start | bytes 491528 | tf_op jit(solution)/shard_map/ppermute | solution.py:356
  14.3 1.4 %collective-permute-start.8 = (bf16[6,64,128]{2,1,0:T(8,128)(2,1)S(1)}, bf16[6,64,128]{2,1,0:T(8,128)(2,1)S(1)}, u32[]{:S(2)}, u32[]{:S(2)}) collective-permute-start(bf16[6,64,128]{2,1,0:T(8,128)(2,1)S(1)} %get-tuple-element.59), channel_id=1, source_target_pairs={{0,1},{1,0},{2,3},{3,2},{4,5},{5,4},{6,7},{7,6},{8,9},{9,8},{10,11... | collective-permute-start | bytes 294920 | tf_op jit(solution)/shard_map/ppermute | solution.py:356
  14.4 3.9 %collective-permute-start.2 = (bf16[640,128]{1,0:T(8,128)(2,1)S(1)}, bf16[640,128]{1,0:T(8,128)(2,1)S(1)}, u32[]{:S(2)}, u32[]{:S(2)}) collective-permute-start(bf16[640,128]{1,0:T(8,128)(2,1)S(1)} %get-tuple-element.49.refs_0_), channel_id=1, source_target_pairs={{0,1},{1,0},{2,3},{3,2},{4,5},{5,4},{6,7},{7,6},{8,9},{9,8},{10,11... | collective-permute-start | bytes 491528 | tf_op jit(solution)/shard_map/ppermute | solution.py:356
  14.9 5.6 %collective-permute-start.7 = (bf16[8,64,128]{2,1,0:T(8,128)(2,1)S(1)}, bf16[8,64,128]{2,1,0:T(8,128)(2,1)S(1)}, u32[]{:S(2)}, u32[]{:S(2)}) collective-permute-start(bf16[8,64,128]{2,1,0:T(8,128)(2,1)S(1)} %get-tuple-element.57), channel_id=1, source_target_pairs={{0,1},{1,0},{2,3},{3,2},{4,5},{5,4},{6,7},{7,6},{8,9},{9,8},{10,11... | collective-permute-start | bytes 393224 | tf_op jit(solution)/shard_map/ppermute | solution.py:356
  15.7 17.0 %copy-start = (bf16[3,3,2,160,160]{4,3,2,1,0:T(8,128)(2,1)S(1)}, bf16[3,3,2,160,160]{4,3,2,1,0:T(8,128)(2,1)}, u32[]{:S(2)}) copy-start(bf16[3,3,2,160,160]{4,3,2,1,0:T(8,128)(2,1)} %refs_9_.1) | copy-start | bytes 2764804
  15.7 16.9 %copy-start.1 = (bf16[2,1,64,320]{3,2,1,0:T(8,128)(2,1)S(1)}, bf16[2,1,64,320]{3,2,1,0:T(8,128)(2,1)}, u32[]{:S(2)}) copy-start(bf16[2,1,64,320]{3,2,1,0:T(8,128)(2,1)} %refs_5_.1) | copy-start | bytes 245764
  15.7 16.9 %copy-start.2 = (bf16[2,1,64,320]{3,2,1,0:T(8,128)(2,1)S(1)}, bf16[2,1,64,320]{3,2,1,0:T(8,128)(2,1)}, u32[]{:S(2)}) copy-start(bf16[2,1,64,320]{3,2,1,0:T(8,128)(2,1)} %refs_6_.1) | copy-start | bytes 245764
  15.7 4.9 %collective-permute-start.9 = (bf16[6,64,128]{2,1,0:T(8,128)(2,1)S(1)}, bf16[6,64,128]{2,1,0:T(8,128)(2,1)S(1)}, u32[]{:S(2)}, u32[]{:S(2)}) collective-permute-start(bf16[6,64,128]{2,1,0:T(8,128)(2,1)S(1)} %shard_map.115), channel_id=1, source_target_pairs={{0,2},{1,3},{2,0},{3,1},{4,6},{5,7},{6,4},{7,5},{8,10},{9,11},{10,... | collective-permute-start | bytes 294920 | tf_op jit(solution)/shard_map/ppermute | solution.py:356
  17.7 1.3 %collective-permute-start.5 = (bf16[320,128]{1,0:T(8,128)(2,1)S(1)}, bf16[320,128]{1,0:T(8,128)(2,1)S(1)}, u32[]{:S(2)}, u32[]{:S(2)}) collective-permute-start(bf16[320,128]{1,0:T(8,128)(2,1)S(1)} %get-tuple-element.70), channel_id=1, source_target_pairs={{0,1},{1,0},{2,3},{3,2},{4,5},{5,4},{6,7},{7,6},{8,9},{9,8},{10,11... | collective-permute-start | bytes 245768 | tf_op jit(solution)/shard_map/ppermute | solution.py:356
  17.8 1.4 %collective-permute-start.4 = (bf16[320,128]{1,0:T(8,128)(2,1)S(1)}, bf16[320,128]{1,0:T(8,128)(2,1)S(1)}, u32[]{:S(2)}, u32[]{:S(2)}) collective-permute-start(bf16[320,128]{1,0:T(8,128)(2,1)S(1)} %get-tuple-element.71), channel_id=1, source_target_pairs={{0,1},{1,0},{2,3},{3,2},{4,5},{5,4},{6,7},{7,6},{8,9},{9,8},{10,11... | collective-permute-start | bytes 245768 | tf_op jit(solution)/shard_map/ppermute | solution.py:356
  20.7 10.3 %collective-permute-start.10 = (bf16[176,128]{1,0:T(8,128)(2,1)S(1)}, bf16[176,128]{1,0:T(8,128)(2,1)S(1)}, u32[]{:S(2)}, u32[]{:S(2)}) collective-permute-start(bf16[176,128]{1,0:T(8,128)(2,1)S(1)} %get-tuple-element.61), channel_id=1, source_target_pairs={{0,24},{4,28},{8,16},{12,20},{16,8},{20,12},{24,0},{28,4},{1,25},{... | collective-permute-start | bytes 135176 | tf_op jit(solution)/shard_map/ppermute | solution.py:356
  25.8 6.0 %collective-permute-start.11 = (bf16[176,128]{1,0:T(8,128)(2,1)S(1)}, bf16[176,128]{1,0:T(8,128)(2,1)S(1)}, u32[]{:S(2)}, u32[]{:S(2)}) collective-permute-start(bf16[176,128]{1,0:T(8,128)(2,1)S(1)} %get-tuple-element.62), channel_id=1, source_target_pairs={{0,16},{4,20},{8,24},{12,28},{16,0},{20,4},{24,8},{28,12},{1,17},{... | collective-permute-start | bytes 135176 | tf_op jit(solution)/shard_map/ppermute | solution.py:356
  25.8 9.0 %collective-permute-start.12 = (bf16[176,128]{1,0:T(8,128)(2,1)S(1)}, bf16[176,128]{1,0:T(8,128)(2,1)S(1)}, u32[]{:S(2)}, u32[]{:S(2)}) collective-permute-start(bf16[176,128]{1,0:T(8,128)(2,1)S(1)} %get-tuple-element.63), channel_id=1, source_target_pairs={{0,28},{4,24},{8,20},{12,16},{16,12},{20,8},{24,4},{28,0},{1,29},{... | collective-permute-start | bytes 135176 | tf_op jit(solution)/shard_map/ppermute | solution.py:356
  28.2 6.6 %collective-permute-start.13 = (bf16[176,128]{1,0:T(8,128)(2,1)S(1)}, bf16[176,128]{1,0:T(8,128)(2,1)S(1)}, u32[]{:S(2)}, u32[]{:S(2)}) collective-permute-start(bf16[176,128]{1,0:T(8,128)(2,1)S(1)} %get-tuple-element.64), channel_id=1, source_target_pairs={{0,20},{4,16},{8,28},{12,24},{16,4},{20,0},{24,12},{28,8},{1,21},{... | collective-permute-start | bytes 135176 | tf_op jit(solution)/shard_map/ppermute | solution.py:356
  28.8 6.1 %collective-permute-start.14 = (bf16[176,128]{1,0:T(8,128)(2,1)S(1)}, bf16[176,128]{1,0:T(8,128)(2,1)S(1)}, u32[]{:S(2)}, u32[]{:S(2)}) collective-permute-start(bf16[176,128]{1,0:T(8,128)(2,1)S(1)} %get-tuple-element.65), channel_id=1, source_target_pairs={{0,12},{4,8},{8,4},{12,0},{16,28},{20,24},{24,20},{28,16},{1,13},{... | collective-permute-start | bytes 135176 | tf_op jit(solution)/shard_map/ppermute | solution.py:356
  31.0 4.1 %collective-permute-start.15 = (bf16[176,128]{1,0:T(8,128)(2,1)S(1)}, bf16[176,128]{1,0:T(8,128)(2,1)S(1)}, u32[]{:S(2)}, u32[]{:S(2)}) collective-permute-start(bf16[176,128]{1,0:T(8,128)(2,1)S(1)} %get-tuple-element.66), channel_id=1, source_target_pairs={{0,8},{4,12},{8,0},{12,4},{16,24},{20,28},{24,16},{28,20},{1,9},{5... | collective-permute-start | bytes 135176 | tf_op jit(solution)/shard_map/ppermute | solution.py:356
  31.8 4.0 %collective-permute-start.16 = (bf16[176,128]{1,0:T(8,128)(2,1)S(1)}, bf16[176,128]{1,0:T(8,128)(2,1)S(1)}, u32[]{:S(2)}, u32[]{:S(2)}) collective-permute-start(bf16[176,128]{1,0:T(8,128)(2,1)S(1)} %get-tuple-element.67), channel_id=1, source_target_pairs={{0,4},{4,0},{8,12},{12,8},{16,20},{20,16},{24,28},{28,24},{1,5},{5... | collective-permute-start | bytes 135176 | tf_op jit(solution)/shard_map/ppermute | solution.py:356

commit v7 on v6

--- a/solution.py
+++ b/solution.py
@@ -304,16 +304,17 @@
     space_terms(slots, rows_ref, LANES // 2, store)
 
 
-def final_body(factor, stride, *refs):
+def final_body(factor, stride, short, *refs):
     (mine, *came), (space_out, time_out) = refs[:-2], refs[-2:]
     total = mine[...]
     for ref in came:
         total = total + ref[...].astype(F32)
     total = total * factor
-    first, short = time_out.shape[0], space_out.shape[0] // stride
+    first, held = time_out.shape[0], space_out.shape[0] // stride
     time_out[...] = total[:first]
     for j in range(stride):
-        space_out[pl.ds(j, short, stride=stride), :] = total[first + j * short : first + (j + 1) * short]
+        at = first + j * short
+        space_out[pl.ds(j, held, stride=stride), :] = total[at : at + held]
 
 
 def space_body(count, *refs):
@@ -442,8 +443,10 @@
     if even:
         rows = space_rows // devices
         period, layout = segments(width)
-        full = -(-rows // period) * len(layout)
-        deep = round_up(time_rows // devices + full, 16)
+        short = -(-rows // period)
+        held_rows = round_up(short, 8)
+        full = short * len(layout)
+        deep = round_up(time_rows // devices + full - short + held_rows, 16)
         piece = (deep, LANES)
         scratch = (round_up(space_rows + 8 * period + rows, 8), LANES)
         pieces = on_device(
@@ -460,9 +463,12 @@
         order = sorted(range(1, steps), key=lambda k: (k < steps // 2, k >= steps // 2 and k & 1, -k))
         arrived = [swap(sends[k - 1], "tm", k) for k in order]
         space_share, time_share = on_device(
-            functools.partial(final_body, factor, len(layout)),
+            functools.partial(final_body, factor, len(layout), short),
             (mine, *arrived),
-            [shape((full, LANES), F32), shape((time_rows // devices, time_width), F32)],
+            [
+                shape((held_rows * len(layout), LANES), F32),
+                shape((time_rows // devices, time_width), F32),
+            ],
         )
         space_share = space_share.reshape(-1)[: rows * width]
         time_share = time_share.reshape(-1)

time: 36.7 us -> 36.7 us (level)
  no operation moved by 1% of the time
where the time goes in v7:
time: 36.7 us; the launch traced here: 36.5 us
  starting transfers between devices  20.4 us (56%)
  Pallas kernels  7.8 us (21%)
  waiting for transfers between devices  7.49 us (20%)
  between operations  0.76 us (2%)
    ppermute x15, starting transfers between devices, swap(): lax.ppermute(x, axis, [(i, i ^ bit) for i in range(lax.axis_size(axis))])  16.7 us
    pallas_call x9, Pallas kernels, on_device(): pl.pallas_call(body, out_shape=outs, in_specs=[pl.BlockSpec(memory_space=...  7.8 us
    ppermute x15, waiting for transfers between devices, swap(): lax.ppermute(x, axis, [(i, i ^ bit) for i in range(lax.axis_size(axis))])  4.24 us
    ppermute x2, starting transfers between devices, neighbours(): lax.ppermute(x, axis, [p for i in lower for p in ((i, i + 1), (i + 1, i))])  3.69 us
    ppermute x2, waiting for transfers between devices, neighbours(): lax.ppermute(x, axis, [p for i in lower for p in ((i, i + 1), (i + 1, i))])  3.26 us
  transfers between devices with their start and end apart: 17, of which 10 were waited for; matrix products, arithmetic and copies ran while one was open for 0% of the time, Pallas kernels for 16%

profile of v7, /device:TPU:0, one launch (start us, length us, event | category | flops | bytes accessed | tf_op | source)
XLA Modules:
  0.0 36.5 jit_solution(5778101519854243234)
XLA Ops:
  0.6 1.1 %shard_map.109.own.refs_0_ = bf16[128,640]{1,0:T(8,128)(2,1)S(1)} custom-call(bf16[2,1,64,320]{3,2,1,0:T(8,128)(2,1)} %refs_5_.1, bf16[2,1,64,320]{3,2,1,0:T(8,128)(2,1)} %refs_6_.1), custom_call_target="tpu_custom_call" | custom-call | bytes 327680 | tf_op jit(solution)/shard_map/pallas_call | solution.py:27
  1.7 3.0 %collective-permute-start = (bf16[128,640]{1,0:T(8,128)(2,1)S(1)}, bf16[128,640]{1,0:T(8,128)(2,1)S(1)}, u32[]{:S(2)}, u32[]{:S(2)}) collective-permute-start(bf16[128,640]{1,0:T(8,128)(2,1)S(1)} %shard_map.109.own.refs_0_), channel_id=1, source_target_pairs={{0,4},{4,0},{8,12},{12,8},{16,20},{20,16},{24,28},{28,24},{1,5},{5... | collective-permute-start | bytes 491528 | tf_op jit(solution)/shard_map/ppermute | solution.py:382
  4.8 0.7 %collective-permute-start.1 = (bf16[128,640]{1,0:T(8,128)(2,1)S(1)}, bf16[128,640]{1,0:T(8,128)(2,1)S(1)}, u32[]{:S(2)}, u32[]{:S(2)}) collective-permute-start(bf16[128,640]{1,0:T(8,128)(2,1)S(1)} %shard_map.109.own.refs_0_), channel_id=1, source_target_pairs={{4,8},{8,4},{12,16},{16,12},{20,24},{24,20},{5,9},{9,5},{13,17},{1... | collective-permute-start | bytes 491528 | tf_op jit(solution)/shard_map/ppermute | solution.py:382
  5.4 1.6 %collective-permute-start.6 = (bf16[128,640]{1,0:T(8,128)(2,1)S(1)}, bf16[128,640]{1,0:T(8,128)(2,1)S(1)}, u32[]{:S(2)}, u32[]{:S(2)}) collective-permute-start(bf16[128,640]{1,0:T(8,128)(2,1)S(1)} %shard_map.109.own.refs_0_), channel_id=1, source_target_pairs={{0,2},{1,3},{2,0},{3,1},{4,6},{5,7},{6,4},{7,5},{8,10},{9,11},{10,... | collective-permute-start | bytes 491528 | tf_op jit(solution)/shard_map/ppermute | solution.py:357
  7.0 1.5 %shard_map.110 = (f32[64,640]{1,0:T(8,128)S(1)}, f32[64,640]{1,0:T(8,128)S(1)}, f32[64,640]{1,0:T(8,128)S(1)}, bf16[2,2,64,320]{3,2,1,0:T(8,128)(2,1)S(1)}, bf16[3,5,128,128]{3,2,1,0:T(8,128)(2,1)S(1)}) custom-call(bf16[2,1,64,320]{3,2,1,0:T(8,128)(2,1)} %refs_5_.1, bf16[2,1,64,320]{3,2,1,0:T(8,128)(2,1)} %y2_far.1, bf16[2,1,64,320]{3,2,1,0:T(8,128)(2,1)} %c1_far.1, ...), custom_call_target="tpu_custom_call" | custom-call | bytes 2048000 | tf_op jit(solution)/shard_map/pallas_call | solution.py:27
  8.5 3.3 %collective-permute-done.near = bf16[128,640]{1,0:T(8,128)(2,1)S(1)} collective-permute-done((bf16[128,640]{1,0:T(8,128)(2,1)S(1)}, bf16[128,640]{1,0:T(8,128)(2,1)S(1)}, u32[]{:S(2)}, u32[]{:S(2)}) %collective-permute-start) | collective-permute-done | bytes 163872 | tf_op jit(solution)/shard_map/ppermute | solution.py:382
  11.8 0.5 %shard_map.111 = (bf16[2,1,64,320]{3,2,1,0:T(8,128)(2,1)S(1)}, bf16[2,1,64,320]{3,2,1,0:T(8,128)(2,1)S(1)}, bf16[640,128]{1,0:T(8,128)(2,1)S(1)}) custom-call(bf16[128,640]{1,0:T(8,128)(2,1)S(1)} %collective-permute-done.near, bf16[64,640]{1,0:T(8,128)(2,1)S(1)} %slice.12.near_cot, bf16[128,640]{1,0:T(8,128)(2,1)S(1)} %collective-permute-done.1.far, ...), custom_call_target="tpu_custom_call" | custom-call | bytes 1884160 | tf_op jit(solution)/shard_map/pallas_call | solution.py:27
  12.3 1.6 %collective-permute-start.3 = (bf16[640,128]{1,0:T(8,128)(2,1)S(1)}, bf16[640,128]{1,0:T(8,128)(2,1)S(1)}, u32[]{:S(2)}, u32[]{:S(2)}) collective-permute-start(bf16[640,128]{1,0:T(8,128)(2,1)S(1)} %get-tuple-element.49.refs_0_), channel_id=1, source_target_pairs={{0,2},{1,3},{2,0},{3,1},{4,6},{5,7},{6,4},{7,5},{8,10},{9,11},{10,... | collective-permute-start | bytes 491528 | tf_op jit(solution)/shard_map/ppermute | solution.py:357
  14.4 0.5 %collective-permute-start.2 = (bf16[640,128]{1,0:T(8,128)(2,1)S(1)}, bf16[640,128]{1,0:T(8,128)(2,1)S(1)}, u32[]{:S(2)}, u32[]{:S(2)}) collective-permute-start(bf16[640,128]{1,0:T(8,128)(2,1)S(1)} %get-tuple-element.49.refs_0_), channel_id=1, source_target_pairs={{0,1},{1,0},{2,3},{3,2},{4,5},{5,4},{6,7},{7,6},{8,9},{9,8},{10,11... | collective-permute-start | bytes 491528 | tf_op jit(solution)/shard_map/ppermute | solution.py:357
  14.9 0.7 %collective-permute-done.8.came = bf16[6,64,128]{2,1,0:T(8,128)(2,1)S(1)} collective-permute-done((bf16[6,64,128]{2,1,0:T(8,128)(2,1)S(1)}, bf16[6,64,128]{2,1,0:T(8,128)(2,1)S(1)}, u32[]{:S(2)}, u32[]{:S(2)}) %collective-permute-start.8) | collective-permute-done | bytes 98336 | tf_op jit(solution)/shard_map/ppermute | solution.py:357
  15.7 0.6 %collective-permute-start.9 = (bf16[6,64,128]{2,1,0:T(8,128)(2,1)S(1)}, bf16[6,64,128]{2,1,0:T(8,128)(2,1)S(1)}, u32[]{:S(2)}, u32[]{:S(2)}) collective-permute-start(bf16[6,64,128]{2,1,0:T(8,128)(2,1)S(1)} %shard_map.115), channel_id=1, source_target_pairs={{0,2},{1,3},{2,0},{3,1},{4,6},{5,7},{6,4},{7,5},{8,10},{9,11},{10,... | collective-permute-start | bytes 294920 | tf_op jit(solution)/shard_map/ppermute | solution.py:357
  16.3 1.4 %collective-permute-done.3.refs_2_ = bf16[640,128]{1,0:T(8,128)(2,1)S(1)} collective-permute-done((bf16[640,128]{1,0:T(8,128)(2,1)S(1)}, bf16[640,128]{1,0:T(8,128)(2,1)S(1)}, u32[]{:S(2)}, u32[]{:S(2)}) %collective-permute-start.3) | collective-permute-done | bytes 163872 | tf_op jit(solution)/shard_map/ppermute | solution.py:357
  17.8 0.5 %collective-permute-start.4 = (bf16[320,128]{1,0:T(8,128)(2,1)S(1)}, bf16[320,128]{1,0:T(8,128)(2,1)S(1)}, u32[]{:S(2)}, u32[]{:S(2)}) collective-permute-start(bf16[320,128]{1,0:T(8,128)(2,1)S(1)} %get-tuple-element.71), channel_id=1, source_target_pairs={{0,1},{1,0},{2,3},{3,2},{4,5},{5,4},{6,7},{7,6},{8,9},{9,8},{10,11... | collective-permute-start | bytes 245768 | tf_op jit(solution)/shard_map/ppermute | solution.py:357
  18.3 0.8 %collective-permute-done.5.refs_4_ = bf16[320,128]{1,0:T(8,128)(2,1)S(1)} collective-permute-done((bf16[320,128]{1,0:T(8,128)(2,1)S(1)}, bf16[320,128]{1,0:T(8,128)(2,1)S(1)}, u32[]{:S(2)}, u32[]{:S(2)}) %collective-permute-start.5) | collective-permute-done | bytes 81952 | tf_op jit(solution)/shard_map/ppermute | solution.py:357
  19.2 1.3 %shard_map.113.pieces = f32[8,176,128]{2,1,0:T(8,128)S(1)} custom-call(bf16[640,128]{1,0:T(8,128)(2,1)S(1)} %get-tuple-element.49.refs_0_, bf16[640,128]{1,0:T(8,128)(2,1)S(1)} %collective-permute-done.2.refs_1_, bf16[640,128]{1,0:T(8,128)(2,1)S(1)} %collective-permute-done.3.refs_2_, bf16[320,128]{1,0:T(8,128)(2,1)S(1)} %collective-permute-done.4.refs_3_, ...), custom_call_target="tpu_custom_call" | custom-call | bytes 1376256 | tf_op jit(solution)/shard_map/pallas_call | solution.py:27
  20.7 5.1 %collective-permute-start.10 = (bf16[176,128]{1,0:T(8,128)(2,1)S(1)}, bf16[176,128]{1,0:T(8,128)(2,1)S(1)}, u32[]{:S(2)}, u32[]{:S(2)}) collective-permute-start(bf16[176,128]{1,0:T(8,128)(2,1)S(1)} %get-tuple-element.61), channel_id=1, source_target_pairs={{0,24},{4,28},{8,16},{12,20},{16,8},{20,12},{24,0},{28,4},{1,25},{... | collective-permute-start | bytes 135176 | tf_op jit(solution)/shard_map/ppermute | solution.py:357
  25.8 2.4 %collective-permute-start.12 = (bf16[176,128]{1,0:T(8,128)(2,1)S(1)}, bf16[176,128]{1,0:T(8,128)(2,1)S(1)}, u32[]{:S(2)}, u32[]{:S(2)}) collective-permute-start(bf16[176,128]{1,0:T(8,128)(2,1)S(1)} %get-tuple-element.63), channel_id=1, source_target_pairs={{0,28},{4,24},{8,20},{12,16},{16,12},{20,8},{24,4},{28,0},{1,29},{... | collective-permute-start | bytes 135176 | tf_op jit(solution)/shard_map/ppermute | solution.py:357
  28.2 0.6 %collective-permute-start.13 = (bf16[176,128]{1,0:T(8,128)(2,1)S(1)}, bf16[176,128]{1,0:T(8,128)(2,1)S(1)}, u32[]{:S(2)}, u32[]{:S(2)}) collective-permute-start(bf16[176,128]{1,0:T(8,128)(2,1)S(1)} %get-tuple-element.64), channel_id=1, source_target_pairs={{0,20},{4,16},{8,28},{12,24},{16,4},{20,0},{24,12},{28,8},{1,21},{... | collective-permute-start | bytes 135176 | tf_op jit(solution)/shard_map/ppermute | solution.py:357
  28.8 2.2 %collective-permute-start.14 = (bf16[176,128]{1,0:T(8,128)(2,1)S(1)}, bf16[176,128]{1,0:T(8,128)(2,1)S(1)}, u32[]{:S(2)}, u32[]{:S(2)}) collective-permute-start(bf16[176,128]{1,0:T(8,128)(2,1)S(1)} %get-tuple-element.65), channel_id=1, source_target_pairs={{0,12},{4,8},{8,4},{12,0},{16,28},{20,24},{24,20},{28,16},{1,13},{... | collective-permute-start | bytes 135176 | tf_op jit(solution)/shard_map/ppermute | solution.py:357
  31.0 0.6 %collective-permute-start.15 = (bf16[176,128]{1,0:T(8,128)(2,1)S(1)}, bf16[176,128]{1,0:T(8,128)(2,1)S(1)}, u32[]{:S(2)}, u32[]{:S(2)}) collective-permute-start(bf16[176,128]{1,0:T(8,128)(2,1)S(1)} %get-tuple-element.66), channel_id=1, source_target_pairs={{0,8},{4,12},{8,0},{12,4},{16,24},{20,28},{24,16},{28,20},{1,9},{5... | collective-permute-start | bytes 135176 | tf_op jit(solution)/shard_map/ppermute | solution.py:357
  31.8 0.9 %collective-permute-start.16 = (bf16[176,128]{1,0:T(8,128)(2,1)S(1)}, bf16[176,128]{1,0:T(8,128)(2,1)S(1)}, u32[]{:S(2)}, u32[]{:S(2)}) collective-permute-start(bf16[176,128]{1,0:T(8,128)(2,1)S(1)} %get-tuple-element.67), channel_id=1, source_target_pairs={{0,4},{4,0},{8,12},{12,8},{16,20},{20,16},{24,28},{28,24},{1,5},{5... | collective-permute-start | bytes 135176 | tf_op jit(solution)/shard_map/ppermute | solution.py:357
  32.7 2.2 %shard_map.112 = (bf16[2,1,64,320]{3,2,1,0:T(8,128)(2,1)}, bf16[2,1,64,320]{3,2,1,0:T(8,128)(2,1)}, bf16[2,1,64,320]{3,2,1,0:T(8,128)(2,1)}, bf16[2,1,64,320]{3,2,1,0:T(8,128)(2,1)}) custom-call(bf16[640,128]{1,0:T(8,128)(2,1)S(1)} %get-tuple-element.49.refs_0_, bf16[640,128]{1,0:T(8,128)(2,1)S(1)} %collective-permute-done.2.refs_1_, ...), custom_call_target="tpu_custom_call" | custom-call | bytes 2232320 | tf_op jit(solution)/shard_map/pallas_call | solution.py:27
  35.1 0.7 %collective-permute-done.16.refs_7_ = bf16[176,128]{1,0:T(8,128)(2,1)S(1)} collective-permute-done((bf16[176,128]{1,0:T(8,128)(2,1)S(1)}, bf16[176,128]{1,0:T(8,128)(2,1)S(1)}, u32[]{:S(2)}, u32[]{:S(2)}) %collective-permute-start.16) | collective-permute-done | bytes 45088 | tf_op jit(solution)/shard_map/ppermute | solution.py:357
  35.8 0.7 %shard_map.117 = (f32[120,128]{1,0:T(8,128)}, f32[60,128]{1,0:T(8,128)}) custom-call(f32[176,128]{1,0:T(8,128)S(1)} %get-tuple-element.60.refs_0_, bf16[176,128]{1,0:T(8,128)(2,1)S(1)} %collective-permute-done.10.refs_1_, bf16[176,128]{1,0:T(8,128)(2,1)S(1)} %collective-permute-done.11.refs_2_, bf16[176,128]{1,0:T(8,128)(2,1)S(1)} %collective-permute-done.12.refs_3_, ...), custom_call_target="tpu_custom_call" | custom-call | bytes 497664 | tf_op jit(solution)/shard_map/pallas_call | solution.py:27
  (27 shorter events, 1.5 us)
Async XLA Ops:
  1.7 10.0 %collective-permute-start = (bf16[128,640]{1,0:T(8,128)(2,1)S(1)}, bf16[128,640]{1,0:T(8,128)(2,1)S(1)}, u32[]{:S(2)}, u32[]{:S(2)}) collective-permute-start(bf16[128,640]{1,0:T(8,128)(2,1)S(1)} %shard_map.109.own.refs_0_), channel_id=1, source_target_pairs={{0,4},{4,0},{8,12},{12,8},{16,20},{20,16},{24,28},{28,24},{1,5},{5... | collective-permute-start | bytes 491528 | tf_op jit(solution)/shard_map/ppermute | solution.py:382
  4.8 7.0 %collective-permute-start.1 = (bf16[128,640]{1,0:T(8,128)(2,1)S(1)}, bf16[128,640]{1,0:T(8,128)(2,1)S(1)}, u32[]{:S(2)}, u32[]{:S(2)}) collective-permute-start(bf16[128,640]{1,0:T(8,128)(2,1)S(1)} %shard_map.109.own.refs_0_), channel_id=1, source_target_pairs={{4,8},{8,4},{12,16},{16,12},{20,24},{24,20},{5,9},{9,5},{13,17},{1... | collective-permute-start | bytes 491528 | tf_op jit(solution)/shard_map/ppermute | solution.py:382
  5.4 8.4 %collective-permute-start.6 = (bf16[128,640]{1,0:T(8,128)(2,1)S(1)}, bf16[128,640]{1,0:T(8,128)(2,1)S(1)}, u32[]{:S(2)}, u32[]{:S(2)}) collective-permute-start(bf16[128,640]{1,0:T(8,128)(2,1)S(1)} %shard_map.109.own.refs_0_), channel_id=1, source_target_pairs={{0,2},{1,3},{2,0},{3,1},{4,6},{5,7},{6,4},{7,5},{8,10},{9,11},{10,... | collective-permute-start | bytes 491528 | tf_op jit(solution)/shard_map/ppermute | solution.py:357
  12.3 5.4 %collective-permute-start.3 = (bf16[640,128]{1,0:T(8,128)(2,1)S(1)}, bf16[640,128]{1,0:T(8,128)(2,1)S(1)}, u32[]{:S(2)}, u32[]{:S(2)}) collective-permute-start(bf16[640,128]{1,0:T(8,128)(2,1)S(1)} %get-tuple-element.49.refs_0_), channel_id=1, source_target_pairs={{0,2},{1,3},{2,0},{3,1},{4,6},{5,7},{6,4},{7,5},{8,10},{9,11},{10,... | collective-permute-start | bytes 491528 | tf_op jit(solution)/shard_map/ppermute | solution.py:357
  14.3 1.4 %collective-permute-start.8 = (bf16[6,64,128]{2,1,0:T(8,128)(2,1)S(1)}, bf16[6,64,128]{2,1,0:T(8,128)(2,1)S(1)}, u32[]{:S(2)}, u32[]{:S(2)}) collective-permute-start(bf16[6,64,128]{2,1,0:T(8,128)(2,1)S(1)} %get-tuple-element.59), channel_id=1, source_target_pairs={{0,1},{1,0},{2,3},{3,2},{4,5},{5,4},{6,7},{7,6},{8,9},{9,8},{10,11... | collective-permute-start | bytes 294920 | tf_op jit(solution)/shard_map/ppermute | solution.py:357
  14.4 3.9 %collective-permute-start.2 = (bf16[640,128]{1,0:T(8,128)(2,1)S(1)}, bf16[640,128]{1,0:T(8,128)(2,1)S(1)}, u32[]{:S(2)}, u32[]{:S(2)}) collective-permute-start(bf16[640,128]{1,0:T(8,128)(2,1)S(1)} %get-tuple-element.49.refs_0_), channel_id=1, source_target_pairs={{0,1},{1,0},{2,3},{3,2},{4,5},{5,4},{6,7},{7,6},{8,9},{9,8},{10,11... | collective-permute-start | bytes 491528 | tf_op jit(solution)/shard_map/ppermute | solution.py:357
  14.9 5.6 %collective-permute-start.7 = (bf16[8,64,128]{2,1,0:T(8,128)(2,1)S(1)}, bf16[8,64,128]{2,1,0:T(8,128)(2,1)S(1)}, u32[]{:S(2)}, u32[]{:S(2)}) collective-permute-start(bf16[8,64,128]{2,1,0:T(8,128)(2,1)S(1)} %get-tuple-element.57), channel_id=1, source_target_pairs={{0,1},{1,0},{2,3},{3,2},{4,5},{5,4},{6,7},{7,6},{8,9},{9,8},{10,11... | collective-permute-start | bytes 393224 | tf_op jit(solution)/shard_map/ppermute | solution.py:357
  15.7 17.0 %copy-start = (bf16[3,3,2,160,160]{4,3,2,1,0:T(8,128)(2,1)S(1)}, bf16[3,3,2,160,160]{4,3,2,1,0:T(8,128)(2,1)}, u32[]{:S(2)}) copy-start(bf16[3,3,2,160,160]{4,3,2,1,0:T(8,128)(2,1)} %refs_9_.1) | copy-start | bytes 2764804
  15.7 16.9 %copy-start.1 = (bf16[2,1,64,320]{3,2,1,0:T(8,128)(2,1)S(1)}, bf16[2,1,64,320]{3,2,1,0:T(8,128)(2,1)}, u32[]{:S(2)}) copy-start(bf16[2,1,64,320]{3,2,1,0:T(8,128)(2,1)} %refs_5_.1) | copy-start | bytes 245764
  15.7 16.9 %copy-start.2 = (bf16[2,1,64,320]{3,2,1,0:T(8,128)(2,1)S(1)}, bf16[2,1,64,320]{3,2,1,0:T(8,128)(2,1)}, u32[]{:S(2)}) copy-start(bf16[2,1,64,320]{3,2,1,0:T(8,128)(2,1)} %refs_6_.1) | copy-start | bytes 245764
  15.7 4.9 %collective-permute-start.9 = (bf16[6,64,128]{2,1,0:T(8,128)(2,1)S(1)}, bf16[6,64,128]{2,1,0:T(8,128)(2,1)S(1)}, u32[]{:S(2)}, u32[]{:S(2)}) collective-permute-start(bf16[6,64,128]{2,1,0:T(8,128)(2,1)S(1)} %shard_map.115), channel_id=1, source_target_pairs={{0,2},{1,3},{2,0},{3,1},{4,6},{5,7},{6,4},{7,5},{8,10},{9,11},{10,... | collective-permute-start | bytes 294920 | tf_op jit(solution)/shard_map/ppermute | solution.py:357
  17.7 1.3 %collective-permute-start.5 = (bf16[320,128]{1,0:T(8,128)(2,1)S(1)}, bf16[320,128]{1,0:T(8,128)(2,1)S(1)}, u32[]{:S(2)}, u32[]{:S(2)}) collective-permute-start(bf16[320,128]{1,0:T(8,128)(2,1)S(1)} %get-tuple-element.70), channel_id=1, source_target_pairs={{0,1},{1,0},{2,3},{3,2},{4,5},{5,4},{6,7},{7,6},{8,9},{9,8},{10,11... | collective-permute-start | bytes 245768 | tf_op jit(solution)/shard_map/ppermute | solution.py:357
  17.8 1.4 %collective-permute-start.4 = (bf16[320,128]{1,0:T(8,128)(2,1)S(1)}, bf16[320,128]{1,0:T(8,128)(2,1)S(1)}, u32[]{:S(2)}, u32[]{:S(2)}) collective-permute-start(bf16[320,128]{1,0:T(8,128)(2,1)S(1)} %get-tuple-element.71), channel_id=1, source_target_pairs={{0,1},{1,0},{2,3},{3,2},{4,5},{5,4},{6,7},{7,6},{8,9},{9,8},{10,11... | collective-permute-start | bytes 245768 | tf_op jit(solution)/shard_map/ppermute | solution.py:357
  20.7 10.3 %collective-permute-start.10 = (bf16[176,128]{1,0:T(8,128)(2,1)S(1)}, bf16[176,128]{1,0:T(8,128)(2,1)S(1)}, u32[]{:S(2)}, u32[]{:S(2)}) collective-permute-start(bf16[176,128]{1,0:T(8,128)(2,1)S(1)} %get-tuple-element.61), channel_id=1, source_target_pairs={{0,24},{4,28},{8,16},{12,20},{16,8},{20,12},{24,0},{28,4},{1,25},{... | collective-permute-start | bytes 135176 | tf_op jit(solution)/shard_map/ppermute | solution.py:357
  25.8 6.0 %collective-permute-start.11 = (bf16[176,128]{1,0:T(8,128)(2,1)S(1)}, bf16[176,128]{1,0:T(8,128)(2,1)S(1)}, u32[]{:S(2)}, u32[]{:S(2)}) collective-permute-start(bf16[176,128]{1,0:T(8,128)(2,1)S(1)} %get-tuple-element.62), channel_id=1, source_target_pairs={{0,16},{4,20},{8,24},{12,28},{16,0},{20,4},{24,8},{28,12},{1,17},{... | collective-permute-start | bytes 135176 | tf_op jit(solution)/shard_map/ppermute | solution.py:357
  25.8 9.0 %collective-permute-start.12 = (bf16[176,128]{1,0:T(8,128)(2,1)S(1)}, bf16[176,128]{1,0:T(8,128)(2,1)S(1)}, u32[]{:S(2)}, u32[]{:S(2)}) collective-permute-start(bf16[176,128]{1,0:T(8,128)(2,1)S(1)} %get-tuple-element.63), channel_id=1, source_target_pairs={{0,28},{4,24},{8,20},{12,16},{16,12},{20,8},{24,4},{28,0},{1,29},{... | collective-permute-start | bytes 135176 | tf_op jit(solution)/shard_map/ppermute | solution.py:357
  28.2 6.6 %collective-permute-start.13 = (bf16[176,128]{1,0:T(8,128)(2,1)S(1)}, bf16[176,128]{1,0:T(8,128)(2,1)S(1)}, u32[]{:S(2)}, u32[]{:S(2)}) collective-permute-start(bf16[176,128]{1,0:T(8,128)(2,1)S(1)} %get-tuple-element.64), channel_id=1, source_target_pairs={{0,20},{4,16},{8,28},{12,24},{16,4},{20,0},{24,12},{28,8},{1,21},{... | collective-permute-start | bytes 135176 | tf_op jit(solution)/shard_map/ppermute | solution.py:357
  28.8 6.1 %collective-permute-start.14 = (bf16[176,128]{1,0:T(8,128)(2,1)S(1)}, bf16[176,128]{1,0:T(8,128)(2,1)S(1)}, u32[]{:S(2)}, u32[]{:S(2)}) collective-permute-start(bf16[176,128]{1,0:T(8,128)(2,1)S(1)} %get-tuple-element.65), channel_id=1, source_target_pairs={{0,12},{4,8},{8,4},{12,0},{16,28},{20,24},{24,20},{28,16},{1,13},{... | collective-permute-start | bytes 135176 | tf_op jit(solution)/shard_map/ppermute | solution.py:357
  31.0 4.1 %collective-permute-start.15 = (bf16[176,128]{1,0:T(8,128)(2,1)S(1)}, bf16[176,128]{1,0:T(8,128)(2,1)S(1)}, u32[]{:S(2)}, u32[]{:S(2)}) collective-permute-start(bf16[176,128]{1,0:T(8,128)(2,1)S(1)} %get-tuple-element.66), channel_id=1, source_target_pairs={{0,8},{4,12},{8,0},{12,4},{16,24},{20,28},{24,16},{28,20},{1,9},{5... | collective-permute-start | bytes 135176 | tf_op jit(solution)/shard_map/ppermute | solution.py:357
  31.8 4.0 %collective-permute-start.16 = (bf16[176,128]{1,0:T(8,128)(2,1)S(1)}, bf16[176,128]{1,0:T(8,128)(2,1)S(1)}, u32[]{:S(2)}, u32[]{:S(2)}) collective-permute-start(bf16[176,128]{1,0:T(8,128)(2,1)S(1)} %get-tuple-element.67), channel_id=1, source_target_pairs={{0,4},{4,0},{8,12},{12,8},{16,20},{20,16},{24,28},{28,24},{1,5},{5... | collective-permute-start | bytes 135176 | tf_op jit(solution)/shard_map/ppermute | solution.py:357

commit v8 on v7

--- a/solution.py
+++ b/solution.py
@@ -126,18 +126,27 @@
     held_out[ch:] = jnp.concatenate(cots, axis=0).astype(BF16).T
 
 
-def time_terms(near_cot, far, owns, total):
-    cols = far.shape[0] // 2
+def time_terms(acts, pairs, total):
     width = total.shape[1]
-    groups = far.shape[1] // width
-    act = jnp.concatenate([v[:cols] for v in owns], axis=0).T
-    own = jnp.concatenate([v[cols:] for v in owns], axis=0)
-    tap = jnp.where(lax.axis_index("tm") % 2 == 0, 0, 2)
-    for k, cot in ((1, own), (tap, near_cot[...]), (2 - tap, far[cols:])):
+    act = jnp.concatenate(acts, axis=0).T
+    groups = act.shape[0] // width
+    for k, cot in pairs:
         for q in range(groups):
             part = slice(q * width, (q + 1) * width)
             at = pl.multiple_of((k * groups + q) * width, width)
-            total[pl.ds(at, width), :] = dot(act[part, : cot.shape[0]], cot[:, part], 1, 0)
+            total[pl.ds(at, width), :] = dot(act[part], cot[:, part], 1, 0)
+
+
+def side_terms(near_cot, far, own, total):
+    cols = far.shape[0] // 2
+    tap = jnp.where(lax.axis_index("tm") % 2 == 0, 0, 2)
+    time_terms([own[:cols]], ((tap, near_cot[...]), (2 - tap, far[cols:])), total)
+
+
+def middle_terms(owns, total):
+    cols = owns[0].shape[0] // 2
+    cot = jnp.concatenate([v[cols:] for v in owns], axis=0)
+    time_terms([v[:cols] for v in owns], ((1, cot),), total)
 
 
 def outer_steps(steps, peers, taps, rows):
@@ -149,24 +158,33 @@
     ]
 
 
-def time_sum_body(offsets, rows, near_cot, far, *refs):
-    owns, refs, total = refs[: len(offsets)], refs[len(offsets) : -1], refs[-1]
-    keeps, sends = refs[: len(offsets)], refs[len(offsets) :]
-    time_terms(near_cot, far, owns, total)
+def time_outer_body(rows, offset, near_cot, far, own, keep, send, total):
     me, peers, steps = lax.axis_index("row"), lax.axis_size("row"), lax.axis_size("tm")
-    held, third = keeps[0].shape[1], steps * peers * rows // 3
-    for u, offset in enumerate(offsets):
-        if u == 1:
-            total[third : 2 * third] = jnp.zeros((third, total.shape[1]), F32)
-        for i, t in enumerate(range(steps) if u == 0 else outer_steps(steps, peers, 3, rows)):
-            mine = (t * peers + (me ^ offset)) * rows
-            other = (t * peers + (me ^ offset ^ 1)) * rows
-            keeps[u][i] = total[pl.ds(mine, held), :]
-            sends[u][i] = total[pl.ds(other, held), :].astype(BF16)
+    held, third = keep.shape[1], steps * peers * rows // 3
+    total[third : 2 * third] = jnp.zeros((third, total.shape[1]), F32)
+    side_terms(near_cot, far, own, total)
+    for i, t in enumerate(outer_steps(steps, peers, 3, rows)):
+        mine = (t * peers + (me ^ offset)) * rows
+        other = (t * peers + (me ^ offset ^ 1)) * rows
+        keep[i] = total[pl.ds(mine, held), :]
+        send[i] = total[pl.ds(other, held), :].astype(BF16)
+
+
+def time_own_body(rows, outer, *refs):
+    owns, (keep, send, total) = refs[:-3], refs[-3:]
+    me, peers, steps = lax.axis_index("row"), lax.axis_size("row"), lax.axis_size("tm")
+    held, third = keep.shape[1], steps * peers * rows // 3
+    total[:third] = outer[:third]
+    total[2 * third :] = outer[2 * third :]
+    middle_terms(owns, total)
+    for t in range(steps):
+        keep[t] = total[pl.ds((t * peers + me) * rows, held), :]
+        send[t] = total[pl.ds((t * peers + (me ^ 1)) * rows, held), :].astype(BF16)
 
 
 def time_sum_whole_body(near_cot, far, own, total):
-    time_terms(near_cot, far, (own,), total)
+    side_terms(near_cot, far, own, total)
+    middle_terms((own,), total)
 
 
 def fold_body(kept, came, send):
@@ -418,11 +436,17 @@
         block = (steps, tall, time_width)
         outer = outer_steps(steps, peers, 3, rows)
         rest = (len(outer), *block[1:])
-        kept, other, sent_own, core_sent = on_device(
-            functools.partial(time_sum_body, offsets, rows),
-            (near_cot, far, *owns),
-            [shape(block, F32), shape(rest, F32), shape(block, BF16), shape(rest, BF16)],
-            [pltpu.VMEM((round_up(time_rows + tall, 8), time_width), F32)],
+        table = shape((round_up(time_rows + tall, 8), time_width), F32)
+        other, core_sent, table_outer = on_device(
+            functools.partial(time_outer_body, rows, offsets[1]),
+            (near_cot, far, packed),
+            [shape(rest, F32), shape(rest, BF16), table],
+        )
+        kept, sent_own = on_device(
+            functools.partial(time_own_body, rows),
+            (table_outer, *owns),
+            [shape(block, F32), shape(block, BF16)],
+            [pltpu.VMEM(table.shape, F32)],
         )
         sent = on_device(fold_body, (other, swap(core_sent, "row", 1)), [shape(rest, BF16)])[0]
         came = [swap(sent_own, "row", 1), swap(sent, "row", bits[1])]

time: 36.7 us -> 36.6 us (level)
    pallas_call x9 -> x10, Pallas kernels: 7.8 us -> 7.95 us  [on_device(): pl.pallas_call(body, out_shape=outs, in_specs=[pl.BlockSpec(memory_space=...]
  transfers between devices with their start and end apart: 17 -> 17, of which waited for: 10 -> 9; matrix products, arithmetic and copies ran while one was open for 0% -> 0% of each run, Pallas kernels for 16% -> 17%
where the time goes in v8:
time: 36.6 us; the launch traced here: 36.5 us
  starting transfers between devices  20.4 us (56%)
  Pallas kernels  7.95 us (22%)
  waiting for transfers between devices  7.28 us (20%)
  between operations  0.77 us (2%)
    ppermute x15, starting transfers between devices, swap(): lax.ppermute(x, axis, [(i, i ^ bit) for i in range(lax.axis_size(axis))])  16.7 us
    pallas_call x10, Pallas kernels, on_device(): pl.pallas_call(body, out_shape=outs, in_specs=[pl.BlockSpec(memory_space=...  7.95 us
    ppermute x15, waiting for transfers between devices, swap(): lax.ppermute(x, axis, [(i, i ^ bit) for i in range(lax.axis_size(axis))])  4.02 us
    ppermute x2, starting transfers between devices, neighbours(): lax.ppermute(x, axis, [p for i in lower for p in ((i, i + 1), (i + 1, i))])  3.69 us
    ppermute x2, waiting for transfers between devices, neighbours(): lax.ppermute(x, axis, [p for i in lower for p in ((i, i + 1), (i + 1, i))])  3.26 us
  transfers between devices with their start and end apart: 17, of which 9 were waited for; matrix products, arithmetic and copies ran while one was open for 0% of the time, Pallas kernels for 17%

profile of v8, /device:TPU:0, one launch (start us, length us, event | category | flops | bytes accessed | tf_op | source)
XLA Modules:
  0.0 36.5 jit_solution(8227078518349360795)
XLA Ops:
  0.6 1.1 %shard_map.109.own.refs_0_ = bf16[128,640]{1,0:T(8,128)(2,1)S(1)} custom-call(bf16[2,1,64,320]{3,2,1,0:T(8,128)(2,1)} %refs_5_.1, bf16[2,1,64,320]{3,2,1,0:T(8,128)(2,1)} %refs_6_.1), custom_call_target="tpu_custom_call" | custom-call | bytes 327680 | tf_op jit(solution)/shard_map/pallas_call | solution.py:27
  1.7 3.0 %collective-permute-start = (bf16[128,640]{1,0:T(8,128)(2,1)S(1)}, bf16[128,640]{1,0:T(8,128)(2,1)S(1)}, u32[]{:S(2)}, u32[]{:S(2)}) collective-permute-start(bf16[128,640]{1,0:T(8,128)(2,1)S(1)} %shard_map.109.own.refs_0_), channel_id=1, source_target_pairs={{0,4},{4,0},{8,12},{12,8},{16,20},{20,16},{24,28},{28,24},{1,5},{5... | collective-permute-start | bytes 491528 | tf_op jit(solution)/shard_map/ppermute | solution.py:400
  4.8 0.7 %collective-permute-start.1 = (bf16[128,640]{1,0:T(8,128)(2,1)S(1)}, bf16[128,640]{1,0:T(8,128)(2,1)S(1)}, u32[]{:S(2)}, u32[]{:S(2)}) collective-permute-start(bf16[128,640]{1,0:T(8,128)(2,1)S(1)} %shard_map.109.own.refs_0_), channel_id=1, source_target_pairs={{4,8},{8,4},{12,16},{16,12},{20,24},{24,20},{5,9},{9,5},{13,17},{1... | collective-permute-start | bytes 491528 | tf_op jit(solution)/shard_map/ppermute | solution.py:400
  5.4 1.6 %collective-permute-start.6 = (bf16[128,640]{1,0:T(8,128)(2,1)S(1)}, bf16[128,640]{1,0:T(8,128)(2,1)S(1)}, u32[]{:S(2)}, u32[]{:S(2)}) collective-permute-start(bf16[128,640]{1,0:T(8,128)(2,1)S(1)} %shard_map.109.own.refs_0_), channel_id=1, source_target_pairs={{0,2},{1,3},{2,0},{3,1},{4,6},{5,7},{6,4},{7,5},{8,10},{9,11},{10,... | collective-permute-start | bytes 491528 | tf_op jit(solution)/shard_map/ppermute | solution.py:375
  7.0 1.5 %shard_map.110 = (f32[64,640]{1,0:T(8,128)S(1)}, f32[64,640]{1,0:T(8,128)S(1)}, f32[64,640]{1,0:T(8,128)S(1)}, bf16[2,2,64,320]{3,2,1,0:T(8,128)(2,1)S(1)}, bf16[3,5,128,128]{3,2,1,0:T(8,128)(2,1)S(1)}) custom-call(bf16[2,1,64,320]{3,2,1,0:T(8,128)(2,1)} %refs_5_.1, bf16[2,1,64,320]{3,2,1,0:T(8,128)(2,1)} %y2_far.1, bf16[2,1,64,320]{3,2,1,0:T(8,128)(2,1)} %c1_far.1, ...), custom_call_target="tpu_custom_call" | custom-call | bytes 2048000 | tf_op jit(solution)/shard_map/pallas_call | solution.py:27
  8.5 3.3 %collective-permute-done.near = bf16[128,640]{1,0:T(8,128)(2,1)S(1)} collective-permute-done((bf16[128,640]{1,0:T(8,128)(2,1)S(1)}, bf16[128,640]{1,0:T(8,128)(2,1)S(1)}, u32[]{:S(2)}, u32[]{:S(2)}) %collective-permute-start) | collective-permute-done | bytes 163872 | tf_op jit(solution)/shard_map/ppermute | solution.py:400
  11.8 0.5 %shard_map.111 = (bf16[2,1,64,320]{3,2,1,0:T(8,128)(2,1)S(1)}, bf16[2,1,64,320]{3,2,1,0:T(8,128)(2,1)S(1)}, bf16[640,128]{1,0:T(8,128)(2,1)S(1)}) custom-call(bf16[128,640]{1,0:T(8,128)(2,1)S(1)} %collective-permute-done.near, bf16[64,640]{1,0:T(8,128)(2,1)S(1)} %slice.12.near_cot, bf16[128,640]{1,0:T(8,128)(2,1)S(1)} %collective-permute-done.1.far, ...), custom_call_target="tpu_custom_call" | custom-call | bytes 1884160 | tf_op jit(solution)/shard_map/pallas_call | solution.py:27
  12.3 1.6 %collective-permute-start.3 = (bf16[640,128]{1,0:T(8,128)(2,1)S(1)}, bf16[640,128]{1,0:T(8,128)(2,1)S(1)}, u32[]{:S(2)}, u32[]{:S(2)}) collective-permute-start(bf16[640,128]{1,0:T(8,128)(2,1)S(1)} %get-tuple-element.50.refs_0_), channel_id=1, source_target_pairs={{0,2},{1,3},{2,0},{3,1},{4,6},{5,7},{6,4},{7,5},{8,10},{9,11},{10,... | collective-permute-start | bytes 491528 | tf_op jit(solution)/shard_map/ppermute | solution.py:375
  14.2 0.5 %collective-permute-start.2 = (bf16[640,128]{1,0:T(8,128)(2,1)S(1)}, bf16[640,128]{1,0:T(8,128)(2,1)S(1)}, u32[]{:S(2)}, u32[]{:S(2)}) collective-permute-start(bf16[640,128]{1,0:T(8,128)(2,1)S(1)} %get-tuple-element.50.refs_0_), channel_id=1, source_target_pairs={{0,1},{1,0},{2,3},{3,2},{4,5},{5,4},{6,7},{7,6},{8,9},{9,8},{10,11... | collective-permute-start | bytes 491528 | tf_op jit(solution)/shard_map/ppermute | solution.py:375
  15.2 0.4 collective-permute-done.8.came
  15.6 0.6 %collective-permute-start.9 = (bf16[6,64,128]{2,1,0:T(8,128)(2,1)S(1)}, bf16[6,64,128]{2,1,0:T(8,128)(2,1)S(1)}, u32[]{:S(2)}, u32[]{:S(2)}) collective-permute-start(bf16[6,64,128]{2,1,0:T(8,128)(2,1)S(1)} %shard_map.116), channel_id=1, source_target_pairs={{0,2},{1,3},{2,0},{3,1},{4,6},{5,7},{6,4},{7,5},{8,10},{9,11},{10,... | collective-permute-start | bytes 294920 | tf_op jit(solution)/shard_map/ppermute | solution.py:375
  16.2 1.5 %collective-permute-done.3.refs_2_ = bf16[640,128]{1,0:T(8,128)(2,1)S(1)} collective-permute-done((bf16[640,128]{1,0:T(8,128)(2,1)S(1)}, bf16[640,128]{1,0:T(8,128)(2,1)S(1)}, u32[]{:S(2)}, u32[]{:S(2)}) %collective-permute-start.3) | collective-permute-done | bytes 163872 | tf_op jit(solution)/shard_map/ppermute | solution.py:375
  17.8 0.5 %collective-permute-start.4 = (bf16[320,128]{1,0:T(8,128)(2,1)S(1)}, bf16[320,128]{1,0:T(8,128)(2,1)S(1)}, u32[]{:S(2)}, u32[]{:S(2)}) collective-permute-start(bf16[320,128]{1,0:T(8,128)(2,1)S(1)} %get-tuple-element.73), channel_id=1, source_target_pairs={{0,1},{1,0},{2,3},{3,2},{4,5},{5,4},{6,7},{7,6},{8,9},{9,8},{10,11... | collective-permute-start | bytes 245768 | tf_op jit(solution)/shard_map/ppermute | solution.py:375
  18.3 0.8 %collective-permute-done.5.refs_4_ = bf16[320,128]{1,0:T(8,128)(2,1)S(1)} collective-permute-done((bf16[320,128]{1,0:T(8,128)(2,1)S(1)}, bf16[320,128]{1,0:T(8,128)(2,1)S(1)}, u32[]{:S(2)}, u32[]{:S(2)}) %collective-permute-start.5) | collective-permute-done | bytes 81952 | tf_op jit(solution)/shard_map/ppermute | solution.py:375
  19.2 1.3 %shard_map.113.pieces = f32[8,176,128]{2,1,0:T(8,128)S(1)} custom-call(bf16[640,128]{1,0:T(8,128)(2,1)S(1)} %get-tuple-element.50.refs_0_, bf16[640,128]{1,0:T(8,128)(2,1)S(1)} %collective-permute-done.2.refs_1_, bf16[640,128]{1,0:T(8,128)(2,1)S(1)} %collective-permute-done.3.refs_2_, bf16[320,128]{1,0:T(8,128)(2,1)S(1)} %collective-permute-done.4.refs_3_, ...), custom_call_target="tpu_custom_call" | custom-call | bytes 1376256 | tf_op jit(solution)/shard_map/pallas_call | solution.py:27
  20.6 5.1 %collective-permute-start.10 = (bf16[176,128]{1,0:T(8,128)(2,1)S(1)}, bf16[176,128]{1,0:T(8,128)(2,1)S(1)}, u32[]{:S(2)}, u32[]{:S(2)}) collective-permute-start(bf16[176,128]{1,0:T(8,128)(2,1)S(1)} %get-tuple-element.63), channel_id=1, source_target_pairs={{0,24},{4,28},{8,16},{12,20},{16,8},{20,12},{24,0},{28,4},{1,25},{... | collective-permute-start | bytes 135176 | tf_op jit(solution)/shard_map/ppermute | solution.py:375
  25.7 2.4 %collective-permute-start.12 = (bf16[176,128]{1,0:T(8,128)(2,1)S(1)}, bf16[176,128]{1,0:T(8,128)(2,1)S(1)}, u32[]{:S(2)}, u32[]{:S(2)}) collective-permute-start(bf16[176,128]{1,0:T(8,128)(2,1)S(1)} %get-tuple-element.65), channel_id=1, source_target_pairs={{0,28},{4,24},{8,20},{12,16},{16,12},{20,8},{24,4},{28,0},{1,29},{... | collective-permute-start | bytes 135176 | tf_op jit(solution)/shard_map/ppermute | solution.py:375
  28.1 0.6 %collective-permute-start.13 = (bf16[176,128]{1,0:T(8,128)(2,1)S(1)}, bf16[176,128]{1,0:T(8,128)(2,1)S(1)}, u32[]{:S(2)}, u32[]{:S(2)}) collective-permute-start(bf16[176,128]{1,0:T(8,128)(2,1)S(1)} %get-tuple-element.66), channel_id=1, source_target_pairs={{0,20},{4,16},{8,28},{12,24},{16,4},{20,0},{24,12},{28,8},{1,21},{... | collective-permute-start | bytes 135176 | tf_op jit(solution)/shard_map/ppermute | solution.py:375
  28.7 2.2 %collective-permute-start.14 = (bf16[176,128]{1,0:T(8,128)(2,1)S(1)}, bf16[176,128]{1,0:T(8,128)(2,1)S(1)}, u32[]{:S(2)}, u32[]{:S(2)}) collective-permute-start(bf16[176,128]{1,0:T(8,128)(2,1)S(1)} %get-tuple-element.67), channel_id=1, source_target_pairs={{0,12},{4,8},{8,4},{12,0},{16,28},{20,24},{24,20},{28,16},{1,13},{... | collective-permute-start | bytes 135176 | tf_op jit(solution)/shard_map/ppermute | solution.py:375
  30.9 0.6 %collective-permute-start.15 = (bf16[176,128]{1,0:T(8,128)(2,1)S(1)}, bf16[176,128]{1,0:T(8,128)(2,1)S(1)}, u32[]{:S(2)}, u32[]{:S(2)}) collective-permute-start(bf16[176,128]{1,0:T(8,128)(2,1)S(1)} %get-tuple-element.68), channel_id=1, source_target_pairs={{0,8},{4,12},{8,0},{12,4},{16,24},{20,28},{24,16},{28,20},{1,9},{5... | collective-permute-start | bytes 135176 | tf_op jit(solution)/shard_map/ppermute | solution.py:375
  31.7 0.8 %collective-permute-start.16 = (bf16[176,128]{1,0:T(8,128)(2,1)S(1)}, bf16[176,128]{1,0:T(8,128)(2,1)S(1)}, u32[]{:S(2)}, u32[]{:S(2)}) collective-permute-start(bf16[176,128]{1,0:T(8,128)(2,1)S(1)} %get-tuple-element.69), channel_id=1, source_target_pairs={{0,4},{4,0},{8,12},{12,8},{16,20},{20,16},{24,28},{28,24},{1,5},{5... | collective-permute-start | bytes 135176 | tf_op jit(solution)/shard_map/ppermute | solution.py:375
  32.5 2.2 %shard_map.112 = (bf16[2,1,64,320]{3,2,1,0:T(8,128)(2,1)}, bf16[2,1,64,320]{3,2,1,0:T(8,128)(2,1)}, bf16[2,1,64,320]{3,2,1,0:T(8,128)(2,1)}, bf16[2,1,64,320]{3,2,1,0:T(8,128)(2,1)}) custom-call(bf16[640,128]{1,0:T(8,128)(2,1)S(1)} %get-tuple-element.50.refs_0_, bf16[640,128]{1,0:T(8,128)(2,1)S(1)} %collective-permute-done.2.refs_1_, ...), custom_call_target="tpu_custom_call" | custom-call | bytes 2232320 | tf_op jit(solution)/shard_map/pallas_call | solution.py:27
  35.0 0.8 %collective-permute-done.16.refs_7_ = bf16[176,128]{1,0:T(8,128)(2,1)S(1)} collective-permute-done((bf16[176,128]{1,0:T(8,128)(2,1)S(1)}, bf16[176,128]{1,0:T(8,128)(2,1)S(1)}, u32[]{:S(2)}, u32[]{:S(2)}) %collective-permute-start.16) | collective-permute-done | bytes 45088 | tf_op jit(solution)/shard_map/ppermute | solution.py:375
  35.8 0.7 %shard_map.118 = (f32[120,128]{1,0:T(8,128)}, f32[60,128]{1,0:T(8,128)}) custom-call(f32[176,128]{1,0:T(8,128)S(1)} %get-tuple-element.62.refs_0_, bf16[176,128]{1,0:T(8,128)(2,1)S(1)} %collective-permute-done.10.refs_1_, bf16[176,128]{1,0:T(8,128)(2,1)S(1)} %collective-permute-done.11.refs_2_, bf16[176,128]{1,0:T(8,128)(2,1)S(1)} %collective-permute-done.12.refs_3_, ...), custom_call_target="tpu_custom_call" | custom-call | bytes 497664 | tf_op jit(solution)/shard_map/pallas_call | solution.py:27
  (28 shorter events, 1.6 us)
Async XLA Ops:
  1.7 10.0 %collective-permute-start = (bf16[128,640]{1,0:T(8,128)(2,1)S(1)}, bf16[128,640]{1,0:T(8,128)(2,1)S(1)}, u32[]{:S(2)}, u32[]{:S(2)}) collective-permute-start(bf16[128,640]{1,0:T(8,128)(2,1)S(1)} %shard_map.109.own.refs_0_), channel_id=1, source_target_pairs={{0,4},{4,0},{8,12},{12,8},{16,20},{20,16},{24,28},{28,24},{1,5},{5... | collective-permute-start | bytes 491528 | tf_op jit(solution)/shard_map/ppermute | solution.py:400
  4.8 7.0 %collective-permute-start.1 = (bf16[128,640]{1,0:T(8,128)(2,1)S(1)}, bf16[128,640]{1,0:T(8,128)(2,1)S(1)}, u32[]{:S(2)}, u32[]{:S(2)}) collective-permute-start(bf16[128,640]{1,0:T(8,128)(2,1)S(1)} %shard_map.109.own.refs_0_), channel_id=1, source_target_pairs={{4,8},{8,4},{12,16},{16,12},{20,24},{24,20},{5,9},{9,5},{13,17},{1... | collective-permute-start | bytes 491528 | tf_op jit(solution)/shard_map/ppermute | solution.py:400
  5.4 9.3 %collective-permute-start.6 = (bf16[128,640]{1,0:T(8,128)(2,1)S(1)}, bf16[128,640]{1,0:T(8,128)(2,1)S(1)}, u32[]{:S(2)}, u32[]{:S(2)}) collective-permute-start(bf16[128,640]{1,0:T(8,128)(2,1)S(1)} %shard_map.109.own.refs_0_), channel_id=1, source_target_pairs={{0,2},{1,3},{2,0},{3,1},{4,6},{5,7},{6,4},{7,5},{8,10},{9,11},{10,... | collective-permute-start | bytes 491528 | tf_op jit(solution)/shard_map/ppermute | solution.py:375
  12.3 5.4 %collective-permute-start.3 = (bf16[640,128]{1,0:T(8,128)(2,1)S(1)}, bf16[640,128]{1,0:T(8,128)(2,1)S(1)}, u32[]{:S(2)}, u32[]{:S(2)}) collective-permute-start(bf16[640,128]{1,0:T(8,128)(2,1)S(1)} %get-tuple-element.50.refs_0_), channel_id=1, source_target_pairs={{0,2},{1,3},{2,0},{3,1},{4,6},{5,7},{6,4},{7,5},{8,10},{9,11},{10,... | collective-permute-start | bytes 491528 | tf_op jit(solution)/shard_map/ppermute | solution.py:375
  14.2 1.4 %collective-permute-start.8 = (bf16[6,64,128]{2,1,0:T(8,128)(2,1)S(1)}, bf16[6,64,128]{2,1,0:T(8,128)(2,1)S(1)}, u32[]{:S(2)}, u32[]{:S(2)}) collective-permute-start(bf16[6,64,128]{2,1,0:T(8,128)(2,1)S(1)} %get-tuple-element.61), channel_id=1, source_target_pairs={{0,1},{1,0},{2,3},{3,2},{4,5},{5,4},{6,7},{7,6},{8,9},{9,8},{10,11... | collective-permute-start | bytes 294920 | tf_op jit(solution)/shard_map/ppermute | solution.py:375
  14.2 4.0 %collective-permute-start.2 = (bf16[640,128]{1,0:T(8,128)(2,1)S(1)}, bf16[640,128]{1,0:T(8,128)(2,1)S(1)}, u32[]{:S(2)}, u32[]{:S(2)}) collective-permute-start(bf16[640,128]{1,0:T(8,128)(2,1)S(1)} %get-tuple-element.50.refs_0_), channel_id=1, source_target_pairs={{0,1},{1,0},{2,3},{3,2},{4,5},{5,4},{6,7},{7,6},{8,9},{9,8},{10,11... | collective-permute-start | bytes 491528 | tf_op jit(solution)/shard_map/ppermute | solution.py:375
  15.0 5.5 %collective-permute-start.7 = (bf16[8,64,128]{2,1,0:T(8,128)(2,1)S(1)}, bf16[8,64,128]{2,1,0:T(8,128)(2,1)S(1)}, u32[]{:S(2)}, u32[]{:S(2)}) collective-permute-start(bf16[8,64,128]{2,1,0:T(8,128)(2,1)S(1)} %get-tuple-element.59), channel_id=1, source_target_pairs={{0,1},{1,0},{2,3},{3,2},{4,5},{5,4},{6,7},{7,6},{8,9},{9,8},{10,11... | collective-permute-start | bytes 393224 | tf_op jit(solution)/shard_map/ppermute | solution.py:375
  15.5 17.0 %copy-start = (bf16[3,3,2,160,160]{4,3,2,1,0:T(8,128)(2,1)S(1)}, bf16[3,3,2,160,160]{4,3,2,1,0:T(8,128)(2,1)}, u32[]{:S(2)}) copy-start(bf16[3,3,2,160,160]{4,3,2,1,0:T(8,128)(2,1)} %refs_9_.1) | copy-start | bytes 2764804
  15.6 17.0 %copy-start.1 = (bf16[2,1,64,320]{3,2,1,0:T(8,128)(2,1)S(1)}, bf16[2,1,64,320]{3,2,1,0:T(8,128)(2,1)}, u32[]{:S(2)}) copy-start(bf16[2,1,64,320]{3,2,1,0:T(8,128)(2,1)} %refs_5_.1) | copy-start | bytes 245764
  15.6 17.0 %copy-start.2 = (bf16[2,1,64,320]{3,2,1,0:T(8,128)(2,1)S(1)}, bf16[2,1,64,320]{3,2,1,0:T(8,128)(2,1)}, u32[]{:S(2)}) copy-start(bf16[2,1,64,320]{3,2,1,0:T(8,128)(2,1)} %refs_6_.1) | copy-start | bytes 245764
  15.6 4.9 %collective-permute-start.9 = (bf16[6,64,128]{2,1,0:T(8,128)(2,1)S(1)}, bf16[6,64,128]{2,1,0:T(8,128)(2,1)S(1)}, u32[]{:S(2)}, u32[]{:S(2)}) collective-permute-start(bf16[6,64,128]{2,1,0:T(8,128)(2,1)S(1)} %shard_map.116), channel_id=1, source_target_pairs={{0,2},{1,3},{2,0},{3,1},{4,6},{5,7},{6,4},{7,5},{8,10},{9,11},{10,... | collective-permute-start | bytes 294920 | tf_op jit(solution)/shard_map/ppermute | solution.py:375
  17.7 1.3 %collective-permute-start.5 = (bf16[320,128]{1,0:T(8,128)(2,1)S(1)}, bf16[320,128]{1,0:T(8,128)(2,1)S(1)}, u32[]{:S(2)}, u32[]{:S(2)}) collective-permute-start(bf16[320,128]{1,0:T(8,128)(2,1)S(1)} %get-tuple-element.72), channel_id=1, source_target_pairs={{0,1},{1,0},{2,3},{3,2},{4,5},{5,4},{6,7},{7,6},{8,9},{9,8},{10,11... | collective-permute-start | bytes 245768 | tf_op jit(solution)/shard_map/ppermute | solution.py:375
  17.8 1.4 %collective-permute-start.4 = (bf16[320,128]{1,0:T(8,128)(2,1)S(1)}, bf16[320,128]{1,0:T(8,128)(2,1)S(1)}, u32[]{:S(2)}, u32[]{:S(2)}) collective-permute-start(bf16[320,128]{1,0:T(8,128)(2,1)S(1)} %get-tuple-element.73), channel_id=1, source_target_pairs={{0,1},{1,0},{2,3},{3,2},{4,5},{5,4},{6,7},{7,6},{8,9},{9,8},{10,11... | collective-permute-start | bytes 245768 | tf_op jit(solution)/shard_map/ppermute | solution.py:375
  20.6 10.3 %collective-permute-start.10 = (bf16[176,128]{1,0:T(8,128)(2,1)S(1)}, bf16[176,128]{1,0:T(8,128)(2,1)S(1)}, u32[]{:S(2)}, u32[]{:S(2)}) collective-permute-start(bf16[176,128]{1,0:T(8,128)(2,1)S(1)} %get-tuple-element.63), channel_id=1, source_target_pairs={{0,24},{4,28},{8,16},{12,20},{16,8},{20,12},{24,0},{28,4},{1,25},{... | collective-permute-start | bytes 135176 | tf_op jit(solution)/shard_map/ppermute | solution.py:375
  25.7 6.0 %collective-permute-start.11 = (bf16[176,128]{1,0:T(8,128)(2,1)S(1)}, bf16[176,128]{1,0:T(8,128)(2,1)S(1)}, u32[]{:S(2)}, u32[]{:S(2)}) collective-permute-start(bf16[176,128]{1,0:T(8,128)(2,1)S(1)} %get-tuple-element.64), channel_id=1, source_target_pairs={{0,16},{4,20},{8,24},{12,28},{16,0},{20,4},{24,8},{28,12},{1,17},{... | collective-permute-start | bytes 135176 | tf_op jit(solution)/shard_map/ppermute | solution.py:375
  25.7 9.0 %collective-permute-start.12 = (bf16[176,128]{1,0:T(8,128)(2,1)S(1)}, bf16[176,128]{1,0:T(8,128)(2,1)S(1)}, u32[]{:S(2)}, u32[]{:S(2)}) collective-permute-start(bf16[176,128]{1,0:T(8,128)(2,1)S(1)} %get-tuple-element.65), channel_id=1, source_target_pairs={{0,28},{4,24},{8,20},{12,16},{16,12},{20,8},{24,4},{28,0},{1,29},{... | collective-permute-start | bytes 135176 | tf_op jit(solution)/shard_map/ppermute | solution.py:375
  28.1 6.6 %collective-permute-start.13 = (bf16[176,128]{1,0:T(8,128)(2,1)S(1)}, bf16[176,128]{1,0:T(8,128)(2,1)S(1)}, u32[]{:S(2)}, u32[]{:S(2)}) collective-permute-start(bf16[176,128]{1,0:T(8,128)(2,1)S(1)} %get-tuple-element.66), channel_id=1, source_target_pairs={{0,20},{4,16},{8,28},{12,24},{16,4},{20,0},{24,12},{28,8},{1,21},{... | collective-permute-start | bytes 135176 | tf_op jit(solution)/shard_map/ppermute | solution.py:375
  28.7 6.1 %collective-permute-start.14 = (bf16[176,128]{1,0:T(8,128)(2,1)S(1)}, bf16[176,128]{1,0:T(8,128)(2,1)S(1)}, u32[]{:S(2)}, u32[]{:S(2)}) collective-permute-start(bf16[176,128]{1,0:T(8,128)(2,1)S(1)} %get-tuple-element.67), channel_id=1, source_target_pairs={{0,12},{4,8},{8,4},{12,0},{16,28},{20,24},{24,20},{28,16},{1,13},{... | collective-permute-start | bytes 135176 | tf_op jit(solution)/shard_map/ppermute | solution.py:375
  30.9 4.0 %collective-permute-start.15 = (bf16[176,128]{1,0:T(8,128)(2,1)S(1)}, bf16[176,128]{1,0:T(8,128)(2,1)S(1)}, u32[]{:S(2)}, u32[]{:S(2)}) collective-permute-start(bf16[176,128]{1,0:T(8,128)(2,1)S(1)} %get-tuple-element.68), channel_id=1, source_target_pairs={{0,8},{4,12},{8,0},{12,4},{16,24},{20,28},{24,16},{28,20},{1,9},{5... | collective-permute-start | bytes 135176 | tf_op jit(solution)/shard_map/ppermute | solution.py:375
  31.7 4.0 %collective-permute-start.16 = (bf16[176,128]{1,0:T(8,128)(2,1)S(1)}, bf16[176,128]{1,0:T(8,128)(2,1)S(1)}, u32[]{:S(2)}, u32[]{:S(2)}) collective-permute-start(bf16[176,128]{1,0:T(8,128)(2,1)S(1)} %get-tuple-element.69), channel_id=1, source_target_pairs={{0,4},{4,0},{8,12},{12,8},{16,20},{20,16},{24,28},{28,24},{1,5},{5... | collective-permute-start | bytes 135176 | tf_op jit(solution)/shard_map/ppermute | solution.py:375

commit v9 on v8

--- a/solution.py
+++ b/solution.py
@@ -276,17 +276,13 @@
                 rolled[j, tile, amount] = pltpu.roll(value, amount, 1) if amount else value
             return rolled[j, tile, amount]
 
-        parts = [jnp.zeros((time_rows, LANES), F32)]
-        for row in layout:
+        out[k, : round_up(time_rows, 8)] = jnp.zeros((round_up(time_rows, 8), LANES), F32)
+        for i, row in enumerate(layout):
             value = None
             for first, j, tile, amount in row:
                 piece = source(j, tile, amount)
                 value = piece if value is None else jnp.where(lane < first, value, piece)
-            parts.append(value[:short])
-        blank = out.shape[1] - time_rows - short * len(layout)
-        if blank:
-            parts.append(jnp.zeros((blank, LANES), F32))
-        out[k] = jnp.concatenate(parts, axis=0)
+            out[k, pl.ds(time_rows + i * short, held), :] = value
 
 
 def join_body(time_rows, outer, pieces, kept, core_came, came, mine, *sends):

time: 36.6 us -> 36.6 us (level)
  no operation moved by 1% of the time
where the time goes in v9:
time: 36.6 us; the launch traced here: 36.5 us
  starting transfers between devices  20.4 us (56%)
  Pallas kernels  7.95 us (22%)
  waiting for transfers between devices  7.28 us (20%)
  between operations  0.77 us (2%)
    ppermute x15, starting transfers between devices, swap(): lax.ppermute(x, axis, [(i, i ^ bit) for i in range(lax.axis_size(axis))])  16.7 us
    pallas_call x10, Pallas kernels, on_device(): pl.pallas_call(body, out_shape=outs, in_specs=[pl.BlockSpec(memory_space=...  7.95 us
    ppermute x15, waiting for transfers between devices, swap(): lax.ppermute(x, axis, [(i, i ^ bit) for i in range(lax.axis_size(axis))])  4.02 us
    ppermute x2, starting transfers between devices, neighbours(): lax.ppermute(x, axis, [p for i in lower for p in ((i, i + 1), (i + 1, i))])  3.69 us
    ppermute x2, waiting for transfers between devices, neighbours(): lax.ppermute(x, axis, [p for i in lower for p in ((i, i + 1), (i + 1, i))])  3.26 us
  transfers between devices with their start and end apart: 17, of which 9 were waited for; matrix products, arithmetic and copies ran while one was open for 0% of the time, Pallas kernels for 17%

profile of v9, /device:TPU:0, one launch (start us, length us, event | category | flops | bytes accessed | tf_op | source)
XLA Modules:
  0.0 36.5 jit_solution(5333518022801306086)
XLA Ops:
  0.6 1.1 %shard_map.109.own.refs_0_ = bf16[128,640]{1,0:T(8,128)(2,1)S(1)} custom-call(bf16[2,1,64,320]{3,2,1,0:T(8,128)(2,1)} %refs_5_.1, bf16[2,1,64,320]{3,2,1,0:T(8,128)(2,1)} %refs_6_.1), custom_call_target="tpu_custom_call" | custom-call | bytes 327680 | tf_op jit(solution)/shard_map/pallas_call | solution.py:27
  1.7 3.0 %collective-permute-start = (bf16[128,640]{1,0:T(8,128)(2,1)S(1)}, bf16[128,640]{1,0:T(8,128)(2,1)S(1)}, u32[]{:S(2)}, u32[]{:S(2)}) collective-permute-start(bf16[128,640]{1,0:T(8,128)(2,1)S(1)} %shard_map.109.own.refs_0_), channel_id=1, source_target_pairs={{0,4},{4,0},{8,12},{12,8},{16,20},{20,16},{24,28},{28,24},{1,5},{5... | collective-permute-start | bytes 491528 | tf_op jit(solution)/shard_map/ppermute | solution.py:396
  4.8 0.7 %collective-permute-start.1 = (bf16[128,640]{1,0:T(8,128)(2,1)S(1)}, bf16[128,640]{1,0:T(8,128)(2,1)S(1)}, u32[]{:S(2)}, u32[]{:S(2)}) collective-permute-start(bf16[128,640]{1,0:T(8,128)(2,1)S(1)} %shard_map.109.own.refs_0_), channel_id=1, source_target_pairs={{4,8},{8,4},{12,16},{16,12},{20,24},{24,20},{5,9},{9,5},{13,17},{1... | collective-permute-start | bytes 491528 | tf_op jit(solution)/shard_map/ppermute | solution.py:396
  5.4 1.6 %collective-permute-start.6 = (bf16[128,640]{1,0:T(8,128)(2,1)S(1)}, bf16[128,640]{1,0:T(8,128)(2,1)S(1)}, u32[]{:S(2)}, u32[]{:S(2)}) collective-permute-start(bf16[128,640]{1,0:T(8,128)(2,1)S(1)} %shard_map.109.own.refs_0_), channel_id=1, source_target_pairs={{0,2},{1,3},{2,0},{3,1},{4,6},{5,7},{6,4},{7,5},{8,10},{9,11},{10,... | collective-permute-start | bytes 491528 | tf_op jit(solution)/shard_map/ppermute | solution.py:371
  7.0 1.5 %shard_map.110 = (f32[64,640]{1,0:T(8,128)S(1)}, f32[64,640]{1,0:T(8,128)S(1)}, f32[64,640]{1,0:T(8,128)S(1)}, bf16[2,2,64,320]{3,2,1,0:T(8,128)(2,1)S(1)}, bf16[3,5,128,128]{3,2,1,0:T(8,128)(2,1)S(1)}) custom-call(bf16[2,1,64,320]{3,2,1,0:T(8,128)(2,1)} %refs_5_.1, bf16[2,1,64,320]{3,2,1,0:T(8,128)(2,1)} %y2_far.1, bf16[2,1,64,320]{3,2,1,0:T(8,128)(2,1)} %c1_far.1, ...), custom_call_target="tpu_custom_call" | custom-call | bytes 2048000 | tf_op jit(solution)/shard_map/pallas_call | solution.py:27
  8.5 3.3 %collective-permute-done.near = bf16[128,640]{1,0:T(8,128)(2,1)S(1)} collective-permute-done((bf16[128,640]{1,0:T(8,128)(2,1)S(1)}, bf16[128,640]{1,0:T(8,128)(2,1)S(1)}, u32[]{:S(2)}, u32[]{:S(2)}) %collective-permute-start) | collective-permute-done | bytes 163872 | tf_op jit(solution)/shard_map/ppermute | solution.py:396
  11.8 0.5 %shard_map.111 = (bf16[2,1,64,320]{3,2,1,0:T(8,128)(2,1)S(1)}, bf16[2,1,64,320]{3,2,1,0:T(8,128)(2,1)S(1)}, bf16[640,128]{1,0:T(8,128)(2,1)S(1)}) custom-call(bf16[128,640]{1,0:T(8,128)(2,1)S(1)} %collective-permute-done.near, bf16[64,640]{1,0:T(8,128)(2,1)S(1)} %slice.12.near_cot, bf16[128,640]{1,0:T(8,128)(2,1)S(1)} %collective-permute-done.1.far, ...), custom_call_target="tpu_custom_call" | custom-call | bytes 1884160 | tf_op jit(solution)/shard_map/pallas_call | solution.py:27
  12.3 1.6 %collective-permute-start.3 = (bf16[640,128]{1,0:T(8,128)(2,1)S(1)}, bf16[640,128]{1,0:T(8,128)(2,1)S(1)}, u32[]{:S(2)}, u32[]{:S(2)}) collective-permute-start(bf16[640,128]{1,0:T(8,128)(2,1)S(1)} %get-tuple-element.50.refs_0_), channel_id=1, source_target_pairs={{0,2},{1,3},{2,0},{3,1},{4,6},{5,7},{6,4},{7,5},{8,10},{9,11},{10,... | collective-permute-start | bytes 491528 | tf_op jit(solution)/shard_map/ppermute | solution.py:371
  14.2 0.5 %collective-permute-start.2 = (bf16[640,128]{1,0:T(8,128)(2,1)S(1)}, bf16[640,128]{1,0:T(8,128)(2,1)S(1)}, u32[]{:S(2)}, u32[]{:S(2)}) collective-permute-start(bf16[640,128]{1,0:T(8,128)(2,1)S(1)} %get-tuple-element.50.refs_0_), channel_id=1, source_target_pairs={{0,1},{1,0},{2,3},{3,2},{4,5},{5,4},{6,7},{7,6},{8,9},{9,8},{10,11... | collective-permute-start | bytes 491528 | tf_op jit(solution)/shard_map/ppermute | solution.py:371
  15.2 0.4 collective-permute-done.8.came
  15.6 0.6 %collective-permute-start.9 = (bf16[6,64,128]{2,1,0:T(8,128)(2,1)S(1)}, bf16[6,64,128]{2,1,0:T(8,128)(2,1)S(1)}, u32[]{:S(2)}, u32[]{:S(2)}) collective-permute-start(bf16[6,64,128]{2,1,0:T(8,128)(2,1)S(1)} %shard_map.116), channel_id=1, source_target_pairs={{0,2},{1,3},{2,0},{3,1},{4,6},{5,7},{6,4},{7,5},{8,10},{9,11},{10,... | collective-permute-start | bytes 294920 | tf_op jit(solution)/shard_map/ppermute | solution.py:371
  16.2 1.5 %collective-permute-done.3.refs_2_ = bf16[640,128]{1,0:T(8,128)(2,1)S(1)} collective-permute-done((bf16[640,128]{1,0:T(8,128)(2,1)S(1)}, bf16[640,128]{1,0:T(8,128)(2,1)S(1)}, u32[]{:S(2)}, u32[]{:S(2)}) %collective-permute-start.3) | collective-permute-done | bytes 163872 | tf_op jit(solution)/shard_map/ppermute | solution.py:371
  17.8 0.5 %collective-permute-start.4 = (bf16[320,128]{1,0:T(8,128)(2,1)S(1)}, bf16[320,128]{1,0:T(8,128)(2,1)S(1)}, u32[]{:S(2)}, u32[]{:S(2)}) collective-permute-start(bf16[320,128]{1,0:T(8,128)(2,1)S(1)} %get-tuple-element.73), channel_id=1, source_target_pairs={{0,1},{1,0},{2,3},{3,2},{4,5},{5,4},{6,7},{7,6},{8,9},{9,8},{10,11... | collective-permute-start | bytes 245768 | tf_op jit(solution)/shard_map/ppermute | solution.py:371
  18.3 0.8 %collective-permute-done.5.refs_4_ = bf16[320,128]{1,0:T(8,128)(2,1)S(1)} collective-permute-done((bf16[320,128]{1,0:T(8,128)(2,1)S(1)}, bf16[320,128]{1,0:T(8,128)(2,1)S(1)}, u32[]{:S(2)}, u32[]{:S(2)}) %collective-permute-start.5) | collective-permute-done | bytes 81952 | tf_op jit(solution)/shard_map/ppermute | solution.py:371
  19.2 1.3 %shard_map.113.pieces = f32[8,176,128]{2,1,0:T(8,128)S(1)} custom-call(bf16[640,128]{1,0:T(8,128)(2,1)S(1)} %get-tuple-element.50.refs_0_, bf16[640,128]{1,0:T(8,128)(2,1)S(1)} %collective-permute-done.2.refs_1_, bf16[640,128]{1,0:T(8,128)(2,1)S(1)} %collective-permute-done.3.refs_2_, bf16[320,128]{1,0:T(8,128)(2,1)S(1)} %collective-permute-done.4.refs_3_, ...), custom_call_target="tpu_custom_call" | custom-call | bytes 1376256 | tf_op jit(solution)/shard_map/pallas_call | solution.py:27
  20.6 5.1 %collective-permute-start.10 = (bf16[176,128]{1,0:T(8,128)(2,1)S(1)}, bf16[176,128]{1,0:T(8,128)(2,1)S(1)}, u32[]{:S(2)}, u32[]{:S(2)}) collective-permute-start(bf16[176,128]{1,0:T(8,128)(2,1)S(1)} %get-tuple-element.63), channel_id=1, source_target_pairs={{0,24},{4,28},{8,16},{12,20},{16,8},{20,12},{24,0},{28,4},{1,25},{... | collective-permute-start | bytes 135176 | tf_op jit(solution)/shard_map/ppermute | solution.py:371
  25.7 2.4 %collective-permute-start.12 = (bf16[176,128]{1,0:T(8,128)(2,1)S(1)}, bf16[176,128]{1,0:T(8,128)(2,1)S(1)}, u32[]{:S(2)}, u32[]{:S(2)}) collective-permute-start(bf16[176,128]{1,0:T(8,128)(2,1)S(1)} %get-tuple-element.65), channel_id=1, source_target_pairs={{0,28},{4,24},{8,20},{12,16},{16,12},{20,8},{24,4},{28,0},{1,29},{... | collective-permute-start | bytes 135176 | tf_op jit(solution)/shard_map/ppermute | solution.py:371
  28.1 0.6 %collective-permute-start.13 = (bf16[176,128]{1,0:T(8,128)(2,1)S(1)}, bf16[176,128]{1,0:T(8,128)(2,1)S(1)}, u32[]{:S(2)}, u32[]{:S(2)}) collective-permute-start(bf16[176,128]{1,0:T(8,128)(2,1)S(1)} %get-tuple-element.66), channel_id=1, source_target_pairs={{0,20},{4,16},{8,28},{12,24},{16,4},{20,0},{24,12},{28,8},{1,21},{... | collective-permute-start | bytes 135176 | tf_op jit(solution)/shard_map/ppermute | solution.py:371
  28.7 2.2 %collective-permute-start.14 = (bf16[176,128]{1,0:T(8,128)(2,1)S(1)}, bf16[176,128]{1,0:T(8,128)(2,1)S(1)}, u32[]{:S(2)}, u32[]{:S(2)}) collective-permute-start(bf16[176,128]{1,0:T(8,128)(2,1)S(1)} %get-tuple-element.67), channel_id=1, source_target_pairs={{0,12},{4,8},{8,4},{12,0},{16,28},{20,24},{24,20},{28,16},{1,13},{... | collective-permute-start | bytes 135176 | tf_op jit(solution)/shard_map/ppermute | solution.py:371
  30.9 0.6 %collective-permute-start.15 = (bf16[176,128]{1,0:T(8,128)(2,1)S(1)}, bf16[176,128]{1,0:T(8,128)(2,1)S(1)}, u32[]{:S(2)}, u32[]{:S(2)}) collective-permute-start(bf16[176,128]{1,0:T(8,128)(2,1)S(1)} %get-tuple-element.68), channel_id=1, source_target_pairs={{0,8},{4,12},{8,0},{12,4},{16,24},{20,28},{24,16},{28,20},{1,9},{5... | collective-permute-start | bytes 135176 | tf_op jit(solution)/shard_map/ppermute | solution.py:371
  31.7 0.8 %collective-permute-start.16 = (bf16[176,128]{1,0:T(8,128)(2,1)S(1)}, bf16[176,128]{1,0:T(8,128)(2,1)S(1)}, u32[]{:S(2)}, u32[]{:S(2)}) collective-permute-start(bf16[176,128]{1,0:T(8,128)(2,1)S(1)} %get-tuple-element.69), channel_id=1, source_target_pairs={{0,4},{4,0},{8,12},{12,8},{16,20},{20,16},{24,28},{28,24},{1,5},{5... | collective-permute-start | bytes 135176 | tf_op jit(solution)/shard_map/ppermute | solution.py:371
  32.5 2.2 %shard_map.112 = (bf16[2,1,64,320]{3,2,1,0:T(8,128)(2,1)}, bf16[2,1,64,320]{3,2,1,0:T(8,128)(2,1)}, bf16[2,1,64,320]{3,2,1,0:T(8,128)(2,1)}, bf16[2,1,64,320]{3,2,1,0:T(8,128)(2,1)}) custom-call(bf16[640,128]{1,0:T(8,128)(2,1)S(1)} %get-tuple-element.50.refs_0_, bf16[640,128]{1,0:T(8,128)(2,1)S(1)} %collective-permute-done.2.refs_1_, ...), custom_call_target="tpu_custom_call" | custom-call | bytes 2232320 | tf_op jit(solution)/shard_map/pallas_call | solution.py:27
  35.0 0.8 %collective-permute-done.16.refs_7_ = bf16[176,128]{1,0:T(8,128)(2,1)S(1)} collective-permute-done((bf16[176,128]{1,0:T(8,128)(2,1)S(1)}, bf16[176,128]{1,0:T(8,128)(2,1)S(1)}, u32[]{:S(2)}, u32[]{:S(2)}) %collective-permute-start.16) | collective-permute-done | bytes 45088 | tf_op jit(solution)/shard_map/ppermute | solution.py:371
  35.8 0.7 %shard_map.118 = (f32[120,128]{1,0:T(8,128)}, f32[60,128]{1,0:T(8,128)}) custom-call(f32[176,128]{1,0:T(8,128)S(1)} %get-tuple-element.62.refs_0_, bf16[176,128]{1,0:T(8,128)(2,1)S(1)} %collective-permute-done.10.refs_1_, bf16[176,128]{1,0:T(8,128)(2,1)S(1)} %collective-permute-done.11.refs_2_, bf16[176,128]{1,0:T(8,128)(2,1)S(1)} %collective-permute-done.12.refs_3_, ...), custom_call_target="tpu_custom_call" | custom-call | bytes 497664 | tf_op jit(solution)/shard_map/pallas_call | solution.py:27
  (28 shorter events, 1.6 us)
Async XLA Ops:
  1.7 10.0 %collective-permute-start = (bf16[128,640]{1,0:T(8,128)(2,1)S(1)}, bf16[128,640]{1,0:T(8,128)(2,1)S(1)}, u32[]{:S(2)}, u32[]{:S(2)}) collective-permute-start(bf16[128,640]{1,0:T(8,128)(2,1)S(1)} %shard_map.109.own.refs_0_), channel_id=1, source_target_pairs={{0,4},{4,0},{8,12},{12,8},{16,20},{20,16},{24,28},{28,24},{1,5},{5... | collective-permute-start | bytes 491528 | tf_op jit(solution)/shard_map/ppermute | solution.py:396
  4.8 7.0 %collective-permute-start.1 = (bf16[128,640]{1,0:T(8,128)(2,1)S(1)}, bf16[128,640]{1,0:T(8,128)(2,1)S(1)}, u32[]{:S(2)}, u32[]{:S(2)}) collective-permute-start(bf16[128,640]{1,0:T(8,128)(2,1)S(1)} %shard_map.109.own.refs_0_), channel_id=1, source_target_pairs={{4,8},{8,4},{12,16},{16,12},{20,24},{24,20},{5,9},{9,5},{13,17},{1... | collective-permute-start | bytes 491528 | tf_op jit(solution)/shard_map/ppermute | solution.py:396
  5.4 9.3 %collective-permute-start.6 = (bf16[128,640]{1,0:T(8,128)(2,1)S(1)}, bf16[128,640]{1,0:T(8,128)(2,1)S(1)}, u32[]{:S(2)}, u32[]{:S(2)}) collective-permute-start(bf16[128,640]{1,0:T(8,128)(2,1)S(1)} %shard_map.109.own.refs_0_), channel_id=1, source_target_pairs={{0,2},{1,3},{2,0},{3,1},{4,6},{5,7},{6,4},{7,5},{8,10},{9,11},{10,... | collective-permute-start | bytes 491528 | tf_op jit(solution)/shard_map/ppermute | solution.py:371
  12.3 5.4 %collective-permute-start.3 = (bf16[640,128]{1,0:T(8,128)(2,1)S(1)}, bf16[640,128]{1,0:T(8,128)(2,1)S(1)}, u32[]{:S(2)}, u32[]{:S(2)}) collective-permute-start(bf16[640,128]{1,0:T(8,128)(2,1)S(1)} %get-tuple-element.50.refs_0_), channel_id=1, source_target_pairs={{0,2},{1,3},{2,0},{3,1},{4,6},{5,7},{6,4},{7,5},{8,10},{9,11},{10,... | collective-permute-start | bytes 491528 | tf_op jit(solution)/shard_map/ppermute | solution.py:371
  14.2 1.4 %collective-permute-start.8 = (bf16[6,64,128]{2,1,0:T(8,128)(2,1)S(1)}, bf16[6,64,128]{2,1,0:T(8,128)(2,1)S(1)}, u32[]{:S(2)}, u32[]{:S(2)}) collective-permute-start(bf16[6,64,128]{2,1,0:T(8,128)(2,1)S(1)} %get-tuple-element.61), channel_id=1, source_target_pairs={{0,1},{1,0},{2,3},{3,2},{4,5},{5,4},{6,7},{7,6},{8,9},{9,8},{10,11... | collective-permute-start | bytes 294920 | tf_op jit(solution)/shard_map/ppermute | solution.py:371
  14.2 4.0 %collective-permute-start.2 = (bf16[640,128]{1,0:T(8,128)(2,1)S(1)}, bf16[640,128]{1,0:T(8,128)(2,1)S(1)}, u32[]{:S(2)}, u32[]{:S(2)}) collective-permute-start(bf16[640,128]{1,0:T(8,128)(2,1)S(1)} %get-tuple-element.50.refs_0_), channel_id=1, source_target_pairs={{0,1},{1,0},{2,3},{3,2},{4,5},{5,4},{6,7},{7,6},{8,9},{9,8},{10,11... | collective-permute-start | bytes 491528 | tf_op jit(solution)/shard_map/ppermute | solution.py:371
  15.0 5.5 %collective-permute-start.7 = (bf16[8,64,128]{2,1,0:T(8,128)(2,1)S(1)}, bf16[8,64,128]{2,1,0:T(8,128)(2,1)S(1)}, u32[]{:S(2)}, u32[]{:S(2)}) collective-permute-start(bf16[8,64,128]{2,1,0:T(8,128)(2,1)S(1)} %get-tuple-element.59), channel_id=1, source_target_pairs={{0,1},{1,0},{2,3},{3,2},{4,5},{5,4},{6,7},{7,6},{8,9},{9,8},{10,11... | collective-permute-start | bytes 393224 | tf_op jit(solution)/shard_map/ppermute | solution.py:371
  15.5 17.0 %copy-start = (bf16[3,3,2,160,160]{4,3,2,1,0:T(8,128)(2,1)S(1)}, bf16[3,3,2,160,160]{4,3,2,1,0:T(8,128)(2,1)}, u32[]{:S(2)}) copy-start(bf16[3,3,2,160,160]{4,3,2,1,0:T(8,128)(2,1)} %refs_9_.1) | copy-start | bytes 2764804
  15.6 17.0 %copy-start.1 = (bf16[2,1,64,320]{3,2,1,0:T(8,128)(2,1)S(1)}, bf16[2,1,64,320]{3,2,1,0:T(8,128)(2,1)}, u32[]{:S(2)}) copy-start(bf16[2,1,64,320]{3,2,1,0:T(8,128)(2,1)} %refs_5_.1) | copy-start | bytes 245764
  15.6 17.0 %copy-start.2 = (bf16[2,1,64,320]{3,2,1,0:T(8,128)(2,1)S(1)}, bf16[2,1,64,320]{3,2,1,0:T(8,128)(2,1)}, u32[]{:S(2)}) copy-start(bf16[2,1,64,320]{3,2,1,0:T(8,128)(2,1)} %refs_6_.1) | copy-start | bytes 245764
  15.6 4.9 %collective-permute-start.9 = (bf16[6,64,128]{2,1,0:T(8,128)(2,1)S(1)}, bf16[6,64,128]{2,1,0:T(8,128)(2,1)S(1)}, u32[]{:S(2)}, u32[]{:S(2)}) collective-permute-start(bf16[6,64,128]{2,1,0:T(8,128)(2,1)S(1)} %shard_map.116), channel_id=1, source_target_pairs={{0,2},{1,3},{2,0},{3,1},{4,6},{5,7},{6,4},{7,5},{8,10},{9,11},{10,... | collective-permute-start | bytes 294920 | tf_op jit(solution)/shard_map/ppermute | solution.py:371
  17.7 1.3 %collective-permute-start.5 = (bf16[320,128]{1,0:T(8,128)(2,1)S(1)}, bf16[320,128]{1,0:T(8,128)(2,1)S(1)}, u32[]{:S(2)}, u32[]{:S(2)}) collective-permute-start(bf16[320,128]{1,0:T(8,128)(2,1)S(1)} %get-tuple-element.72), channel_id=1, source_target_pairs={{0,1},{1,0},{2,3},{3,2},{4,5},{5,4},{6,7},{7,6},{8,9},{9,8},{10,11... | collective-permute-start | bytes 245768 | tf_op jit(solution)/shard_map/ppermute | solution.py:371
  17.8 1.4 %collective-permute-start.4 = (bf16[320,128]{1,0:T(8,128)(2,1)S(1)}, bf16[320,128]{1,0:T(8,128)(2,1)S(1)}, u32[]{:S(2)}, u32[]{:S(2)}) collective-permute-start(bf16[320,128]{1,0:T(8,128)(2,1)S(1)} %get-tuple-element.73), channel_id=1, source_target_pairs={{0,1},{1,0},{2,3},{3,2},{4,5},{5,4},{6,7},{7,6},{8,9},{9,8},{10,11... | collective-permute-start | bytes 245768 | tf_op jit(solution)/shard_map/ppermute | solution.py:371
  20.6 10.3 %collective-permute-start.10 = (bf16[176,128]{1,0:T(8,128)(2,1)S(1)}, bf16[176,128]{1,0:T(8,128)(2,1)S(1)}, u32[]{:S(2)}, u32[]{:S(2)}) collective-permute-start(bf16[176,128]{1,0:T(8,128)(2,1)S(1)} %get-tuple-element.63), channel_id=1, source_target_pairs={{0,24},{4,28},{8,16},{12,20},{16,8},{20,12},{24,0},{28,4},{1,25},{... | collective-permute-start | bytes 135176 | tf_op jit(solution)/shard_map/ppermute | solution.py:371
  25.7 6.0 %collective-permute-start.11 = (bf16[176,128]{1,0:T(8,128)(2,1)S(1)}, bf16[176,128]{1,0:T(8,128)(2,1)S(1)}, u32[]{:S(2)}, u32[]{:S(2)}) collective-permute-start(bf16[176,128]{1,0:T(8,128)(2,1)S(1)} %get-tuple-element.64), channel_id=1, source_target_pairs={{0,16},{4,20},{8,24},{12,28},{16,0},{20,4},{24,8},{28,12},{1,17},{... | collective-permute-start | bytes 135176 | tf_op jit(solution)/shard_map/ppermute | solution.py:371
  25.7 9.0 %collective-permute-start.12 = (bf16[176,128]{1,0:T(8,128)(2,1)S(1)}, bf16[176,128]{1,0:T(8,128)(2,1)S(1)}, u32[]{:S(2)}, u32[]{:S(2)}) collective-permute-start(bf16[176,128]{1,0:T(8,128)(2,1)S(1)} %get-tuple-element.65), channel_id=1, source_target_pairs={{0,28},{4,24},{8,20},{12,16},{16,12},{20,8},{24,4},{28,0},{1,29},{... | collective-permute-start | bytes 135176 | tf_op jit(solution)/shard_map/ppermute | solution.py:371
  28.1 6.6 %collective-permute-start.13 = (bf16[176,128]{1,0:T(8,128)(2,1)S(1)}, bf16[176,128]{1,0:T(8,128)(2,1)S(1)}, u32[]{:S(2)}, u32[]{:S(2)}) collective-permute-start(bf16[176,128]{1,0:T(8,128)(2,1)S(1)} %get-tuple-element.66), channel_id=1, source_target_pairs={{0,20},{4,16},{8,28},{12,24},{16,4},{20,0},{24,12},{28,8},{1,21},{... | collective-permute-start | bytes 135176 | tf_op jit(solution)/shard_map/ppermute | solution.py:371
  28.7 6.1 %collective-permute-start.14 = (bf16[176,128]{1,0:T(8,128)(2,1)S(1)}, bf16[176,128]{1,0:T(8,128)(2,1)S(1)}, u32[]{:S(2)}, u32[]{:S(2)}) collective-permute-start(bf16[176,128]{1,0:T(8,128)(2,1)S(1)} %get-tuple-element.67), channel_id=1, source_target_pairs={{0,12},{4,8},{8,4},{12,0},{16,28},{20,24},{24,20},{28,16},{1,13},{... | collective-permute-start | bytes 135176 | tf_op jit(solution)/shard_map/ppermute | solution.py:371
  30.9 4.0 %collective-permute-start.15 = (bf16[176,128]{1,0:T(8,128)(2,1)S(1)}, bf16[176,128]{1,0:T(8,128)(2,1)S(1)}, u32[]{:S(2)}, u32[]{:S(2)}) collective-permute-start(bf16[176,128]{1,0:T(8,128)(2,1)S(1)} %get-tuple-element.68), channel_id=1, source_target_pairs={{0,8},{4,12},{8,0},{12,4},{16,24},{20,28},{24,16},{28,20},{1,9},{5... | collective-permute-start | bytes 135176 | tf_op jit(solution)/shard_map/ppermute | solution.py:371
  31.7 4.0 %collective-permute-start.16 = (bf16[176,128]{1,0:T(8,128)(2,1)S(1)}, bf16[176,128]{1,0:T(8,128)(2,1)S(1)}, u32[]{:S(2)}, u32[]{:S(2)}) collective-permute-start(bf16[176,128]{1,0:T(8,128)(2,1)S(1)} %get-tuple-element.69), channel_id=1, source_target_pairs={{0,4},{4,0},{8,12},{12,8},{16,20},{20,16},{24,28},{28,24},{1,5},{5... | collective-permute-start | bytes 135176 | tf_op jit(solution)/shard_map/ppermute | solution.py:371
